TPU v7x, 1024 devices: a whole 8x8x8 slice. The times are simulated.
1024 devices in a mesh: node: 64 (over z_hi, x, core), local: 16 (over z_lo, y).
Axes of the slice: x: 8, y: 8, z: 8 (z_hi: 4, z_lo: 2; z = z_hi * 2 + z_lo), core: 2. Of those that a mesh axis runs over, the one named last changes fastest.
Arguments:
- tokens: bfloat16 [2048, 6144], P(None, 'local'), may hold values from -6 to 6
- codes: bfloat16 [6144, 24576], P('local', 'node'), may hold values from -4 to 4
- scales: float32 [3, 24576], P(None, 'node'), may hold values from 0.008 to 0.02
- cotangent: bfloat16 [2048, 24576], P('local', 'node'), may hold values from -16 to 16
Outputs:
- activated: bfloat16 [2048, 24576], P('local', 'node')
- input_grad: bfloat16 [2048, 6144], P('node', 'local')
- weight_grad: float32 [6144, 24576], P('local', 'node')
All inputs are finite; a program needn't handle non-finite values.
Results may differ from a plain program's by a relative error of at most 0.0063.
Values may be sent and summed in bfloat16 or wider, within the bound.
No kernel may reach another device: no remote copies, remote signals or barrier semaphores. Data moves between devices by JAX's collectives and lax.ppermute only.
A program may use at most 64 MiB of HBM per device.

v0:
```python
import math

import jax
import jax.numpy as jnp
from jax import lax
from jax.sharding import PartitionSpec as P

BLOCK = 2048


def gelu_tanh(value):
    inner = math.sqrt(2.0 / math.pi) * (value + 0.044715 * value * value * value)
    return 0.5 * value * (1.0 + jnp.tanh(inner))


def dequant(piece, start, scales):
    blocks = scales.shape[0]
    index = (start + jnp.arange(piece.shape[0])) // BLOCK
    picked = (index[:, None] == jnp.arange(blocks)[None, :]).astype(jnp.float32)
    row_scale = jnp.sum(picked[:, :, None] * scales[None, :, :], axis=1)
    return (piece.astype(jnp.float32) * row_scale).astype(jnp.bfloat16)


def shards(tokens, codes, scales, cotangent):
    all_rows = tokens.shape[0]
    feat_loc = codes.shape[0]
    first_row = lax.axis_index("local") * feat_loc
    weight = dequant(codes, first_row, scales)
    pre = lax.psum_scatter(
        jnp.dot(tokens, weight, preferred_element_type=jnp.float32),
        "local",
        scatter_dimension=0,
        tiled=True,
    )
    act, pull = jax.vjp(gelu_tanh, pre)
    slope = pull(cotangent.astype(jnp.float32))[0].astype(jnp.bfloat16)
    factor = all_rows ** (-0.5)
    slope_full = lax.all_gather(slope, "local", axis=0, tiled=True)
    weight_grad = (
        lax.dot_general(
            tokens, slope_full, (((0,), (0,)), ((), ())), preferred_element_type=jnp.float32
        )
        * factor
    )
    input_grad = lax.psum_scatter(
        lax.dot_general(
            slope_full, weight, (((1,), (1,)), ((), ())), preferred_element_type=jnp.float32
        ),
        "node",
        scatter_dimension=0,
        tiled=True,
    )
    return (act.astype(jnp.bfloat16), input_grad.astype(jnp.bfloat16), weight_grad)


def solution(mesh):
    placed = (P(None, "local"), P("local", "node"), P(None, "node"), P("local", "node"))
    return jax.shard_map(
        shards,
        mesh=mesh,
        in_specs=placed,
        out_specs=(P("local", "node"), P("node", "local"), P("local", "node")),
        check_vma=False,
    )
```

profile of v0, /device:TPU:14, one launch (start us, length us, event | category | flops | bytes accessed | tf_op | source)
XLA Modules:
  0.0 358.0 jit_solution(16310016823720181967)
XLA Ops:
  7.2 0.0 copy-start
  7.2 0.0 reduce-scatter.3.cloned.1.call-start
  7.3 1.0 multiply_reduce_fusion
  8.3 0.3 copy-done
  8.6 3.6 %convolution_bitcast_fusion = f32[2048,384]{0,1:T(8,128)} fusion(bf16[2048,384]{1,0:T(8,128)(2,1)S(1)} %copy-done, f32[384,384]{1,0:T(8,128)S(1)} %multiply_reduce_fusion, bf16[384,384]{1,0:T(8,128)(2,1)} %param.5), kind=kOutput, calls=%fused_computation | convolution fusion | flops 604422144 | bytes 5603328 | tf_op jit(solution)/shard_map/dot_general | solution.py:30
  12.2 0.0 copy-start.3
  12.2 0.0 copy-start.2
  12.2 0.0 reduce-scatter.3.cloned.1.call-update
  12.3 0.0 all-gather.2.cloned.1.call-start
  12.3 0.8 copy-done.3
  13.1 0.1 copy.10
  13.3 93.2 %reduce-scatter.3.cloned.1.call-done = f32[128,384]{0,1:T(8,128)} async-done(((f32[2048,384]{0,1:T(8,128)}), f32[128,384]{0,1:T(8,128)}) %reduce-scatter.3.cloned.1.call-update) | async-done | bytes 196624 | tf_op jit(solution)/shard_map/reduce_scatter | solution.py:29
  106.5 1.8 fusion.7
  108.3 0.0 all-gather.2.cloned.1.call-update
  108.3 0.0 reduce-scatter.5.cloned.1.call-start
  108.3 71.4 %all-gather.2.cloned.1.call-done = bf16[2048,384]{0,1:T(8,128)(2,1)} async-done(((bf16[128,384]{0,1:T(8,128)(2,1)}), bf16[2048,384]{0,1:T(8,128)(2,1)}) %all-gather.2.cloned.1.call-update) | async-done | bytes 1572880 | tf_op jit(solution)/shard_map/all_gather | solution.py:38
  179.7 0.0 copy-done.2
  179.7 4.2 %fusion.16 = f32[2048,384]{1,0:T(8,128)} fusion(bf16[2048,384]{0,1:T(8,128)(2,1)} %all-gather.2.cloned.1.call-done, f32[384,384]{1,0:T(8,128)S(1)} %multiply_reduce_fusion, bf16[384,384]{1,0:T(8,128)(2,1)S(1)} %copy-done.2), kind=kOutput, calls=%fused_computation.33 | convolution fusion | flops 604422144 | bytes 5603328 | tf_op jit(solution)/shard_map/dot_general | solution.py:46
  184.0 0.0 copy-start.1
  184.0 0.0 reduce-scatter.5.cloned.1.call-update
  184.0 0.8 copy.11
  184.8 0.7 copy-done.1
  185.4 1.8 fusion
  187.2 2.1 copy.12
  189.3 160.7 %reduce-scatter.5.cloned.1.call-done = f32[32,384]{1,0:T(8,128)} async-done(((f32[2048,384]{1,0:T(8,128)}), f32[32,384]{1,0:T(8,128)}) %reduce-scatter.5.cloned.1.call-update) | async-done | bytes 49168 | tf_op jit(solution)/shard_map/reduce_scatter | solution.py:45
  350.0 1.4 convert_element_type.31
  (2 shorter events, 0.0 us)
Async XLA Ops:
  7.2 1.4 copy-start
  7.2 99.3 %reduce-scatter.3.cloned.1.call-start = ((), (), s32[]{:S(2)}) async-start(), calls=%async_computation.2 | async-start | bytes 3342336 | tf_op jit(solution)/shard_map/reduce_scatter | solution.py:29
  12.2 0.9 copy-start.3
  12.2 167.5 %copy-start.2 = (bf16[384,384]{1,0:T(8,128)(2,1)S(1)}, bf16[384,384]{1,0:T(8,128)(2,1)}, u32[]{:S(2)}) copy-start(bf16[384,384]{1,0:T(8,128)(2,1)} %param.5) | copy-start | bytes 884740
  12.3 167.5 %all-gather.2.cloned.1.call-start = ((), (), s32[]{:S(2)}) async-start(), calls=%async_computation.3 | async-start | bytes 1671168 | tf_op jit(solution)/shard_map/all_gather | solution.py:38
  108.3 241.8 %reduce-scatter.5.cloned.1.call-start = ((), (), s32[]{:S(2)}) async-start(), calls=%async_computation.4 | async-start | bytes 3194880 | tf_op jit(solution)/shard_map/reduce_scatter | solution.py:45
  184.0 1.4 copy-start.1
Sparse Core Ops, SparseCore 0:
  12.4 94.0 reduce-scatter.2
  109.7 70.0 all-gather.1
  185.6 164.3 reduce-scatter.4
where the time goes:
time: 359 us; the launch traced here: 358 us
  waiting for transfers between devices  325 us (91%)
  between operations  13.8 us (4%)
  matrix products  9.68 us (3%)
  local copies, waits for them, and re-layouts  4.76 us (1%)
  other arithmetic  4.23 us (1%)
    reduce_scatter x1, waiting for transfers between devices, shards(): lax.psum_scatter(lax.dot_general(slope_full, weight, (((1,), (1,)), ((),...  161 us
    reduce_scatter x1, waiting for transfers between devices, shards(): lax.psum_scatter(jnp.dot(tokens, weight, preferred_element_type=jnp.float...  93.2 us
    all_gather x1, waiting for transfers between devices, shards(): slope_full = lax.all_gather(slope, 'local', axis=0, tiled=True)  71.4 us
  transfers between devices with their start and end apart: 3, of which 3 were waited for; matrix products, arithmetic and copies ran while one was open for 1% of the time, Pallas kernels for 0%

commit v1 on v0

v1 whole, which is shorter than its diff:
```python
import math

import jax
import jax.numpy as jnp
from jax import lax
from jax.sharding import PartitionSpec as P

BLOCK = 2048
F32 = jnp.float32
BF16 = jnp.bfloat16


def gelu_tanh(value):
    inner = math.sqrt(2.0 / math.pi) * (value + 0.044715 * value * value * value)
    return 0.5 * value * (1.0 + jnp.tanh(inner))


def dequant(piece, start, scales):
    block = (start + lax.broadcasted_iota(jnp.int32, piece.shape, 0)) // BLOCK
    scale = jnp.broadcast_to(scales[0:1], piece.shape)
    for i in range(1, scales.shape[0]):
        scale = jnp.where(block == i, scales[i : i + 1], scale)
    return (piece.astype(F32) * scale).astype(BF16)


def shards(locals_, nodes, tokens, codes, scales, cotangent):
    rows = tokens.shape[0]
    feat = codes.shape[0]
    units = codes.shape[1]
    mine = rows // locals_
    out_rows = rows // nodes
    weight = dequant(codes, lax.axis_index("local") * feat, scales)
    partial = jnp.dot(tokens, weight, preferred_element_type=F32).astype(BF16)
    partial = partial.reshape(locals_, mine, units)
    partial = lax.all_to_all(partial, "local", 0, 0, tiled=True)
    pre = jnp.sum(partial.astype(F32), axis=0)
    act, pull = jax.vjp(gelu_tanh, pre)
    slope = pull(cotangent.astype(F32))[0].astype(BF16)
    spread = jnp.broadcast_to(slope[None], (locals_, mine, units))
    spread = lax.all_to_all(spread, "local", 0, 0, tiled=True)
    slope_full = spread.reshape(rows, units)
    core = lax.axis_index("node") % 2
    by_core = slope_full.reshape(nodes // 2, 2, out_rows, units)

    def grad_rows(which):
        part = lax.dynamic_index_in_dim(by_core, which, 1, keepdims=False)
        return lax.dot_general(
            part.reshape(rows // 2, units),
            weight,
            (((1,), (1,)), ((), ())),
            preferred_element_type=F32,
        )

    other = lax.ppermute(
        grad_rows(1 - core).astype(BF16), "node", [(i, i ^ 1) for i in range(nodes)]
    )
    both = (grad_rows(core) + other.astype(F32)).astype(BF16)
    both = both.reshape(nodes // 2, out_rows, feat)
    groups = [list(range(c, nodes, 2)) for c in range(2)]
    both = lax.all_to_all(both, "node", 0, 0, axis_index_groups=groups, tiled=True)
    input_grad = jnp.sum(both.astype(F32), axis=0).astype(BF16)
    weight_grad = lax.dot_general(
        tokens, slope_full, (((0,), (0,)), ((), ())), preferred_element_type=F32
    ) * (rows ** (-0.5))
    return act.astype(BF16), input_grad, weight_grad


def solution(mesh):
    locals_, nodes = mesh.shape["local"], mesh.shape["node"]

    def body(*args):
        return shards(locals_, nodes, *args)

    placed = (P(None, "local"), P("local", "node"), P(None, "node"), P("local", "node"))
    return jax.shard_map(
        body,
        mesh=mesh,
        in_specs=placed,
        out_specs=(P("local", "node"), P("node", "local"), P("local", "node")),
        check_vma=False,
    )
```

time: 359 us -> 156 us (0.43)
  waiting for transfers between devices: 325 us -> 97 us
  starting transfers between devices: 0.12 us -> 37.7 us
  between operations: 13.8 us -> 0.76 us
  local copies, waits for them, and re-layouts: 4.76 us -> 8.41 us
    reduce_scatter x2 -> x0, waiting for transfers between devices: 254 us -> none  [the longest x1 161 us: shards(): lax.psum_scatter(lax.dot_general(slope_full, weight, (((1,), (1,)), ((),...]
    all_to_all x0 -> x3, waiting for transfers between devices: none -> 94.7 us  [the longest x1 37.9 us: shards(): spread = lax.all_to_all(spread, 'local', 0, 0, tiled=True)]
    all_gather x1 -> x0, waiting for transfers between devices: 71.4 us -> none  [shards(): slope_full = lax.all_gather(slope, 'local', axis=0, tiled=True)]
    all_to_all x0 -> x3, starting transfers between devices: none -> 35.7 us  [the longest x1 20.4 us: shards(): lax.all_to_all(both, 'node', 0, 0, axis_index_groups=groups, tiled=True)]
    dot_general x2 -> x3, matrix products: 7.88 us -> 4.69 us  [the longest x2 2.49 us: grad_rows(): lax.dot_general(part.reshape(rows // 2, units), weight, (((1,), (1,)), ((...]
  transfers between devices with their start and end apart: 3 -> 4, of which waited for: 3 -> 4; matrix products, arithmetic and copies ran while one was open for 1% -> 3% of each run, Pallas kernels for 0% -> 0%
where the time goes in v1:
time: 156 us; the launch traced here: 153 us
  waiting for transfers between devices  97 us (62%)
  starting transfers between devices  37.7 us (24%)
  local copies, waits for them, and re-layouts  8.41 us (5%)
  matrix products  6.5 us (4%)
  other arithmetic  2.31 us (1%)
    all_to_all x1, waiting for transfers between devices, shards(): spread = lax.all_to_all(spread, 'local', 0, 0, tiled=True)  37.9 us
    all_to_all x1, waiting for transfers between devices, shards(): partial = lax.all_to_all(partial, 'local', 0, 0, tiled=True)  37.9 us
    all_to_all x1, starting transfers between devices, shards(): lax.all_to_all(both, 'node', 0, 0, axis_index_groups=groups, tiled=True)  20.4 us
    all_to_all x1, waiting for transfers between devices, shards(): lax.all_to_all(both, 'node', 0, 0, axis_index_groups=groups, tiled=True)  18.9 us
    all_to_all x1, starting transfers between devices, shards(): partial = lax.all_to_all(partial, 'local', 0, 0, tiled=True)  10.5 us
    all_to_all x1, starting transfers between devices, shards(): spread = lax.all_to_all(spread, 'local', 0, 0, tiled=True)  4.89 us
    unnamed x9, local copies, waits for them, and re-layouts  4.27 us
  transfers between devices with their start and end apart: 4, of which 4 were waited for; matrix products, arithmetic and copies ran while one was open for 3% of the time, Pallas kernels for 0%

profile of v1, /device:TPU:14, one launch (start us, length us, event | category | flops | bytes accessed | tf_op | source)
XLA Modules:
  0.0 152.6 jit_solution(1409483025424061417)
XLA Ops:
  0.6 0.0 copy-start
  0.7 0.9 slice_reduce_fusion.2
  1.5 0.5 copy-done
  2.1 2.2 %fusion = bf16[48,16,8,128]{3,2,1,0:T(8,128)(2,1)S(1)} fusion(bf16[2048,384]{1,0:T(8,128)(2,1)S(1)} %copy-done, bf16[384,384]{1,0:T(8,128)(2,1)} %param.5, f32[384]{0:T(512)S(1)} %get-tuple-element.10, f32[384]{0:T(512)S(1)} %get-tuple-element.11, f32[384]{0:T(512)S(1)} %get-tuple-element.9, s32[384]{0:T(512)S(1)} %get-tuple-element.16, ...), kind=kOutput, calls=%fused_computation.4 | convolution fusion | flops 605945856 | bytes 3448704 | tf_op jit(solution)/shard_map/dot_general | solution.py:33
  4.3 1.6 %copy.17 = bf16[48,16,8,128]{3,2,0,1:T(8,128)(2,1)} copy(bf16[48,16,8,128]{3,2,1,0:T(8,128)(2,1)S(1)} %fusion) | data formatting | bytes 3145728 | tf_op jit(solution)/shard_map/reshape | solution.py:34
  5.9 0.0 copy-start.1
  5.9 10.5 %all-to-all-start = ((bf16[16,128,384]{1,2,0:T(8,128)(2,1)}), bf16[16,128,384]{1,2,0:T(8,128)(2,1)S(1)}, u32[]{:S(2)}, u32[]{:S(2)}) async-start(bf16[16,128,384]{1,2,0:T(8,128)(2,1)} %bitcast.20), calls=%async_computation | async-start | bytes 3145728 | tf_op jit(solution)/shard_map/all_to_all | solution.py:35
  16.4 0.0 copy-done.1
  16.4 0.1 copy.10
  16.5 37.9 %all-to-all-done = bf16[16,128,384]{1,2,0:T(8,128)(2,1)S(1)} async-done(((bf16[16,128,384]{1,2,0:T(8,128)(2,1)}), bf16[16,128,384]{1,2,0:T(8,128)(2,1)S(1)}, u32[]{:S(2)}, u32[]{:S(2)}) %all-to-all-start) | async-done | bytes 1572896 | tf_op jit(solution)/shard_map/all_to_all | solution.py:35
  54.4 0.2 convert_reduce_fusion
  54.7 0.2 fusion.8
  54.9 0.1 copy.11
  55.0 1.4 broadcast_in_dim.36
  56.3 4.9 %all-to-all-start.1 = ((bf16[16,128,384]{2,1,0:T(8,128)(2,1)}), bf16[16,128,384]{2,1,0:T(8,128)(2,1)S(1)}, u32[]{:S(2)}, u32[]{:S(2)}) async-start(bf16[16,128,384]{2,1,0:T(8,128)(2,1)} %broadcast_in_dim.36), calls=%async_computation.1 | async-start | bytes 3145728 | tf_op jit(solution)/shard_map/all_to_all | solution.py:40
  61.3 37.9 %all-to-all-done.1 = bf16[16,128,384]{2,1,0:T(8,128)(2,1)S(1)} async-done(((bf16[16,128,384]{2,1,0:T(8,128)(2,1)}), bf16[16,128,384]{2,1,0:T(8,128)(2,1)S(1)}, u32[]{:S(2)}, u32[]{:S(2)}) %all-to-all-start.1) | async-done | bytes 1572896 | tf_op jit(solution)/shard_map/all_to_all | solution.py:40
  99.2 0.0 copy-start.2
  99.2 0.2 constant_dynamic-slice_fusion.1
  99.4 0.7 copy-done.2
  100.1 0.8 convolution_convert_fusion.1
  100.9 1.9 %collective-permute-start = (bf16[1024,384]{1,0:T(8,128)(2,1)S(1)}, bf16[1024,384]{1,0:T(8,128)(2,1)S(1)}, u32[]{:S(2)}, u32[]{:S(2)}) collective-permute-start(bf16[1024,384]{1,0:T(8,128)(2,1)S(1)} %convolution_convert_fusion.1), channel_id=1, source_target_pairs={{0,16},{16,0},{32,48},{48,32},{64,80},{80,64},{96,112},{112,96},{1... | collective-permute-start | bytes 2359304 | tf_op jit(solution)/shard_map/ppermute | solution.py:54
  102.9 2.3 %collective-permute-done = bf16[1024,384]{1,0:T(8,128)(2,1)S(1)} collective-permute-done((bf16[1024,384]{1,0:T(8,128)(2,1)S(1)}, bf16[1024,384]{1,0:T(8,128)(2,1)S(1)}, u32[]{:S(2)}, u32[]{:S(2)}) %collective-permute-start) | collective-permute-done | bytes 786464 | tf_op jit(solution)/shard_map/ppermute | solution.py:54
  105.1 1.7 %add_convert_fusion = bf16[1024,384]{1,0:T(8,128)(2,1)} fusion(bf16[1024,384]{1,0:T(8,128)(2,1)S(1)} %collective-permute-done, bf16[1024,384]{1,0:T(8,128)(2,1)S(1)} %bitcast.22, bf16[384,384]{1,0:T(8,128)(2,1)S(1)} %copy-done.2, f32[384]{0:T(512)S(1)} %get-tuple-element.10, f32[384]{0:T(512)S(1)} %get-tuple-element.11, f32[384]{0:T(512)S(1)} %get-tuple-element.9, ...), kind=kOutput, calls=%fused_computation.3 | convolution fusion | flops 304349184 | bytes 2662272 | tf_op jit(solution)/shard_map/dot_general | solution.py:47
  106.8 20.4 %all-to-all-start.2 = ((bf16[32,32,384]{2,1,0:T(8,128)(2,1)}), bf16[32,32,384]{2,1,0:T(8,128)(2,1)}, u32[]{:S(2)}, u32[]{:S(2)}) async-start(bf16[32,32,384]{2,1,0:T(8,128)(2,1)} %bitcast.21), calls=%async_computation.2 | async-start | bytes 1572864 | tf_op jit(solution)/shard_map/all_to_all | solution.py:60
  127.2 0.8 copy.12
  127.9 1.8 %fusion.1 = f32[384,384]{0,1:T(8,128)} fusion(bf16[2048,384]{1,0:T(8,128)(2,1)S(1)} %bitcast.19, bf16[2048,384]{1,0:T(8,128)(2,1)S(1)} %copy-done), kind=kOutput, calls=%fused_computation.7 | convolution fusion | flops 604127232 | bytes 3735552 | tf_op jit(solution)/shard_map/dot_general | solution.py:62
  129.7 2.1 %copy.13 = f32[384,384]{1,0:T(8,128)} copy(f32[384,384]{0,1:T(8,128)} %fusion.1) | data formatting | bytes 1179648
  131.9 18.9 %all-to-all-done.2 = bf16[32,32,384]{2,1,0:T(8,128)(2,1)} async-done(((bf16[32,32,384]{2,1,0:T(8,128)(2,1)}), bf16[32,32,384]{2,1,0:T(8,128)(2,1)}, u32[]{:S(2)}, u32[]{:S(2)}) %all-to-all-start.2) | async-done | bytes 786464 | tf_op jit(solution)/shard_map/all_to_all | solution.py:60
  150.8 1.9 %reduce_sum.22 = bf16[32,384]{1,0:T(8,128)(2,1)} reduce(bf16[32,32,384]{2,1,0:T(8,128)(2,1)} %all-to-all-done.2, bf16[]{:T(256)} %constant.65.clone.1), dimensions={0}, to_apply=%region_1.2 | reduce | flops 380928 | bytes 811010 | tf_op jit(solution)/shard_map/reduce_sum | solution.py:61
  (2 shorter events, 0.0 us)
Async XLA Ops:
  0.6 1.5 copy-start
  5.9 10.5 %copy-start.1 = (bf16[128,384]{1,0:T(8,128)(2,1)S(1)}, bf16[128,384]{1,0:T(8,128)(2,1)}, u32[]{:S(2)}) copy-start(bf16[128,384]{1,0:T(8,128)(2,1)} %param.7) | copy-start | bytes 294916
  5.9 48.6 %all-to-all-start = ((bf16[16,128,384]{1,2,0:T(8,128)(2,1)}), bf16[16,128,384]{1,2,0:T(8,128)(2,1)S(1)}, u32[]{:S(2)}, u32[]{:S(2)}) async-start(bf16[16,128,384]{1,2,0:T(8,128)(2,1)} %bitcast.20), calls=%async_computation | async-start | bytes 3145728 | tf_op jit(solution)/shard_map/all_to_all | solution.py:35
  56.3 42.8 %all-to-all-start.1 = ((bf16[16,128,384]{2,1,0:T(8,128)(2,1)}), bf16[16,128,384]{2,1,0:T(8,128)(2,1)S(1)}, u32[]{:S(2)}, u32[]{:S(2)}) async-start(bf16[16,128,384]{2,1,0:T(8,128)(2,1)} %broadcast_in_dim.36), calls=%async_computation.1 | async-start | bytes 3145728 | tf_op jit(solution)/shard_map/all_to_all | solution.py:40
  99.2 1.0 copy-start.2
  100.9 4.2 %collective-permute-start = (bf16[1024,384]{1,0:T(8,128)(2,1)S(1)}, bf16[1024,384]{1,0:T(8,128)(2,1)S(1)}, u32[]{:S(2)}, u32[]{:S(2)}) collective-permute-start(bf16[1024,384]{1,0:T(8,128)(2,1)S(1)} %convolution_convert_fusion.1), channel_id=1, source_target_pairs={{0,16},{16,0},{32,48},{48,32},{64,80},{80,64},{96,112},{112,96},{1... | collective-permute-start | bytes 2359304 | tf_op jit(solution)/shard_map/ppermute | solution.py:54
  106.8 43.9 %all-to-all-start.2 = ((bf16[32,32,384]{2,1,0:T(8,128)(2,1)}), bf16[32,32,384]{2,1,0:T(8,128)(2,1)}, u32[]{:S(2)}, u32[]{:S(2)}) async-start(bf16[32,32,384]{2,1,0:T(8,128)(2,1)} %bitcast.21), calls=%async_computation.2 | async-start | bytes 1572864 | tf_op jit(solution)/shard_map/all_to_all | solution.py:60

commit v2 on v0

v2 whole, which is shorter than its diff:
```python
import functools
import math

import jax
import jax.numpy as jnp
from jax import lax
from jax.experimental import pallas as pl
from jax.experimental.pallas import tpu as pltpu
from jax.sharding import PartitionSpec as P

BLOCK = 2048
F32 = jnp.float32
BF16 = jnp.bfloat16
ROOT = math.sqrt(2.0 / math.pi)
VMEM = pl.BlockSpec(memory_space=pltpu.VMEM)
SMEM = pl.BlockSpec(memory_space=pltpu.SMEM)


def call(kernel, outs, specs, flops, size, *args):
    return pl.pallas_call(
        kernel,
        out_shape=[jax.ShapeDtypeStruct(s, d) for s, d in outs],
        in_specs=specs,
        out_specs=[VMEM] * len(outs),
        compiler_params=pltpu.CompilerParams(vmem_limit_bytes=40 * 2**20),
        cost_estimate=pl.CostEstimate(flops=flops, bytes_accessed=size, transcendentals=0),
    )(*args)


def project(start_ref, tok_ref, codes_ref, scales_ref, w_ref, out_ref):
    feat, units = codes_ref.shape
    row = start_ref[0] + lax.broadcasted_iota(jnp.int32, (feat, units), 0)
    scale = jnp.broadcast_to(scales_ref[0:1, :], (feat, units))
    for i in range(1, scales_ref.shape[0]):
        scale = jnp.where(row >= i * BLOCK, scales_ref[i : i + 1, :], scale)
    weight = (codes_ref[...].astype(F32) * scale).astype(BF16)
    w_ref[...] = weight
    for q in range(out_ref.shape[0]):
        res = jnp.dot(tok_ref[:, q].reshape(-1, feat), weight, preferred_element_type=F32)
        out_ref[q] = res.astype(BF16).reshape(out_ref.shape[1:])


def activate(side_ref, got_ref, cot_ref, far_cot_ref, act_ref, far_act_ref, slope_ref):
    side = side_ref[0]
    for k, (cots, acts) in enumerate(((cot_ref, act_ref), (far_cot_ref, far_act_ref))):
        which = side if k == 0 else 1 - side
        pre = jnp.sum(got_ref[which].astype(F32), axis=0)
        cot = (cots[side] if k == 0 else cots[...]).astype(F32)
        square = pre * pre
        tanh = jnp.tanh(ROOT * (pre + 0.044715 * square * pre))
        acts[...] = (0.5 * pre * (1.0 + tanh)).astype(BF16)
        inner = ROOT * (1.0 + 3.0 * 0.044715 * square)
        grad = 0.5 * (1.0 + tanh) + 0.5 * pre * (1.0 - tanh * tanh) * inner
        slope = (cot * grad).astype(BF16)
        slope_ref[:, k] = jnp.broadcast_to(slope[None], (slope_ref.shape[0],) + slope.shape)


def back(core, slope_ref, weights):
    total = None
    for k, weight in enumerate(weights):
        rows = slope_ref[:, k, core]
        part = lax.dot_general(
            rows.reshape(-1, rows.shape[-1]),
            weight[...],
            (((1,), (1,)), ((), ())),
            preferred_element_type=F32,
        )
        total = part if total is None else total + part
    return total


def back_other(core_ref, slope_ref, w_ref, far_w_ref, out_ref):
    out_ref[...] = back(1 - core_ref[0], slope_ref, (w_ref, far_w_ref)).astype(BF16)


def back_mine(core_ref, slope_ref, w_ref, far_w_ref, other_ref, out_ref):
    total = back(core_ref[0], slope_ref, (w_ref, far_w_ref)) + other_ref[...].astype(F32)
    out_ref[...] = total.astype(BF16).reshape(out_ref.shape)


def finish(got_ref, out_ref):
    out_ref[...] = jnp.sum(got_ref[...].astype(F32), axis=0).astype(BF16)


def outer(side, tok_ref, slope_ref, k):
    rows = tok_ref[:, side]
    grads = slope_ref[:, k]
    return lax.dot_general(
        rows.reshape(-1, rows.shape[-1]),
        grads.reshape(-1, grads.shape[-1]),
        (((0,), (0,)), ((), ())),
        preferred_element_type=F32,
    )


def weigh_far(side_ref, tok_ref, slope_ref, out_ref):
    out_ref[...] = outer(side_ref[0], tok_ref, slope_ref, 1).astype(BF16)


def weigh_own(factor, side_ref, tok_ref, slope_ref, far_ref, out_ref):
    total = outer(side_ref[0], tok_ref, slope_ref, 0) + far_ref[...].astype(F32)
    out_ref[...] = total * factor


def shards(locals_, nodes, tokens, codes, scales, cotangent):
    rows, feat = tokens.shape
    units = codes.shape[1]
    per = nodes // locals_
    each = rows // nodes
    half = rows // locals_ // 2
    node = lax.axis_index("node").astype(jnp.int32)
    start = (lax.axis_index("local").astype(jnp.int32) * feat).reshape(1)
    core = (node % 2).reshape(1)
    side = (node // 2 % 2).reshape(1)
    tok = tokens.reshape(locals_, 2, half, feat)
    cot = cotangent.reshape(2, half, units)
    pair = [(i, i ^ 2) for i in range(nodes)]
    flops = 2 * rows * feat * units
    size = 2 * rows * feat

    weight, partial = call(
        project,
        [((feat, units), BF16), ((2, locals_, half, units), BF16)],
        [SMEM, VMEM, VMEM, VMEM],
        flops, 2 * size,
        start, tok, codes, scales,
    )
    members = [
        [(n + 2 * q) * locals_ + l for q in range(2) for l in range(locals_)]
        for n in range(nodes)
        if n & 2 == 0
    ]
    got = lax.all_to_all(
        partial.reshape(2 * locals_, half, units),
        ("node", "local"), 0, 0, axis_index_groups=members, tiled=True,
    ).reshape(2, locals_, half, units)
    far_weight = lax.ppermute(weight, "node", pair)
    far_cot = lax.ppermute(
        lax.dynamic_index_in_dim(cot, 1 - side[0], 0, False), "node", pair
    )
    act_own, act_far, slope = call(
        activate,
        [((half, units), BF16), ((half, units), BF16), ((locals_, 2, half, units), BF16)],
        [SMEM, VMEM, VMEM, VMEM],
        rows * units * 4, 2 * size,
        side, got, cot, far_cot,
    )
    spread = lax.all_to_all(
        slope.reshape(locals_, 2 * half, units), "local", 0, 0, tiled=True
    )
    by_core = spread.reshape(locals_, 2, 2, each, units)
    by_pair = spread.reshape(locals_, 2, half, units)
    (other,) = call(
        back_other,
        [((rows // 4, feat), BF16)],
        [SMEM, VMEM, VMEM, VMEM],
        flops // 2, size,
        core, by_core, weight, far_weight,
    )
    other = lax.ppermute(other, "node", [(i, i ^ 1) for i in range(nodes)])
    (both,) = call(
        back_mine,
        [((locals_, each, feat), BF16)],
        [SMEM, VMEM, VMEM, VMEM, VMEM],
        flops // 2, size,
        core, by_core, weight, far_weight, other,
    )
    groups = [list(range(c, nodes, per)) for c in range(per)]
    sums = lax.all_to_all(both, "node", 0, 0, axis_index_groups=groups, tiled=True)
    (far_part,) = call(
        weigh_far,
        [((feat, units), BF16)],
        [SMEM, VMEM, VMEM],
        flops // 2, size,
        side, tok, by_pair,
    )
    far_part = lax.ppermute(far_part, "node", pair)
    (weight_grad,) = call(
        functools.partial(weigh_own, rows ** (-0.5)),
        [((feat, units), F32)],
        [SMEM, VMEM, VMEM, VMEM],
        flops // 2, size,
        side, tok, by_pair, far_part,
    )
    (input_grad,) = call(
        finish, [((each, feat), BF16)], [VMEM], rows * feat, size // 4, sums
    )
    act_far = lax.ppermute(act_far, "node", pair)
    first = side[0] == 0
    act = jnp.concatenate(
        [jnp.where(first, act_own, act_far), jnp.where(first, act_far, act_own)], axis=0
    )
    return act, input_grad, weight_grad


def solution(mesh):
    body = functools.partial(shards, mesh.shape["local"], mesh.shape["node"])
    placed = (P(None, "local"), P("local", "node"), P(None, "node"), P("local", "node"))
    return jax.shard_map(
        lambda *args: body(*args),
        mesh=mesh,
        in_specs=placed,
        out_specs=(P("local", "node"), P("node", "local"), P("local", "node")),
        check_vma=False,
    )
```

time: 359 us -> 150 us (0.42)
  waiting for transfers between devices: 325 us -> 83.6 us
  starting transfers between devices: 0.12 us -> 48.2 us
  between operations: 13.8 us -> 0.84 us
  matrix products: 9.68 us -> 0 us
  Pallas kernels: 0 us -> 7.98 us
    reduce_scatter x2 -> x0, waiting for transfers between devices: 254 us -> none  [the longest x1 161 us: shards(): lax.psum_scatter(lax.dot_general(slope_full, weight, (((1,), (1,)), ((),...]
    all_gather x1 -> x0, waiting for transfers between devices: 71.4 us -> none  [shards(): slope_full = lax.all_gather(slope, 'local', axis=0, tiled=True)]
    all_to_all x0 -> x3, waiting for transfers between devices: none -> 44.8 us  [the longest x1 27.4 us: shards(): lax.all_to_all(slope.reshape(locals_, 2 * half, units), 'local', 0, 0, ti...]
    ppermute x0 -> x5, waiting for transfers between devices: none -> 38.9 us  [the longest x1 20.1 us: shards(): lax.ppermute(lax.dynamic_index_in_dim(cot, 1 - side[0], 0, False), 'node'...]
    all_to_all x0 -> x3, starting transfers between devices: none -> 35.9 us  [the longest x1 20.2 us: shards(): lax.all_to_all(both, 'node', 0, 0, axis_index_groups=groups, tiled=True)]
    ppermute x0 -> x5, starting transfers between devices: none -> 12.3 us  [the longest x1 2.98 us: shards(): far_part = lax.ppermute(far_part, 'node', pair)]
    dot_general x3 -> x0, matrix products: 9.68 us -> none  [the longest x1 4.24 us: shards(): lax.dot_general(slope_full, weight, (((1,), (1,)), ((), ())), preferred_e...]
    pallas_call x0 -> x7, Pallas kernels: none -> 7.98 us  [call(): pl.pallas_call(kernel, out_shape=[jax.ShapeDtypeStruct(s, d) for s, d in...]
  transfers between devices with their start and end apart: 3 -> 8, of which waited for: 3 -> 7; matrix products, arithmetic and copies ran while one was open for 1% -> 1% of each run, Pallas kernels for 0% -> 1%
where the time goes in v2:
time: 150 us; the launch traced here: 149 us
  waiting for transfers between devices  83.6 us (56%)
  starting transfers between devices  48.2 us (32%)
  Pallas kernels  7.98 us (5%)
  local copies, waits for them, and re-layouts  6.73 us (4%)
    all_to_all x1, waiting for transfers between devices, shards(): lax.all_to_all(slope.reshape(locals_, 2 * half, units), 'local', 0, 0, ti...  27.4 us
    all_to_all x1, starting transfers between devices, shards(): lax.all_to_all(both, 'node', 0, 0, axis_index_groups=groups, tiled=True)  20.2 us
    ppermute x1, waiting for transfers between devices, shards(): lax.ppermute(lax.dynamic_index_in_dim(cot, 1 - side[0], 0, False), 'node'...  20.1 us
    all_to_all x1, waiting for transfers between devices, shards(): lax.all_to_all(partial.reshape(2 * locals_, half, units), ('node', 'local...  17.3 us
    all_to_all x1, starting transfers between devices, shards(): lax.all_to_all(partial.reshape(2 * locals_, half, units), ('node', 'local...  12 us
    pallas_call x7, Pallas kernels, call(): pl.pallas_call(kernel, out_shape=[jax.ShapeDtypeStruct(s, d) for s, d in...  7.98 us
    ppermute x1, waiting for transfers between devices, shards(): far_weight = lax.ppermute(weight, 'node', pair)  7.59 us
    unnamed x22, local copies, waits for them, and re-layouts  6.72 us
  transfers between devices with their start and end apart: 8, of which 7 were waited for; matrix products, arithmetic and copies ran while one was open for 1% of the time, Pallas kernels for 1%

profile of v2, /device:TPU:14, one launch (start us, length us, event | category | flops | bytes accessed | tf_op | source)
XLA Modules:
  0.0 148.8 jit_solution(4936135105812822839)
XLA Ops:
  0.6 1.4 copy-done
  2.0 1.0 copy-done.8
  3.0 0.7 copy-done.10
  3.7 2.3 %shard_map.67 = (bf16[384,384]{1,0:T(8,128)(2,1)S(1)}, bf16[2,16,64,384]{3,2,1,0:T(8,128)(2,1)}) custom-call(s32[1]{0:T(128)} %bitcast.1.start_ref, bf16[16,2,64,384]{3,2,1,0:T(8,128)(2,1)S(1)} %bitcast.16, bf16[384,384]{1,0:T(8,128)(2,1)S(1)} %copy-done.8, f32[3,384]{1,0:T(4,128)S(1)} %copy-done.10), custom_call_target="tpu_custom_call" | custom-call | flops 603979776 | bytes 3145728 | tf_op jit(solution)/shard_map/pallas_call | solution.py:20
  6.0 12.0 %all-to-all-start = ((bf16[32,64,384]{2,1,0:T(8,128)(2,1)}), bf16[32,64,384]{2,1,0:T(8,128)(2,1)S(1)}, u32[]{:S(2)}, u32[]{:S(2)}) async-start(bf16[32,64,384]{2,1,0:T(8,128)(2,1)} %bitcast.3), calls=%async_computation | async-start | bytes 3145728 | tf_op jit(solution)/shard_map/all_to_all | solution.py:133
  18.1 2.1 %collective-permute-start = (bf16[64,384]{1,0:T(8,128)(2,1)S(1)}, bf16[64,384]{1,0:T(8,128)(2,1)S(1)}, u32[]{:S(2)}, u32[]{:S(2)}) collective-permute-start(bf16[64,384]{1,0:T(8,128)(2,1)S(1)} %dynamic-slice_bitcast_fusion), channel_id=1, source_target_pairs={{0,32},{16,48},{32,0},{48,16},{64,96},{80,112},{96,64},{112,80},{1... | collective-permute-start | bytes 147464 | tf_op jit(solution)/shard_map/ppermute | solution.py:138
  20.3 20.1 %collective-permute-done.far_cot_ref = bf16[64,384]{1,0:T(8,128)(2,1)S(1)} collective-permute-done((bf16[64,384]{1,0:T(8,128)(2,1)S(1)}, bf16[64,384]{1,0:T(8,128)(2,1)S(1)}, u32[]{:S(2)}, u32[]{:S(2)}) %collective-permute-start) | collective-permute-done | bytes 49184 | tf_op jit(solution)/shard_map/ppermute | solution.py:138
  40.4 17.3 %all-to-all-done = bf16[32,64,384]{2,1,0:T(8,128)(2,1)S(1)} async-done(((bf16[32,64,384]{2,1,0:T(8,128)(2,1)}), bf16[32,64,384]{2,1,0:T(8,128)(2,1)S(1)}, u32[]{:S(2)}, u32[]{:S(2)}) %all-to-all-start) | async-done | bytes 1572896 | tf_op jit(solution)/shard_map/all_to_all | solution.py:133
  57.7 1.7 %shard_map.68 = (bf16[64,384]{1,0:T(8,128)(2,1)S(1)}, bf16[64,384]{1,0:T(8,128)(2,1)S(1)}, bf16[16,2,64,384]{3,2,1,0:T(8,128)(2,1)}) custom-call(s32[1]{0:T(128)} %bitcast.side_ref, bf16[2,16,64,384]{3,2,1,0:T(8,128)(2,1)S(1)} %bitcast.19, bf16[2,64,384]{2,1,0:T(8,128)(2,1)S(1)} %bitcast.21, bf16[64,384]{1,0:T(8,128)(2,1)S(1)} %collective-permute-done.far_cot_ref), custom_call_target="tpu_custom_call" | custom-call | flops 3145728 | bytes 3145728 | tf_op jit(solution)/shard_map/pallas_call | solution.py:20
  59.4 0.6 copy-done.6
  60.0 0.6 copy-done.9
  60.6 3.7 %all-to-all-start.1 = ((bf16[16,128,384]{2,1,0:T(8,128)(2,1)}), bf16[16,128,384]{2,1,0:T(8,128)(2,1)S(1)}, u32[]{:S(2)}, u32[]{:S(2)}) async-start(bf16[16,128,384]{2,1,0:T(8,128)(2,1)} %bitcast.8), calls=%async_computation.1 | async-start | bytes 3145728 | tf_op jit(solution)/shard_map/all_to_all | solution.py:148
  64.3 2.2 %collective-permute-start.2 = (bf16[384,384]{1,0:T(8,128)(2,1)S(1)}, bf16[384,384]{1,0:T(8,128)(2,1)S(1)}, u32[]{:S(2)}, u32[]{:S(2)}) collective-permute-start(bf16[384,384]{1,0:T(8,128)(2,1)S(1)} %get-tuple-element.12.w_ref), channel_id=1, source_target_pairs={{0,32},{16,48},{32,0},{48,16},{64,96},{80,112},{96,64},{112,80},{1... | collective-permute-start | bytes 884744 | tf_op jit(solution)/shard_map/ppermute | solution.py:137
  66.6 7.6 %collective-permute-done.2.far_w_ref = bf16[384,384]{1,0:T(8,128)(2,1)S(1)} collective-permute-done((bf16[384,384]{1,0:T(8,128)(2,1)S(1)}, bf16[384,384]{1,0:T(8,128)(2,1)S(1)}, u32[]{:S(2)}, u32[]{:S(2)}) %collective-permute-start.2) | collective-permute-done | bytes 294944 | tf_op jit(solution)/shard_map/ppermute | solution.py:137
  74.2 27.4 %all-to-all-done.1 = bf16[16,128,384]{2,1,0:T(8,128)(2,1)S(1)} async-done(((bf16[16,128,384]{2,1,0:T(8,128)(2,1)}), bf16[16,128,384]{2,1,0:T(8,128)(2,1)S(1)}, u32[]{:S(2)}, u32[]{:S(2)}) %all-to-all-start.1) | async-done | bytes 1572896 | tf_op jit(solution)/shard_map/all_to_all | solution.py:148
  101.6 0.7 shard_map.69
  102.3 0.7 copy-done.3
  103.0 2.0 %collective-permute-start.3 = (bf16[512,384]{1,0:T(8,128)(2,1)S(1)}, bf16[512,384]{1,0:T(8,128)(2,1)S(1)}, u32[]{:S(2)}, u32[]{:S(2)}) collective-permute-start(bf16[512,384]{1,0:T(8,128)(2,1)S(1)} %shard_map.69), channel_id=1, source_target_pairs={{0,16},{16,0},{32,48},{48,32},{64,80},{80,64},{96,112},{112,96},{1... | collective-permute-start | bytes 1179656 | tf_op jit(solution)/shard_map/ppermute | solution.py:160
  105.0 1.7 %collective-permute-done.3.other_ref = bf16[512,384]{1,0:T(8,128)(2,1)S(1)} collective-permute-done((bf16[512,384]{1,0:T(8,128)(2,1)S(1)}, bf16[512,384]{1,0:T(8,128)(2,1)S(1)}, u32[]{:S(2)}, u32[]{:S(2)}) %collective-permute-start.3) | collective-permute-done | bytes 393248 | tf_op jit(solution)/shard_map/ppermute | solution.py:160
  106.7 1.0 copy-done.4
  107.7 0.7 shard_map.70
  108.4 0.7 copy-done.2
  109.1 20.2 %all-to-all-start.2 = ((bf16[16,32,384]{2,1,0:T(8,128)(2,1)}), bf16[16,32,384]{2,1,0:T(8,128)(2,1)S(1)}, u32[]{:S(2)}, u32[]{:S(2)}) async-start(bf16[16,32,384]{2,1,0:T(8,128)(2,1)} %copy-done.2), calls=%async_computation.2 | async-start | bytes 786432 | tf_op jit(solution)/shard_map/all_to_all | solution.py:169
  129.3 2.9 %collective-permute-start.1 = (bf16[64,384]{1,0:T(8,128)(2,1)}, bf16[64,384]{1,0:T(8,128)(2,1)}, u32[]{:S(2)}, u32[]{:S(2)}) collective-permute-start(bf16[64,384]{1,0:T(8,128)(2,1)} %copy-done.9), channel_id=1, source_target_pairs={{0,32},{16,48},{32,0},{48,16},{64,96},{80,112},{96,64},{112,80},{1... | collective-permute-start | bytes 147464 | tf_op jit(solution)/shard_map/ppermute | solution.py:188
  132.2 0.6 shard_map.72
  132.8 3.0 %collective-permute-start.4 = (bf16[384,384]{1,0:T(8,128)(2,1)S(1)}, bf16[384,384]{1,0:T(8,128)(2,1)S(1)}, u32[]{:S(2)}, u32[]{:S(2)}) collective-permute-start(bf16[384,384]{1,0:T(8,128)(2,1)S(1)} %shard_map.72), channel_id=1, source_target_pairs={{0,32},{16,48},{32,0},{48,16},{64,96},{80,112},{96,64},{112,80},{1... | collective-permute-start | bytes 884744 | tf_op jit(solution)/shard_map/ppermute | solution.py:177
  135.8 5.5 %collective-permute-done.1 = bf16[64,384]{1,0:T(8,128)(2,1)} collective-permute-done((bf16[64,384]{1,0:T(8,128)(2,1)}, bf16[64,384]{1,0:T(8,128)(2,1)}, u32[]{:S(2)}, u32[]{:S(2)}) %collective-permute-start.1) | collective-permute-done | bytes 49184 | tf_op jit(solution)/shard_map/ppermute | solution.py:188
  141.3 0.8 broadcast_select_fusion.1
  142.1 0.7 pad_maximum_fusion
  142.8 3.9 %collective-permute-done.4.far_ref = bf16[384,384]{1,0:T(8,128)(2,1)S(1)} collective-permute-done((bf16[384,384]{1,0:T(8,128)(2,1)S(1)}, bf16[384,384]{1,0:T(8,128)(2,1)S(1)}, u32[]{:S(2)}, u32[]{:S(2)}) %collective-permute-start.4) | collective-permute-done | bytes 294944 | tf_op jit(solution)/shard_map/ppermute | solution.py:177
  146.7 1.4 shard_map.73
  148.2 0.7 shard_map.71
  (16 shorter events, 0.0 us)
Async XLA Ops:
  0.6 1.4 copy-start
  2.0 1.0 copy-start.8
  3.0 0.7 copy-start.10
  6.0 12.1 %copy-start.5 = (bf16[128,384]{1,0:T(8,128)(2,1)S(1)}, bf16[128,384]{1,0:T(8,128)(2,1)}, u32[]{:S(2)}) copy-start(bf16[128,384]{1,0:T(8,128)(2,1)} %param.7) | copy-start | bytes 294916
  6.0 51.7 %all-to-all-start = ((bf16[32,64,384]{2,1,0:T(8,128)(2,1)}), bf16[32,64,384]{2,1,0:T(8,128)(2,1)S(1)}, u32[]{:S(2)}, u32[]{:S(2)}) async-start(bf16[32,64,384]{2,1,0:T(8,128)(2,1)} %bitcast.3), calls=%async_computation | async-start | bytes 3145728 | tf_op jit(solution)/shard_map/all_to_all | solution.py:133
  18.1 22.3 %collective-permute-start = (bf16[64,384]{1,0:T(8,128)(2,1)S(1)}, bf16[64,384]{1,0:T(8,128)(2,1)S(1)}, u32[]{:S(2)}, u32[]{:S(2)}) collective-permute-start(bf16[64,384]{1,0:T(8,128)(2,1)S(1)} %dynamic-slice_bitcast_fusion), channel_id=1, source_target_pairs={{0,32},{16,48},{32,0},{48,16},{64,96},{80,112},{96,64},{112,80},{1... | collective-permute-start | bytes 147464 | tf_op jit(solution)/shard_map/ppermute | solution.py:138
  59.4 0.6 copy-start.6
  60.0 0.6 copy-start.9
  60.6 41.0 %all-to-all-start.1 = ((bf16[16,128,384]{2,1,0:T(8,128)(2,1)}), bf16[16,128,384]{2,1,0:T(8,128)(2,1)S(1)}, u32[]{:S(2)}, u32[]{:S(2)}) async-start(bf16[16,128,384]{2,1,0:T(8,128)(2,1)} %bitcast.8), calls=%async_computation.1 | async-start | bytes 3145728 | tf_op jit(solution)/shard_map/all_to_all | solution.py:148
  64.3 9.8 %collective-permute-start.2 = (bf16[384,384]{1,0:T(8,128)(2,1)S(1)}, bf16[384,384]{1,0:T(8,128)(2,1)S(1)}, u32[]{:S(2)}, u32[]{:S(2)}) collective-permute-start(bf16[384,384]{1,0:T(8,128)(2,1)S(1)} %get-tuple-element.12.w_ref), channel_id=1, source_target_pairs={{0,32},{16,48},{32,0},{48,16},{64,96},{80,112},{96,64},{112,80},{1... | collective-permute-start | bytes 884744 | tf_op jit(solution)/shard_map/ppermute | solution.py:137
  102.3 0.7 copy-start.3
  103.0 29.2 %copy-start.1 = (bf16[2048,384]{1,0:T(8,128)(2,1)S(1)}, bf16[2048,384]{1,0:T(8,128)(2,1)}, u32[]{:S(2)}) copy-start(bf16[2048,384]{1,0:T(8,128)(2,1)} %param.4) | copy-start | bytes 4718596
  103.0 3.7 %collective-permute-start.3 = (bf16[512,384]{1,0:T(8,128)(2,1)S(1)}, bf16[512,384]{1,0:T(8,128)(2,1)S(1)}, u32[]{:S(2)}, u32[]{:S(2)}) collective-permute-start(bf16[512,384]{1,0:T(8,128)(2,1)S(1)} %shard_map.69), channel_id=1, source_target_pairs={{0,16},{16,0},{32,48},{48,32},{64,80},{80,64},{96,112},{112,96},{1... | collective-permute-start | bytes 1179656 | tf_op jit(solution)/shard_map/ppermute | solution.py:160
  106.7 1.0 copy-start.4
  108.3 0.8 copy-start.2
  109.1 39.1 %all-to-all-start.2 = ((bf16[16,32,384]{2,1,0:T(8,128)(2,1)}), bf16[16,32,384]{2,1,0:T(8,128)(2,1)S(1)}, u32[]{:S(2)}, u32[]{:S(2)}) async-start(bf16[16,32,384]{2,1,0:T(8,128)(2,1)} %copy-done.2), calls=%async_computation.2 | async-start | bytes 786432 | tf_op jit(solution)/shard_map/all_to_all | solution.py:169
  129.3 12.0 %collective-permute-start.1 = (bf16[64,384]{1,0:T(8,128)(2,1)}, bf16[64,384]{1,0:T(8,128)(2,1)}, u32[]{:S(2)}, u32[]{:S(2)}) collective-permute-start(bf16[64,384]{1,0:T(8,128)(2,1)} %copy-done.9), channel_id=1, source_target_pairs={{0,32},{16,48},{32,0},{48,16},{64,96},{80,112},{96,64},{112,80},{1... | collective-permute-start | bytes 147464 | tf_op jit(solution)/shard_map/ppermute | solution.py:188
  132.2 9.2 %copy-start.7 = (bf16[64,384]{1,0:T(8,128)(2,1)S(1)}, bf16[64,384]{1,0:T(8,128)(2,1)}, u32[]{:S(2)}) copy-start(bf16[64,384]{1,0:T(8,128)(2,1)} %copy-done.6) | copy-start | bytes 147460
  132.8 13.9 %collective-permute-start.4 = (bf16[384,384]{1,0:T(8,128)(2,1)S(1)}, bf16[384,384]{1,0:T(8,128)(2,1)S(1)}, u32[]{:S(2)}, u32[]{:S(2)}) collective-permute-start(bf16[384,384]{1,0:T(8,128)(2,1)S(1)} %shard_map.72), channel_id=1, source_target_pairs={{0,32},{16,48},{32,0},{48,16},{64,96},{80,112},{96,64},{112,80},{1... | collective-permute-start | bytes 884744 | tf_op jit(solution)/shard_map/ppermute | solution.py:177

commit v3 on v2

v3 whole, which is shorter than its diff:
```python
import functools
import math

import jax
import jax.numpy as jnp
from jax import lax
from jax.experimental import pallas as pl
from jax.experimental.pallas import tpu as pltpu
from jax.sharding import PartitionSpec as P

BLOCK = 2048
F32 = jnp.float32
BF16 = jnp.bfloat16
ROOT = math.sqrt(2.0 / math.pi)
VMEM = pl.BlockSpec(memory_space=pltpu.VMEM)
SMEM = pl.BlockSpec(memory_space=pltpu.SMEM)


def call(kernel, outs, specs, flops, size, *args):
    return pl.pallas_call(
        kernel,
        out_shape=[jax.ShapeDtypeStruct(s, d) for s, d in outs],
        in_specs=specs,
        out_specs=[VMEM] * len(outs),
        compiler_params=pltpu.CompilerParams(vmem_limit_bytes=40 * 2**20),
        cost_estimate=pl.CostEstimate(flops=flops, bytes_accessed=size, transcendentals=0),
    )(*args)


HBM = pl.BlockSpec(memory_space=pltpu.HBM)


def project(start_ref, tok_hbm, codes_hbm, scales_hbm, w_ref, out_ref, tok_ref, codes_ref, scales_ref, sems):
    feat, units = codes_ref.shape
    cuts = [(z, y) for z in range(2) for y in (0, 1)]
    span = tok_ref.shape[1] // 2
    first = [
        pltpu.make_async_copy(codes_hbm, codes_ref, sems.at[0]),
        pltpu.make_async_copy(scales_hbm, scales_ref, sems.at[1]),
    ]
    loads = [
        pltpu.make_async_copy(
            tok_hbm.at[z, pl.ds(y * span, span)],
            tok_ref.at[z, pl.ds(y * span, span)],
            sems.at[2 + i],
        )
        for i, (z, y) in enumerate(cuts)
    ]
    for copy in first + loads:
        copy.start()
    for copy in first:
        copy.wait()
    row = start_ref[0] + lax.broadcasted_iota(jnp.int32, (feat, units), 0)
    scale = jnp.broadcast_to(scales_ref[0:1, :], (feat, units))
    for i in range(1, scales_ref.shape[0]):
        scale = jnp.where(row >= i * BLOCK, scales_ref[i : i + 1, :], scale)
    weight = (codes_ref[...].astype(F32) * scale).astype(BF16)
    w_ref[...] = weight
    for (z, y), copy in zip(cuts, loads):
        copy.wait()
        ys = slice(y * span, (y + 1) * span)
        piece = tok_ref[z, ys]
        res = jnp.dot(piece.reshape(-1, feat), weight, preferred_element_type=F32)
        res = res.astype(BF16).reshape(piece.shape[:-1] + (units,))
        for h in range(2):
            out_ref[h, ys, z] = res[:, :, h]


def activate(side_ref, got_ref, cot_ref, far_cot_ref, act_ref, far_act_ref, slope_ref):
    side = side_ref[0]
    for k in range(2):
        which = side if k == 0 else 1 - side
        pre = jnp.sum(got_ref[:, which].astype(F32), axis=0)
        cot = cot_ref[:, side] if k == 0 else far_cot_ref[...]
        cot = cot.reshape(pre.shape).astype(F32)
        square = pre * pre
        tanh = jnp.tanh(ROOT * (pre + 0.044715 * square * pre))
        act = (0.5 * pre * (1.0 + tanh)).astype(BF16)
        if k == 0:
            act_ref[...] = act
        else:
            far_act_ref[...] = act
        inner = ROOT * (1.0 + 3.0 * 0.044715 * square)
        grad = 0.5 * (1.0 + tanh) + 0.5 * pre * (1.0 - tanh * tanh) * inner
        slope_ref[which] = (cot * grad).astype(BF16)


def back(core, slope_ref, w_ref):
    rows = slope_ref[:, :, :, core]
    return lax.dot_general(
        rows.reshape(-1, rows.shape[-1]),
        w_ref[...],
        (((1,), (1,)), ((), ())),
        preferred_element_type=F32,
    )


def back_other(core_ref, slope_ref, w_ref, far_w_ref, out_ref):
    core = 1 - core_ref[0]
    for k, weight in enumerate((w_ref, far_w_ref)):
        out_ref[k] = back(core, slope_ref, weight).astype(BF16)


def back_mine(core_ref, side_ref, slope_ref, w_ref, far_w_ref, other_ref, out_ref):
    core, side = core_ref[0], side_ref[0]
    for k, weight in enumerate((w_ref, far_w_ref)):
        total = back(core, slope_ref, weight) + other_ref[k].astype(F32)
        which = side if k == 0 else 1 - side
        out_ref[which] = total.astype(BF16).reshape(out_ref.shape[1:])


def finish(got_ref, out_ref):
    out_ref[...] = jnp.sum(got_ref[...].astype(F32), axis=1).astype(BF16)


def outer(rows, grads):
    return lax.dot_general(
        rows.reshape(-1, rows.shape[-1]),
        grads.reshape(-1, grads.shape[-1]),
        (((0,), (0,)), ((), ())),
        preferred_element_type=F32,
    )


def weigh_far(far_tok_ref, slope_ref, out_ref):
    total = sum(outer(far_tok_ref[z], slope_ref[:, z]) for z in range(2))
    out_ref[...] = total.astype(BF16)


def weigh_own(factor, side_ref, tok_ref, slope_ref, far_ref, out_ref):
    side = side_ref[0]
    total = sum(outer(tok_ref[z, :, :, side], slope_ref[:, z]) for z in range(2))
    out_ref[...] = (total + far_ref[...].astype(F32)) * factor


def shards(locals_, nodes, tokens, codes, scales, cotangent):
    rows, feat = tokens.shape
    units = codes.shape[1]
    ys = locals_ // 2
    per = nodes // locals_
    sub = rows // nodes // 2
    mine = per * sub
    node = lax.axis_index("node").astype(jnp.int32)
    local = lax.axis_index("local").astype(jnp.int32)
    start = (local * feat).reshape(1)
    core = (node % 2).reshape(1)
    side = (local // ys).reshape(1)
    tok = tokens.reshape(2, ys, per, 2, sub, feat)
    cot = cotangent.reshape(per, 2, sub, units)
    pair = [(i, (i + ys) % locals_) for i in range(locals_)]
    flops = 2 * rows * feat * units
    size = 2 * rows * feat

    weight, partial = pl.pallas_call(
        project,
        out_shape=[
            jax.ShapeDtypeStruct((feat, units), BF16),
            jax.ShapeDtypeStruct((2, ys, 2, per, sub, units), BF16),
        ],
        in_specs=[SMEM, HBM, HBM, HBM],
        out_specs=[VMEM, VMEM],
        scratch_shapes=[
            pltpu.VMEM(tok.shape, BF16),
            pltpu.VMEM(codes.shape, BF16),
            pltpu.VMEM(scales.shape, F32),
            pltpu.SemaphoreType.DMA((6,)),
        ],
        compiler_params=pltpu.CompilerParams(vmem_limit_bytes=58 * 2**20),
        cost_estimate=pl.CostEstimate(flops=flops, bytes_accessed=2 * size, transcendentals=0),
    )(start, tok, codes, scales)
    got = lax.all_to_all(
        partial.reshape(locals_, 2 * mine, units), "local", 0, 0, tiled=True
    ).reshape(locals_, 2, mine, units)
    far_cot = lax.ppermute(
        lax.dynamic_index_in_dim(cot, 1 - side[0], 1, False), "local", pair
    )
    far_weight = lax.ppermute(weight, "local", pair)
    block = nodes // 4
    step = [
        (n * locals_ + l, (n + (block if l >= ys else -block)) % nodes * locals_ + (l + ys) % locals_)
        for n in range(nodes)
        for l in range(locals_)
    ]
    far_tok = lax.ppermute(
        lax.dynamic_index_in_dim(tok, 1 - side[0], 3, False), ("node", "local"), step
    )
    got, far_cot, far_weight, far_tok = lax.optimization_barrier(
        (got, far_cot, far_weight, far_tok)
    )
    act_own, act_far, slope = call(
        activate,
        [((mine, units), BF16), ((mine, units), BF16), ((2, mine, units), BF16)],
        [SMEM, VMEM, VMEM, VMEM],
        rows * units * 4, size,
        side, got, cot, far_cot,
    )
    lines = [list(range(z * ys, (z + 1) * ys)) for z in range(2)]
    spread = lax.all_gather(
        slope.reshape(2 * mine, units), "local", axis=0, tiled=True, axis_index_groups=lines
    )
    by_core = spread.reshape(ys, 2, per // 2, 2, sub, units)
    by_side = spread.reshape(ys, 2, per, sub, units)
    (other,) = call(
        back_other,
        [((2, rows // 4, feat), BF16)],
        [SMEM, VMEM, VMEM, VMEM],
        flops // 2, size,
        core, by_core, weight, far_weight,
    )
    other = lax.ppermute(other, "node", [(i, i ^ 1) for i in range(nodes)])
    (far_part,) = call(
        weigh_far, [((feat, units), BF16)], [VMEM, VMEM], flops // 2, size, far_tok, by_side
    )
    far_part = lax.ppermute(far_part, "local", pair)
    (both,) = call(
        back_mine,
        [((2, ys, 2, per // 2, sub, feat), BF16)],
        [SMEM, SMEM, VMEM, VMEM, VMEM, VMEM],
        flops // 2, size,
        core, side, by_core, weight, far_weight, other,
    )
    groups = [
        [
            (per * (ys * t + y) + 2 * h + c) * locals_ + z * ys + own
            for z in range(2)
            for y in range(ys)
            for t in range(2)
            for h in range(per // 2)
        ]
        for c in range(2)
        for own in range(ys)
    ]
    sums = lax.all_to_all(
        both.reshape(nodes, sub, feat),
        ("node", "local"), 0, 0, axis_index_groups=groups, tiled=True,
    ).reshape(2, nodes // 2, sub, feat)
    (weight_grad,) = call(
        functools.partial(weigh_own, rows ** (-0.5)),
        [((feat, units), F32)],
        [SMEM, VMEM, VMEM, VMEM],
        flops // 2, size,
        side, tok, by_side, far_part,
    )
    (input_grad,) = call(
        finish, [((2, sub, feat), BF16)], [VMEM], rows * feat, size // 2, sums
    )
    act_far = lax.ppermute(act_far, "local", pair)
    first = side[0] == 0
    act_own, act_far = act_own.reshape(per, sub, units), act_far.reshape(per, sub, units)
    act = jnp.stack(
        [jnp.where(first, act_own, act_far), jnp.where(first, act_far, act_own)], axis=1
    )
    return (
        act.reshape(rows // locals_, units),
        input_grad.reshape(rows // nodes, feat),
        weight_grad,
    )


def solution(mesh):
    body = functools.partial(shards, mesh.shape["local"], mesh.shape["node"])
    placed = (P(None, "local"), P("local", "node"), P(None, "node"), P("local", "node"))
    return jax.shard_map(
        lambda *args: body(*args),
        mesh=mesh,
        in_specs=placed,
        out_specs=(P("local", "node"), P("node", "local"), P("local", "node")),
        check_vma=False,
    )
```

time: 150 us -> 141 us (0.940)
  waiting for transfers between devices: 83.6 us -> 34.1 us
  blocking collectives: 0 us -> 26.3 us
  starting transfers between devices: 48.2 us -> 60.9 us
  Pallas kernels: 7.98 us -> 12.3 us
  local copies, waits for them, and re-layouts: 6.73 us -> 3.19 us
    all_to_all x3 -> x2, waiting for transfers between devices: 44.8 us -> 3.48 us  [the longest x1 3.48 us: shards(): lax.all_to_all(partial.reshape(locals_, 2 * mine, units), 'local', 0, 0,...]
    all_gather x0 -> x1, blocking collectives: none -> 26.3 us  [shards(): lax.all_gather(slope.reshape(2 * mine, units), 'local', axis=0, tiled=Tru...]
    ppermute x4 -> x5, starting transfers between devices: 10.2 us -> 27.6 us  [the longest x1 15.9 us: shards(): lax.ppermute(lax.dynamic_index_in_dim(tok, 1 - side[0], 3, False), ('node...]
    ppermute x4 -> x5, waiting for transfers between devices: 37.2 us -> 28.4 us  [the longest x1 12.3 us: shards(): act_far = lax.ppermute(act_far, 'local', pair)]
    unnamed x22 -> x16, local copies, waits for them, and re-layouts: 6.72 us -> 0.91 us
    all_to_all x3 -> x2, starting transfers between devices: 35.9 us -> 31.3 us  [the longest x1 20.8 us: shards(): lax.all_to_all(both.reshape(nodes, sub, feat), ('node', 'local'), 0, 0, a...]
    pallas_call x0 -> x1, Pallas kernels: none -> 4.07 us  [shards(): pl.pallas_call(project, out_shape=[jax.ShapeDtypeStruct((feat, units), BF...]
    squeeze x1 -> x2, local copies, waits for them, and re-layouts: 0.01 us -> 1.62 us  [the longest x1 0.99 us: shards(): lax.dynamic_index_in_dim(tok, 1 - side[0], 3, False)]
  transfers between devices with their start and end apart: 8 -> 8, of which waited for: 7 -> 5; matrix products, arithmetic and copies ran while one was open for 1% -> 2% of each run, Pallas kernels for 1% -> 2%
where the time goes in v3:
time: 141 us; the launch traced here: 139 us
  starting transfers between devices  60.9 us (43%)
  waiting for transfers between devices  34.1 us (24%)
  blocking collectives  26.3 us (19%)
  Pallas kernels  12.3 us (9%)
  local copies, waits for them, and re-layouts  3.19 us (2%)
    all_gather x1, blocking collectives, shards(): lax.all_gather(slope.reshape(2 * mine, units), 'local', axis=0, tiled=Tru...  26.3 us
    all_to_all x1, starting transfers between devices, shards(): lax.all_to_all(both.reshape(nodes, sub, feat), ('node', 'local'), 0, 0, a...  20.8 us
    ppermute x1, starting transfers between devices, shards(): lax.ppermute(lax.dynamic_index_in_dim(tok, 1 - side[0], 3, False), ('node...  15.9 us
    ppermute x1, waiting for transfers between devices, shards(): act_far = lax.ppermute(act_far, 'local', pair)  12.3 us
    ppermute x1, waiting for transfers between devices, shards(): lax.ppermute(lax.dynamic_index_in_dim(cot, 1 - side[0], 1, False), 'local...  11.1 us
    all_to_all x1, starting transfers between devices, shards(): lax.all_to_all(partial.reshape(locals_, 2 * mine, units), 'local', 0, 0,...  10.5 us
    pallas_call x6, Pallas kernels, call(): pl.pallas_call(kernel, out_shape=[jax.ShapeDtypeStruct(s, d) for s, d in...  8.27 us
    ppermute x1, waiting for transfers between devices, shards(): far_part = lax.ppermute(far_part, 'local', pair)  4.98 us
  transfers between devices with their start and end apart: 8, of which 5 were waited for; matrix products, arithmetic and copies ran while one was open for 2% of the time, Pallas kernels for 2%

profile of v3, /device:TPU:14, one launch (start us, length us, event | category | flops | bytes accessed | tf_op | source)
XLA Modules:
  0.0 138.5 jit_solution(12077470382532931859)
XLA Ops:
  0.6 4.1 %shard_map.67 = (bf16[384,384]{1,0:T(8,128)(2,1)}, bf16[2,8,2,4,16,384]{5,4,3,2,1,0:T(8,128)(2,1)}) custom-call(s32[1]{0:T(128)} %bitcast.1.start_ref, bf16[2,8,4,2,16,384]{5,4,3,2,1,0:T(8,128)(2,1)} %bitcast.25, bf16[384,384]{1,0:T(8,128)(2,1)} %codes_hbm.1, f32[3,384]{1,0:T(4,128)} %scales_hbm.1), custom_call_target="tpu_custom_call" | custom-call | flops 603979776 | bytes 3145728 | tf_op jit(solution)/shard_map/pallas_call | solution.py:154
  4.7 0.0 copy-start
  4.7 10.5 %all-to-all-start = ((bf16[16,128,384]{2,1,0:T(8,128)(2,1)}), bf16[16,128,384]{2,1,0:T(8,128)(2,1)S(1)}, u32[]{:S(2)}, u32[]{:S(2)}) async-start(bf16[16,128,384]{2,1,0:T(8,128)(2,1)} %bitcast.33), calls=%async_computation | async-start | bytes 3145728 | tf_op jit(solution)/shard_map/all_to_all | solution.py:171
  15.3 0.0 copy-start.2
  15.3 0.0 copy-start.3
  15.3 1.0 dynamic-slice_bitcast_fusion
  16.3 15.9 %collective-permute-start.2 = (bf16[2,8,4,16,384]{4,3,2,1,0:T(8,128)(2,1)}, bf16[2,8,4,16,384]{4,3,2,1,0:T(8,128)(2,1)}, u32[]{:S(2)}, u32[]{:S(2)}) collective-permute-start(bf16[2,8,4,16,384]{4,3,2,1,0:T(8,128)(2,1)} %dynamic-slice_bitcast_fusion), channel_id=1, source_target_pairs={{0,776},{1,777},{2,778},{3,779},{4,780},{5,781},{6,782},{7,783},{8... | collective-permute-start | bytes 2359304 | tf_op jit(solution)/shard_map/ppermute | solution.py:184
  32.3 1.9 %collective-permute-start.1 = (bf16[384,384]{1,0:T(8,128)(2,1)S(1)}, bf16[384,384]{1,0:T(8,128)(2,1)}, u32[]{:S(2)}, u32[]{:S(2)}) collective-permute-start(bf16[384,384]{1,0:T(8,128)(2,1)S(1)} %copy-done.2), channel_id=1, source_target_pairs={{0,8},{1,9},{2,10},{3,11},{4,12},{5,13},{6,14},{7,15},{8,0},{9,1},... | collective-permute-start | bytes 884744 | tf_op jit(solution)/shard_map/ppermute | solution.py:177
  34.2 0.6 dynamic-slice_bitcast_fusion.1
  34.8 3.9 %collective-permute-start = (bf16[4,16,384]{2,1,0:T(8,128)(2,1)}, bf16[4,16,384]{2,1,0:T(8,128)(2,1)}, u32[]{:S(2)}, u32[]{:S(2)}) collective-permute-start(bf16[4,16,384]{2,1,0:T(8,128)(2,1)} %dynamic-slice_bitcast_fusion.1), channel_id=1, source_target_pairs={{0,8},{1,9},{2,10},{3,11},{4,12},{5,13},{6,14},{7,15},{8,0},{9,1},... | collective-permute-start | bytes 147464 | tf_op jit(solution)/shard_map/ppermute | solution.py:174
  38.8 11.1 %collective-permute-done.far_cot_ref = bf16[4,16,384]{2,1,0:T(8,128)(2,1)} collective-permute-done((bf16[4,16,384]{2,1,0:T(8,128)(2,1)}, bf16[4,16,384]{2,1,0:T(8,128)(2,1)}, u32[]{:S(2)}, u32[]{:S(2)}) %collective-permute-start) | collective-permute-done | bytes 49184 | tf_op jit(solution)/shard_map/ppermute | solution.py:174
  49.8 0.0 collective-permute-done.1.far_w_ref
  49.9 3.5 %all-to-all-done = bf16[16,128,384]{2,1,0:T(8,128)(2,1)S(1)} async-done(((bf16[16,128,384]{2,1,0:T(8,128)(2,1)}), bf16[16,128,384]{2,1,0:T(8,128)(2,1)S(1)}, u32[]{:S(2)}, u32[]{:S(2)}) %all-to-all-start) | async-done | bytes 1572896 | tf_op jit(solution)/shard_map/all_to_all | solution.py:171
  53.3 1.2 shard_map.68
  54.5 0.0 copy-start.4
  54.5 0.0 copy-start.6
  54.5 26.3 %all_gather.3 = bf16[1024,384]{1,0:T(8,128)(2,1)S(1)} all-gather(bf16[128,384]{1,0:T(8,128)(2,1)S(1)} %bitcast.32), channel_id=1, replica_groups={{0,1,2,3,4,5,6,7},{8,9,10,11,12,13,14,15},{16,17,18,19,20,21,22,23},{24..., dimensions={0}, use_global_device_ids=true | all-gather | bytes 884736 | tf_op jit(solution)/shard_map/all_gather | solution.py:198
  80.8 1.6 %shard_map.69 = bf16[2,512,384]{2,1,0:T(8,128)(2,1)S(1)} custom-call(s32[1]{0:T(128)} %bitcast.11.core_ref, bf16[8,2,2,2,16,384]{5,4,3,2,1,0:T(8,128)(2,1)S(1)} %bitcast.20, bf16[384,384]{1,0:T(8,128)(2,1)S(1)} %copy-done.2, bf16[384,384]{1,0:T(8,128)(2,1)} %collective-permute-done.1.far_w_ref), custom_call_target="tpu_custom_call" | custom-call | flops 301989888 | bytes 1572864 | tf_op jit(solution)/shard_map/pallas_call | solution.py:20
  82.5 1.9 %collective-permute-start.4 = (bf16[2,512,384]{2,1,0:T(8,128)(2,1)S(1)}, bf16[2,512,384]{2,1,0:T(8,128)(2,1)S(1)}, u32[]{:S(2)}, u32[]{:S(2)}) collective-permute-start(bf16[2,512,384]{2,1,0:T(8,128)(2,1)S(1)} %shard_map.69), channel_id=1, source_target_pairs={{0,16},{16,0},{32,48},{48,32},{64,80},{80,64},{96,112},{112,96},{1... | collective-permute-start | bytes 2359304 | tf_op jit(solution)/shard_map/ppermute | solution.py:210
  84.4 2.3 %collective-permute-done.4.other_ref = bf16[2,512,384]{2,1,0:T(8,128)(2,1)S(1)} collective-permute-done((bf16[2,512,384]{2,1,0:T(8,128)(2,1)S(1)}, bf16[2,512,384]{2,1,0:T(8,128)(2,1)S(1)}, u32[]{:S(2)}, u32[]{:S(2)}) %collective-permute-start.4) | collective-permute-done | bytes 786464 | tf_op jit(solution)/shard_map/ppermute | solution.py:210
  86.6 1.6 %shard_map.70 = bf16[2,8,2,2,16,384]{5,4,3,2,1,0:T(8,128)(2,1)S(1)} custom-call(s32[1]{0:T(128)} %bitcast.11.core_ref, s32[1]{0:T(128)} %bitcast.side_ref, bf16[8,2,2,2,16,384]{5,4,3,2,1,0:T(8,128)(2,1)S(1)} %bitcast.21, bf16[384,384]{1,0:T(8,128)(2,1)S(1)} %copy-done.2, bf16[384,384]{1,0:T(8,128)(2,1)} %collective-permute-done.1.far_w_ref, ...), custom_call_target="tpu_custom_call" | custom-call | flops 301989888 | bytes 1572864 | tf_op jit(solution)/shard_map/pallas_call | solution.py:20
  88.3 0.9 copy-done.1
  89.2 20.8 %all-to-all-start.1 = ((bf16[64,16,384]{2,1,0:T(8,128)(2,1)}), bf16[64,16,384]{2,1,0:T(8,128)(2,1)S(1)}, u32[]{:S(2)}, u32[]{:S(2)}) async-start(bf16[64,16,384]{2,1,0:T(8,128)(2,1)} %bitcast.29), calls=%async_computation.1 | async-start | bytes 1572864 | tf_op jit(solution)/shard_map/all_to_all | solution.py:233
  110.0 3.6 %collective-permute-start.3 = (bf16[64,384]{1,0:T(8,128)(2,1)S(1)}, bf16[64,384]{1,0:T(8,128)(2,1)}, u32[]{:S(2)}, u32[]{:S(2)}) collective-permute-start(bf16[64,384]{1,0:T(8,128)(2,1)S(1)} %copy-done.7), channel_id=1, source_target_pairs={{0,8},{1,9},{2,10},{3,11},{4,12},{5,13},{6,14},{7,15},{8,0},{9,1},... | collective-permute-start | bytes 147464 | tf_op jit(solution)/shard_map/ppermute | solution.py:247
  113.6 1.7 %shard_map.72 = bf16[384,384]{1,0:T(8,128)(2,1)S(1)} custom-call(bf16[2,8,4,16,384]{4,3,2,1,0:T(8,128)(2,1)} %collective-permute-done.2.far_tok_ref, bf16[8,2,4,16,384]{4,3,2,1,0:T(8,128)(2,1)S(1)} %bitcast.22), custom_call_target="tpu_custom_call" | custom-call | flops 301989888 | bytes 1572864 | tf_op jit(solution)/shard_map/pallas_call | solution.py:20
  115.3 2.3 %collective-permute-start.5 = (bf16[384,384]{1,0:T(8,128)(2,1)S(1)}, bf16[384,384]{1,0:T(8,128)(2,1)S(1)}, u32[]{:S(2)}, u32[]{:S(2)}) collective-permute-start(bf16[384,384]{1,0:T(8,128)(2,1)S(1)} %shard_map.72), channel_id=1, source_target_pairs={{0,8},{1,9},{2,10},{3,11},{4,12},{5,13},{6,14},{7,15},{8,0},{9,1},... | collective-permute-start | bytes 884744 | tf_op jit(solution)/shard_map/ppermute | solution.py:214
  117.6 12.3 %collective-permute-done.3 = bf16[64,384]{1,0:T(8,128)(2,1)} collective-permute-done((bf16[64,384]{1,0:T(8,128)(2,1)S(1)}, bf16[64,384]{1,0:T(8,128)(2,1)}, u32[]{:S(2)}, u32[]{:S(2)}) %collective-permute-start.3) | collective-permute-done | bytes 49184 | tf_op jit(solution)/shard_map/ppermute | solution.py:247
  129.9 0.8 broadcast_select_fusion.1
  130.8 0.7 copy.7
  131.4 5.0 %collective-permute-done.5.far_ref = bf16[384,384]{1,0:T(8,128)(2,1)S(1)} collective-permute-done((bf16[384,384]{1,0:T(8,128)(2,1)S(1)}, bf16[384,384]{1,0:T(8,128)(2,1)S(1)}, u32[]{:S(2)}, u32[]{:S(2)}) %collective-permute-start.5) | collective-permute-done | bytes 294944 | tf_op jit(solution)/shard_map/ppermute | solution.py:214
  136.4 1.4 %shard_map.73 = f32[384,384]{1,0:T(8,128)} custom-call(s32[1]{0:T(128)} %bitcast.side_ref, bf16[2,8,4,2,16,384]{5,4,3,2,1,0:T(8,128)(2,1)S(1)} %bitcast.27, bf16[8,2,4,16,384]{4,3,2,1,0:T(8,128)(2,1)S(1)} %bitcast.23, bf16[384,384]{1,0:T(8,128)(2,1)S(1)} %collective-permute-done.5.far_ref), custom_call_target="tpu_custom_call" | custom-call | flops 301989888 | bytes 1572864 | tf_op jit(solution)/shard_map/pallas_call | solution.py:20
  137.8 0.7 shard_map.71
  (13 shorter events, 0.0 us)
Async XLA Ops:
  4.7 10.6 %copy-start = (bf16[2048,384]{1,0:T(8,128)(2,1)S(1)}, bf16[2048,384]{1,0:T(8,128)(2,1)}, u32[]{:S(2)}) copy-start(bf16[2048,384]{1,0:T(8,128)(2,1)} %param.4) | copy-start | bytes 4718596
  4.7 48.6 %all-to-all-start = ((bf16[16,128,384]{2,1,0:T(8,128)(2,1)}), bf16[16,128,384]{2,1,0:T(8,128)(2,1)S(1)}, u32[]{:S(2)}, u32[]{:S(2)}) async-start(bf16[16,128,384]{2,1,0:T(8,128)(2,1)} %bitcast.33), calls=%async_computation | async-start | bytes 3145728 | tf_op jit(solution)/shard_map/all_to_all | solution.py:171
  15.3 17.0 %copy-start.2 = (bf16[384,384]{1,0:T(8,128)(2,1)S(1)}, bf16[384,384]{1,0:T(8,128)(2,1)}, u32[]{:S(2)}) copy-start(bf16[384,384]{1,0:T(8,128)(2,1)} %get-tuple-element.13.w_ref) | copy-start | bytes 884740
  15.3 18.9 %copy-start.3 = (bf16[128,384]{1,0:T(8,128)(2,1)S(1)}, bf16[128,384]{1,0:T(8,128)(2,1)}, u32[]{:S(2)}) copy-start(bf16[128,384]{1,0:T(8,128)(2,1)} %param.7) | copy-start | bytes 294916
  16.3 33.5 %collective-permute-start.2 = (bf16[2,8,4,16,384]{4,3,2,1,0:T(8,128)(2,1)}, bf16[2,8,4,16,384]{4,3,2,1,0:T(8,128)(2,1)}, u32[]{:S(2)}, u32[]{:S(2)}) collective-permute-start(bf16[2,8,4,16,384]{4,3,2,1,0:T(8,128)(2,1)} %dynamic-slice_bitcast_fusion), channel_id=1, source_target_pairs={{0,776},{1,777},{2,778},{3,779},{4,780},{5,781},{6,782},{7,783},{8... | collective-permute-start | bytes 2359304 | tf_op jit(solution)/shard_map/ppermute | solution.py:184
  32.3 17.6 %collective-permute-start.1 = (bf16[384,384]{1,0:T(8,128)(2,1)S(1)}, bf16[384,384]{1,0:T(8,128)(2,1)}, u32[]{:S(2)}, u32[]{:S(2)}) collective-permute-start(bf16[384,384]{1,0:T(8,128)(2,1)S(1)} %copy-done.2), channel_id=1, source_target_pairs={{0,8},{1,9},{2,10},{3,11},{4,12},{5,13},{6,14},{7,15},{8,0},{9,1},... | collective-permute-start | bytes 884744 | tf_op jit(solution)/shard_map/ppermute | solution.py:177
  34.8 15.0 %collective-permute-start = (bf16[4,16,384]{2,1,0:T(8,128)(2,1)}, bf16[4,16,384]{2,1,0:T(8,128)(2,1)}, u32[]{:S(2)}, u32[]{:S(2)}) collective-permute-start(bf16[4,16,384]{2,1,0:T(8,128)(2,1)} %dynamic-slice_bitcast_fusion.1), channel_id=1, source_target_pairs={{0,8},{1,9},{2,10},{3,11},{4,12},{5,13},{6,14},{7,15},{8,0},{9,1},... | collective-permute-start | bytes 147464 | tf_op jit(solution)/shard_map/ppermute | solution.py:174
  54.5 33.8 %copy-start.4 = (bf16[64,384]{1,0:T(8,128)(2,1)}, bf16[64,384]{1,0:T(8,128)(2,1)S(1)}, u32[]{:S(2)}) copy-start(bf16[64,384]{1,0:T(8,128)(2,1)S(1)} %get-tuple-element.16) | copy-start | bytes 147460
  54.5 33.7 %copy-start.6 = (bf16[64,384]{1,0:T(8,128)(2,1)}, bf16[64,384]{1,0:T(8,128)(2,1)S(1)}, u32[]{:S(2)}) copy-start(bf16[64,384]{1,0:T(8,128)(2,1)S(1)} %get-tuple-element.17) | copy-start | bytes 147460
  82.5 4.2 %collective-permute-start.4 = (bf16[2,512,384]{2,1,0:T(8,128)(2,1)S(1)}, bf16[2,512,384]{2,1,0:T(8,128)(2,1)S(1)}, u32[]{:S(2)}, u32[]{:S(2)}) collective-permute-start(bf16[2,512,384]{2,1,0:T(8,128)(2,1)S(1)} %shard_map.69), channel_id=1, source_target_pairs={{0,16},{16,0},{32,48},{48,32},{64,80},{80,64},{96,112},{112,96},{1... | collective-permute-start | bytes 2359304 | tf_op jit(solution)/shard_map/ppermute | solution.py:210
  88.3 0.9 copy-start.1
  89.2 20.8 %copy-start.7 = (bf16[64,384]{1,0:T(8,128)(2,1)S(1)}, bf16[64,384]{1,0:T(8,128)(2,1)}, u32[]{:S(2)}) copy-start(bf16[64,384]{1,0:T(8,128)(2,1)} %copy-done.6) | copy-start | bytes 147460
  89.2 40.8 %copy-start.5 = (bf16[64,384]{1,0:T(8,128)(2,1)S(1)}, bf16[64,384]{1,0:T(8,128)(2,1)}, u32[]{:S(2)}) copy-start(bf16[64,384]{1,0:T(8,128)(2,1)} %copy-done.4) | copy-start | bytes 147460
  89.2 48.7 %all-to-all-start.1 = ((bf16[64,16,384]{2,1,0:T(8,128)(2,1)}), bf16[64,16,384]{2,1,0:T(8,128)(2,1)S(1)}, u32[]{:S(2)}, u32[]{:S(2)}) async-start(bf16[64,16,384]{2,1,0:T(8,128)(2,1)} %bitcast.29), calls=%async_computation.1 | async-start | bytes 1572864 | tf_op jit(solution)/shard_map/all_to_all | solution.py:233
  110.0 19.9 %collective-permute-start.3 = (bf16[64,384]{1,0:T(8,128)(2,1)S(1)}, bf16[64,384]{1,0:T(8,128)(2,1)}, u32[]{:S(2)}, u32[]{:S(2)}) collective-permute-start(bf16[64,384]{1,0:T(8,128)(2,1)S(1)} %copy-done.7), channel_id=1, source_target_pairs={{0,8},{1,9},{2,10},{3,11},{4,12},{5,13},{6,14},{7,15},{8,0},{9,1},... | collective-permute-start | bytes 147464 | tf_op jit(solution)/shard_map/ppermute | solution.py:247
  115.3 21.1 %collective-permute-start.5 = (bf16[384,384]{1,0:T(8,128)(2,1)S(1)}, bf16[384,384]{1,0:T(8,128)(2,1)S(1)}, u32[]{:S(2)}, u32[]{:S(2)}) collective-permute-start(bf16[384,384]{1,0:T(8,128)(2,1)S(1)} %shard_map.72), channel_id=1, source_target_pairs={{0,8},{1,9},{2,10},{3,11},{4,12},{5,13},{6,14},{7,15},{8,0},{9,1},... | collective-permute-start | bytes 884744 | tf_op jit(solution)/shard_map/ppermute | solution.py:214

commit v4 on v3

--- a/solution.py
+++ b/solution.py
@@ -219,6 +219,7 @@
         flops // 2, size,
         core, side, by_core, weight, far_weight, other,
     )
+    both, act_far = lax.optimization_barrier((both, act_far))
     groups = [
         [
             (per * (ys * t + y) + 2 * h + c) * locals_ + z * ys + own
@@ -238,7 +239,7 @@
         functools.partial(weigh_own, rows ** (-0.5)),
         [((feat, units), F32)],
         [SMEM, VMEM, VMEM, VMEM],
-        flops // 2, size,
+        20 * flops, size,
         side, tok, by_side, far_part,
     )
     (input_grad,) = call(

time: 141 us -> 135 us (0.957)
  the two profiles are of different devices: /device:TPU:14 before, /device:TPU:4 now
where the time goes in v4:
time: 135 us
  starting transfers between devices  61.5 us (46%)
  waiting for transfers between devices  33.7 us (25%)
  blocking collectives  26.3 us (19%)
  Pallas kernels  9.39 us (7%)
  local copies, waits for them, and re-layouts  3.08 us (2%)
    all_gather x1, blocking collectives, shards(): lax.all_gather(slope.reshape(2 * mine, units), 'local', axis=0, tiled=Tru...  26.3 us
    all_to_all x1, starting transfers between devices, shards(): lax.all_to_all(both.reshape(nodes, sub, feat), ('node', 'local'), 0, 0, a...  20.6 us
    ppermute x1, starting transfers between devices, shards(): lax.ppermute(lax.dynamic_index_in_dim(tok, 1 - side[0], 3, False), ('node...  15.9 us
    ppermute x1, waiting for transfers between devices, shards(): lax.ppermute(lax.dynamic_index_in_dim(cot, 1 - side[0], 1, False), 'local...  11.6 us
    all_to_all x1, starting transfers between devices, shards(): lax.all_to_all(partial.reshape(locals_, 2 * mine, units), 'local', 0, 0,...  10.5 us
    ppermute x1, waiting for transfers between devices, shards(): act_far = lax.ppermute(act_far, 'local', pair)  9.8 us
    all_to_all x1, waiting for transfers between devices, shards(): lax.all_to_all(both.reshape(nodes, sub, feat), ('node', 'local'), 0, 0, a...  8.75 us
    pallas_call x6, Pallas kernels, call(): pl.pallas_call(kernel, out_shape=[jax.ShapeDtypeStruct(s, d) for s, d in...  5.32 us
  transfers between devices with their start and end apart: 8, of which 4 were waited for; matrix products, arithmetic and copies ran while one was open for 1% of the time, Pallas kernels for 3%

profile of v4, /device:TPU:4, one launch (start us, length us, event | category | flops | bytes accessed | tf_op | source)
XLA Modules:
  0.0 134.9 jit_solution(2669534900315112259)
XLA Ops:
  0.6 4.1 %shard_map.67 = (bf16[384,384]{1,0:T(8,128)(2,1)}, bf16[2,8,2,4,16,384]{5,4,3,2,1,0:T(8,128)(2,1)}) custom-call(s32[1]{0:T(128)} %bitcast.1.start_ref, bf16[2,8,4,2,16,384]{5,4,3,2,1,0:T(8,128)(2,1)} %bitcast.26, bf16[384,384]{1,0:T(8,128)(2,1)} %codes_hbm.1, f32[3,384]{1,0:T(4,128)} %scales_hbm.1), custom_call_target="tpu_custom_call" | custom-call | flops 603979776 | bytes 3145728 | tf_op jit(solution)/shard_map/pallas_call | solution.py:154
  4.7 0.0 copy-start.1
  4.7 10.5 %all-to-all-start = ((bf16[16,128,384]{2,1,0:T(8,128)(2,1)}), bf16[16,128,384]{2,1,0:T(8,128)(2,1)S(1)}, u32[]{:S(2)}, u32[]{:S(2)}) async-start(bf16[16,128,384]{2,1,0:T(8,128)(2,1)} %bitcast.32), calls=%async_computation | async-start | bytes 3145728 | tf_op jit(solution)/shard_map/all_to_all | solution.py:171
  15.3 0.0 copy-start
  15.3 0.0 copy-start.3
  15.3 0.0 copy-done.1
  15.3 1.0 dynamic-slice_bitcast_fusion
  16.3 15.9 %collective-permute-start.2 = (bf16[2,8,4,16,384]{4,3,2,1,0:T(8,128)(2,1)}, bf16[2,8,4,16,384]{4,3,2,1,0:T(8,128)(2,1)S(1)}, u32[]{:S(2)}, u32[]{:S(2)}) collective-permute-start(bf16[2,8,4,16,384]{4,3,2,1,0:T(8,128)(2,1)} %dynamic-slice_bitcast_fusion), channel_id=1, source_target_pairs={{0,776},{1,777},{2,778},{3,779},{4,780},{5,781},{6,782},{7,783},{8... | collective-permute-start | bytes 2359304 | tf_op jit(solution)/shard_map/ppermute | solution.py:184
  32.3 1.9 %collective-permute-start.1 = (bf16[384,384]{1,0:T(8,128)(2,1)S(1)}, bf16[384,384]{1,0:T(8,128)(2,1)S(1)}, u32[]{:S(2)}, u32[]{:S(2)}) collective-permute-start(bf16[384,384]{1,0:T(8,128)(2,1)S(1)} %copy-done), channel_id=1, source_target_pairs={{0,8},{1,9},{2,10},{3,11},{4,12},{5,13},{6,14},{7,15},{8,0},{9,1},... | collective-permute-start | bytes 884744 | tf_op jit(solution)/shard_map/ppermute | solution.py:177
  34.2 3.9 %collective-permute-start = (bf16[4,16,384]{2,1,0:T(8,128)(2,1)S(1)}, bf16[4,16,384]{2,1,0:T(8,128)(2,1)S(1)}, u32[]{:S(2)}, u32[]{:S(2)}) collective-permute-start(bf16[4,16,384]{2,1,0:T(8,128)(2,1)S(1)} %dynamic-slice_bitcast_fusion.1), channel_id=1, source_target_pairs={{0,8},{1,9},{2,10},{3,11},{4,12},{5,13},{6,14},{7,15},{8,0},{9,1},... | collective-permute-start | bytes 147464 | tf_op jit(solution)/shard_map/ppermute | solution.py:174
  38.2 11.6 %collective-permute-done.far_cot_ref = bf16[4,16,384]{2,1,0:T(8,128)(2,1)S(1)} collective-permute-done((bf16[4,16,384]{2,1,0:T(8,128)(2,1)S(1)}, bf16[4,16,384]{2,1,0:T(8,128)(2,1)S(1)}, u32[]{:S(2)}, u32[]{:S(2)}) %collective-permute-start) | collective-permute-done | bytes 49184 | tf_op jit(solution)/shard_map/ppermute | solution.py:174
  49.7 0.0 collective-permute-done.1.far_w_ref
  49.8 0.0 collective-permute-done.2.far_tok_ref
  49.8 3.6 %all-to-all-done = bf16[16,128,384]{2,1,0:T(8,128)(2,1)S(1)} async-done(((bf16[16,128,384]{2,1,0:T(8,128)(2,1)}), bf16[16,128,384]{2,1,0:T(8,128)(2,1)S(1)}, u32[]{:S(2)}, u32[]{:S(2)}) %all-to-all-start) | async-done | bytes 1572896 | tf_op jit(solution)/shard_map/all_to_all | solution.py:171
  53.3 0.4 shard_map.68
  53.7 26.3 %all_gather.3 = bf16[1024,384]{1,0:T(8,128)(2,1)S(1)} all-gather(bf16[128,384]{1,0:T(8,128)(2,1)S(1)} %bitcast.31), channel_id=1, replica_groups={{0,1,2,3,4,5,6,7},{8,9,10,11,12,13,14,15},{16,17,18,19,20,21,22,23},{24..., dimensions={0}, use_global_device_ids=true | all-gather | bytes 884736 | tf_op jit(solution)/shard_map/all_gather | solution.py:198
  80.0 0.7 shard_map.69
  80.6 1.9 %collective-permute-start.3 = (bf16[2,512,384]{2,1,0:T(8,128)(2,1)S(1)}, bf16[2,512,384]{2,1,0:T(8,128)(2,1)S(1)}, u32[]{:S(2)}, u32[]{:S(2)}) collective-permute-start(bf16[2,512,384]{2,1,0:T(8,128)(2,1)S(1)} %shard_map.69), channel_id=1, source_target_pairs={{0,16},{16,0},{32,48},{48,32},{64,80},{80,64},{96,112},{112,96},{1... | collective-permute-start | bytes 2359304 | tf_op jit(solution)/shard_map/ppermute | solution.py:210
  82.6 0.6 shard_map.72
  83.2 3.1 %collective-permute-start.5 = (bf16[384,384]{1,0:T(8,128)(2,1)S(1)}, bf16[384,384]{1,0:T(8,128)(2,1)S(1)}, u32[]{:S(2)}, u32[]{:S(2)}) collective-permute-start(bf16[384,384]{1,0:T(8,128)(2,1)S(1)} %shard_map.72), channel_id=1, source_target_pairs={{0,8},{1,9},{2,10},{3,11},{4,12},{5,13},{6,14},{7,15},{8,0},{9,1},... | collective-permute-start | bytes 884744 | tf_op jit(solution)/shard_map/ppermute | solution.py:214
  86.3 0.0 collective-permute-done.3.other_ref
  86.3 1.6 %shard_map.70 = bf16[2,8,2,2,16,384]{5,4,3,2,1,0:T(8,128)(2,1)} custom-call(s32[1]{0:T(128)} %bitcast.8.core_ref, s32[1]{0:T(128)} %bitcast.side_ref, bf16[8,2,2,2,16,384]{5,4,3,2,1,0:T(8,128)(2,1)S(1)} %bitcast.22, bf16[384,384]{1,0:T(8,128)(2,1)S(1)} %copy-done, bf16[384,384]{1,0:T(8,128)(2,1)S(1)} %collective-permute-done.1.far_w_ref, ...), custom_call_target="tpu_custom_call" | custom-call | flops 301989888 | bytes 1572864 | tf_op jit(solution)/shard_map/pallas_call | solution.py:20
  87.9 20.6 %all-to-all-start.1 = ((bf16[64,16,384]{2,1,0:T(8,128)(2,1)}), bf16[64,16,384]{2,1,0:T(8,128)(2,1)S(1)}, u32[]{:S(2)}, u32[]{:S(2)}) async-start(bf16[64,16,384]{2,1,0:T(8,128)(2,1)} %bitcast.14), calls=%async_computation.1 | async-start | bytes 1572864 | tf_op jit(solution)/shard_map/all_to_all | solution.py:234
  108.5 3.5 %collective-permute-start.4 = (bf16[64,384]{1,0:T(8,128)(2,1)S(1)}, bf16[64,384]{1,0:T(8,128)(2,1)S(1)}, u32[]{:S(2)}, u32[]{:S(2)}) collective-permute-start(bf16[64,384]{1,0:T(8,128)(2,1)S(1)} %get-tuple-element.22), channel_id=1, source_target_pairs={{0,8},{1,9},{2,10},{3,11},{4,12},{5,13},{6,14},{7,15},{8,0},{9,1},... | collective-permute-start | bytes 147464 | tf_op jit(solution)/shard_map/ppermute | solution.py:248
  112.0 0.0 collective-permute-done.5.far_ref
  112.1 0.0 copy-start.2
  112.1 1.4 %copy-done.2 = bf16[2048,384]{1,0:T(8,128)(2,1)S(1)} copy-done((bf16[2048,384]{1,0:T(8,128)(2,1)S(1)}, bf16[2048,384]{1,0:T(8,128)(2,1)}, u32[]{:S(2)}) %copy-start.2) | copy-done | bytes 1572888
  113.5 1.4 %shard_map.73 = f32[384,384]{1,0:T(8,128)} custom-call(s32[1]{0:T(128)} %bitcast.side_ref, bf16[2,8,4,2,16,384]{5,4,3,2,1,0:T(8,128)(2,1)S(1)} %bitcast.28, bf16[8,2,4,16,384]{4,3,2,1,0:T(8,128)(2,1)S(1)} %bitcast.23, bf16[384,384]{1,0:T(8,128)(2,1)S(1)} %collective-permute-done.5.far_ref), custom_call_target="tpu_custom_call" | custom-call | flops 12079595520 | bytes 1572864 | tf_op jit(solution)/shard_map/pallas_call | solution.py:20
  114.9 9.8 %collective-permute-done.4 = bf16[64,384]{1,0:T(8,128)(2,1)S(1)} collective-permute-done((bf16[64,384]{1,0:T(8,128)(2,1)S(1)}, bf16[64,384]{1,0:T(8,128)(2,1)S(1)}, u32[]{:S(2)}, u32[]{:S(2)}) %collective-permute-start.4) | collective-permute-done | bytes 49184 | tf_op jit(solution)/shard_map/ppermute | solution.py:248
  124.7 0.7 copy.7
  125.4 8.7 %all-to-all-done.1 = bf16[64,16,384]{2,1,0:T(8,128)(2,1)S(1)} async-done(((bf16[64,16,384]{2,1,0:T(8,128)(2,1)}), bf16[64,16,384]{2,1,0:T(8,128)(2,1)S(1)}, u32[]{:S(2)}, u32[]{:S(2)}) %all-to-all-start.1) | async-done | bytes 786464 | tf_op jit(solution)/shard_map/all_to_all | solution.py:234
  134.1 0.7 shard_map.71
  (5 shorter events, 0.1 us)
Async XLA Ops:
  4.7 10.6 %copy-start.1 = (bf16[2048,384]{1,0:T(8,128)(2,1)S(1)}, bf16[2048,384]{1,0:T(8,128)(2,1)}, u32[]{:S(2)}) copy-start(bf16[2048,384]{1,0:T(8,128)(2,1)} %param.4) | copy-start | bytes 4718596
  4.7 48.6 %all-to-all-start = ((bf16[16,128,384]{2,1,0:T(8,128)(2,1)}), bf16[16,128,384]{2,1,0:T(8,128)(2,1)S(1)}, u32[]{:S(2)}, u32[]{:S(2)}) async-start(bf16[16,128,384]{2,1,0:T(8,128)(2,1)} %bitcast.32), calls=%async_computation | async-start | bytes 3145728 | tf_op jit(solution)/shard_map/all_to_all | solution.py:171
  15.3 17.0 %copy-start = (bf16[384,384]{1,0:T(8,128)(2,1)S(1)}, bf16[384,384]{1,0:T(8,128)(2,1)}, u32[]{:S(2)}) copy-start(bf16[384,384]{1,0:T(8,128)(2,1)} %get-tuple-element.15.w_ref) | copy-start | bytes 884740
  15.3 18.9 %copy-start.3 = (bf16[128,384]{1,0:T(8,128)(2,1)S(1)}, bf16[128,384]{1,0:T(8,128)(2,1)}, u32[]{:S(2)}) copy-start(bf16[128,384]{1,0:T(8,128)(2,1)} %param.7) | copy-start | bytes 294916
  16.3 33.4 %collective-permute-start.2 = (bf16[2,8,4,16,384]{4,3,2,1,0:T(8,128)(2,1)}, bf16[2,8,4,16,384]{4,3,2,1,0:T(8,128)(2,1)S(1)}, u32[]{:S(2)}, u32[]{:S(2)}) collective-permute-start(bf16[2,8,4,16,384]{4,3,2,1,0:T(8,128)(2,1)} %dynamic-slice_bitcast_fusion), channel_id=1, source_target_pairs={{0,776},{1,777},{2,778},{3,779},{4,780},{5,781},{6,782},{7,783},{8... | collective-permute-start | bytes 2359304 | tf_op jit(solution)/shard_map/ppermute | solution.py:184
  32.3 17.5 %collective-permute-start.1 = (bf16[384,384]{1,0:T(8,128)(2,1)S(1)}, bf16[384,384]{1,0:T(8,128)(2,1)S(1)}, u32[]{:S(2)}, u32[]{:S(2)}) collective-permute-start(bf16[384,384]{1,0:T(8,128)(2,1)S(1)} %copy-done), channel_id=1, source_target_pairs={{0,8},{1,9},{2,10},{3,11},{4,12},{5,13},{6,14},{7,15},{8,0},{9,1},... | collective-permute-start | bytes 884744 | tf_op jit(solution)/shard_map/ppermute | solution.py:177
  34.2 15.5 %collective-permute-start = (bf16[4,16,384]{2,1,0:T(8,128)(2,1)S(1)}, bf16[4,16,384]{2,1,0:T(8,128)(2,1)S(1)}, u32[]{:S(2)}, u32[]{:S(2)}) collective-permute-start(bf16[4,16,384]{2,1,0:T(8,128)(2,1)S(1)} %dynamic-slice_bitcast_fusion.1), channel_id=1, source_target_pairs={{0,8},{1,9},{2,10},{3,11},{4,12},{5,13},{6,14},{7,15},{8,0},{9,1},... | collective-permute-start | bytes 147464 | tf_op jit(solution)/shard_map/ppermute | solution.py:174
  80.6 5.7 %collective-permute-start.3 = (bf16[2,512,384]{2,1,0:T(8,128)(2,1)S(1)}, bf16[2,512,384]{2,1,0:T(8,128)(2,1)S(1)}, u32[]{:S(2)}, u32[]{:S(2)}) collective-permute-start(bf16[2,512,384]{2,1,0:T(8,128)(2,1)S(1)} %shard_map.69), channel_id=1, source_target_pairs={{0,16},{16,0},{32,48},{48,32},{64,80},{80,64},{96,112},{112,96},{1... | collective-permute-start | bytes 2359304 | tf_op jit(solution)/shard_map/ppermute | solution.py:210
  83.2 28.9 %collective-permute-start.5 = (bf16[384,384]{1,0:T(8,128)(2,1)S(1)}, bf16[384,384]{1,0:T(8,128)(2,1)S(1)}, u32[]{:S(2)}, u32[]{:S(2)}) collective-permute-start(bf16[384,384]{1,0:T(8,128)(2,1)S(1)} %shard_map.72), channel_id=1, source_target_pairs={{0,8},{1,9},{2,10},{3,11},{4,12},{5,13},{6,14},{7,15},{8,0},{9,1},... | collective-permute-start | bytes 884744 | tf_op jit(solution)/shard_map/ppermute | solution.py:214
  87.9 46.3 %all-to-all-start.1 = ((bf16[64,16,384]{2,1,0:T(8,128)(2,1)}), bf16[64,16,384]{2,1,0:T(8,128)(2,1)S(1)}, u32[]{:S(2)}, u32[]{:S(2)}) async-start(bf16[64,16,384]{2,1,0:T(8,128)(2,1)} %bitcast.14), calls=%async_computation.1 | async-start | bytes 1572864 | tf_op jit(solution)/shard_map/all_to_all | solution.py:234
  108.5 16.2 %collective-permute-start.4 = (bf16[64,384]{1,0:T(8,128)(2,1)S(1)}, bf16[64,384]{1,0:T(8,128)(2,1)S(1)}, u32[]{:S(2)}, u32[]{:S(2)}) collective-permute-start(bf16[64,384]{1,0:T(8,128)(2,1)S(1)} %get-tuple-element.22), channel_id=1, source_target_pairs={{0,8},{1,9},{2,10},{3,11},{4,12},{5,13},{6,14},{7,15},{8,0},{9,1},... | collective-permute-start | bytes 147464 | tf_op jit(solution)/shard_map/ppermute | solution.py:248
  112.1 1.4 %copy-start.2 = (bf16[2048,384]{1,0:T(8,128)(2,1)S(1)}, bf16[2048,384]{1,0:T(8,128)(2,1)}, u32[]{:S(2)}) copy-start(bf16[2048,384]{1,0:T(8,128)(2,1)} %param.4) | copy-start | bytes 4718596

commit v5 on v4

--- a/solution.py
+++ b/solution.py
@@ -16,13 +16,13 @@
 SMEM = pl.BlockSpec(memory_space=pltpu.SMEM)
 
 
-def call(kernel, outs, specs, flops, size, *args):
+def call(kernel, outs, specs, flops, size, *args, room=40):
     return pl.pallas_call(
         kernel,
         out_shape=[jax.ShapeDtypeStruct(s, d) for s, d in outs],
         in_specs=specs,
         out_specs=[VMEM] * len(outs),
-        compiler_params=pltpu.CompilerParams(vmem_limit_bytes=40 * 2**20),
+        compiler_params=pltpu.CompilerParams(vmem_limit_bytes=room * 2**20),
         cost_estimate=pl.CostEstimate(flops=flops, bytes_accessed=size, transcendentals=0),
     )(*args)
 
@@ -30,40 +30,49 @@
 HBM = pl.BlockSpec(memory_space=pltpu.HBM)
 
 
-def project(start_ref, tok_hbm, codes_hbm, scales_hbm, w_ref, out_ref, tok_ref, codes_ref, scales_ref, sems):
-    feat, units = codes_ref.shape
-    cuts = [(z, y) for z in range(2) for y in (0, 1)]
-    span = tok_ref.shape[1] // 2
+def dequant(start_ref, codes, scales_ref):
+    row = start_ref[0] + lax.broadcasted_iota(jnp.int32, codes.shape, 0)
+    scale = jnp.broadcast_to(scales_ref[0:1, :], codes.shape)
+    for i in range(1, scales_ref.shape[0]):
+        scale = jnp.where(row >= i * BLOCK, scales_ref[i : i + 1, :], scale)
+    return (codes.astype(F32) * scale).astype(BF16)
+
+
+def project_own(start_ref, side_ref, tok_hbm, codes_hbm, scales_hbm, w_ref, out_ref, tok_ref, codes_ref, scales_ref, sems):
+    side = side_ref[0]
     first = [
         pltpu.make_async_copy(codes_hbm, codes_ref, sems.at[0]),
         pltpu.make_async_copy(scales_hbm, scales_ref, sems.at[1]),
     ]
     loads = [
-        pltpu.make_async_copy(
-            tok_hbm.at[z, pl.ds(y * span, span)],
-            tok_ref.at[z, pl.ds(y * span, span)],
-            sems.at[2 + i],
-        )
-        for i, (z, y) in enumerate(cuts)
+        pltpu.make_async_copy(tok_hbm.at[z, :, :, side], tok_ref.at[z], sems.at[2 + z])
+        for z in range(2)
     ]
     for copy in first + loads:
         copy.start()
     for copy in first:
         copy.wait()
-    row = start_ref[0] + lax.broadcasted_iota(jnp.int32, (feat, units), 0)
-    scale = jnp.broadcast_to(scales_ref[0:1, :], (feat, units))
-    for i in range(1, scales_ref.shape[0]):
-        scale = jnp.where(row >= i * BLOCK, scales_ref[i : i + 1, :], scale)
-    weight = (codes_ref[...].astype(F32) * scale).astype(BF16)
+    weight = dequant(start_ref, codes_ref[...], scales_ref)
     w_ref[...] = weight
-    for (z, y), copy in zip(cuts, loads):
+    for z, copy in enumerate(loads):
         copy.wait()
-        ys = slice(y * span, (y + 1) * span)
-        piece = tok_ref[z, ys]
-        res = jnp.dot(piece.reshape(-1, feat), weight, preferred_element_type=F32)
-        res = res.astype(BF16).reshape(piece.shape[:-1] + (units,))
-        for h in range(2):
-            out_ref[h, ys, z] = res[:, :, h]
+        rows = tok_ref[z].reshape(-1, tok_ref.shape[-1])
+        res = jnp.dot(rows, weight, preferred_element_type=F32)
+        out_ref[z] = res.reshape(out_ref.shape[1:])
+
+
+def project_far(start_ref, codes_ref, scales_ref, tok_a_ref, tok_b_ref, own_ref, w_ref, out_ref):
+    weight = dequant(start_ref, codes_ref[...], scales_ref)
+    w_ref[...] = weight
+    for z in range(2):
+        low = 0
+        for tok in (tok_a_ref, tok_b_ref):
+            high = low + tok.shape[1]
+            rows = tok[z].reshape(-1, tok.shape[-1])
+            res = jnp.dot(rows, weight, preferred_element_type=F32)
+            both = res.reshape((high - low,) + out_ref.shape[2:]) + own_ref[z, low:high]
+            out_ref[low:high, z] = both.astype(BF16)
+            low = high
 
 
 def activate(side_ref, got_ref, cot_ref, far_cot_ref, act_ref, far_act_ref, slope_ref):
@@ -122,8 +131,15 @@
     )
 
 
-def weigh_far(far_tok_ref, slope_ref, out_ref):
-    total = sum(outer(far_tok_ref[z], slope_ref[:, z]) for z in range(2))
+def weigh_far(tok_a_ref, tok_b_ref, slope_ref, out_ref):
+    total = None
+    for z in range(2):
+        low = 0
+        for tok in (tok_a_ref, tok_b_ref):
+            high = low + tok.shape[1]
+            part = outer(tok[z], slope_ref[low:high, z])
+            total = part if total is None else total + part
+            low = high
     out_ref[...] = total.astype(BF16)
 
 
@@ -151,41 +167,48 @@
     flops = 2 * rows * feat * units
     size = 2 * rows * feat
 
-    weight, partial = pl.pallas_call(
-        project,
-        out_shape=[
-            jax.ShapeDtypeStruct((feat, units), BF16),
-            jax.ShapeDtypeStruct((2, ys, 2, per, sub, units), BF16),
-        ],
-        in_specs=[SMEM, HBM, HBM, HBM],
-        out_specs=[VMEM, VMEM],
-        scratch_shapes=[
-            pltpu.VMEM(tok.shape, BF16),
-            pltpu.VMEM(codes.shape, BF16),
-            pltpu.VMEM(scales.shape, F32),
-            pltpu.SemaphoreType.DMA((6,)),
-        ],
-        compiler_params=pltpu.CompilerParams(vmem_limit_bytes=58 * 2**20),
-        cost_estimate=pl.CostEstimate(flops=flops, bytes_accessed=2 * size, transcendentals=0),
-    )(start, tok, codes, scales)
-    got = lax.all_to_all(
-        partial.reshape(locals_, 2 * mine, units), "local", 0, 0, tiled=True
-    ).reshape(locals_, 2, mine, units)
-    far_cot = lax.ppermute(
-        lax.dynamic_index_in_dim(cot, 1 - side[0], 1, False), "local", pair
-    )
-    far_weight = lax.ppermute(weight, "local", pair)
+    far_codes = lax.ppermute(codes, "local", pair)
+    leave = lax.dynamic_index_in_dim(tok, 1 - side[0], 3, False)
+    cut = (3 * ys) // 4
     block = nodes // 4
     step = [
         (n * locals_ + l, (n + (block if l >= ys else -block)) % nodes * locals_ + (l + ys) % locals_)
         for n in range(nodes)
         for l in range(locals_)
     ]
-    far_tok = lax.ppermute(
-        lax.dynamic_index_in_dim(tok, 1 - side[0], 3, False), ("node", "local"), step
-    )
-    got, far_cot, far_weight, far_tok = lax.optimization_barrier(
-        (got, far_cot, far_weight, far_tok)
+    far_tok_a = lax.ppermute(leave[:, :cut], ("node", "local"), step)
+    far_tok_b = lax.ppermute(leave[:, cut:], "local", pair)
+    far_start = ((local + ys) % locals_ * feat).reshape(1)
+    weight, own = pl.pallas_call(
+        project_own,
+        out_shape=[
+            jax.ShapeDtypeStruct((feat, units), BF16),
+            jax.ShapeDtypeStruct((2, ys, mine, units), F32),
+        ],
+        in_specs=[SMEM, SMEM, HBM, HBM, HBM],
+        out_specs=[VMEM, VMEM],
+        scratch_shapes=[
+            pltpu.VMEM((2, ys, per, sub, feat), BF16),
+            pltpu.VMEM(codes.shape, BF16),
+            pltpu.VMEM(scales.shape, F32),
+            pltpu.SemaphoreType.DMA((4,)),
+        ],
+        compiler_params=pltpu.CompilerParams(vmem_limit_bytes=40 * 2**20),
+        cost_estimate=pl.CostEstimate(flops=flops // 2, bytes_accessed=size, transcendentals=0),
+    )(start, side, tok, codes, scales)
+    far_weight, partial = call(
+        project_far,
+        [((feat, units), BF16), ((ys, 2, mine, units), BF16)],
+        [SMEM] + [VMEM] * 5,
+        flops // 2, size,
+        far_start, far_codes, scales, far_tok_a, far_tok_b, own, room=40,
+    )
+    lines = [list(range(z * ys, (z + 1) * ys)) for z in range(2)]
+    got = lax.all_to_all(
+        partial.reshape(ys, 2 * mine, units), "local", 0, 0, axis_index_groups=lines, tiled=True
+    ).reshape(ys, 2, mine, units)
+    far_cot = lax.ppermute(
+        lax.dynamic_index_in_dim(cot, 1 - side[0], 1, False), "local", pair
     )
     act_own, act_far, slope = call(
         activate,
@@ -194,7 +217,6 @@
         rows * units * 4, size,
         side, got, cot, far_cot,
     )
-    lines = [list(range(z * ys, (z + 1) * ys)) for z in range(2)]
     spread = lax.all_gather(
         slope.reshape(2 * mine, units), "local", axis=0, tiled=True, axis_index_groups=lines
     )
@@ -209,7 +231,8 @@
     )
     other = lax.ppermute(other, "node", [(i, i ^ 1) for i in range(nodes)])
     (far_part,) = call(
-        weigh_far, [((feat, units), BF16)], [VMEM, VMEM], flops // 2, size, far_tok, by_side
+        weigh_far, [((feat, units), BF16)], [VMEM] * 3, flops // 2, size,
+        far_tok_a, far_tok_b, by_side,
     )
     far_part = lax.ppermute(far_part, "local", pair)
     (both,) = call(
@@ -217,7 +240,7 @@
         [((2, ys, 2, per // 2, sub, feat), BF16)],
         [SMEM, SMEM, VMEM, VMEM, VMEM, VMEM],
         flops // 2, size,
-        core, side, by_core, weight, far_weight, other,
+        core, side, by_core, weight, far_weight, other, room=40,
     )
     both, act_far = lax.optimization_barrier((both, act_far))
     groups = [

time: 135 us -> 140 us (1.037)
  waiting for transfers between devices: 33.7 us -> 44.6 us
  starting transfers between devices: 61.5 us -> 51.2 us
  local copies, waits for them, and re-layouts: 3.08 us -> 7.6 us
    all_to_all x1, waiting for transfers between devices: 3.58 us -> 14.2 us  [shards(): lax.all_to_all(partial.reshape(ys, 2 * mine, units), 'local', 0, 0, axis_...]
    all_to_all x1, starting transfers between devices: 20.6 us -> 10.2 us  [shards(): lax.all_to_all(both.reshape(nodes, sub, feat), ('node', 'local'), 0, 0, a...]
    ppermute x1, waiting for transfers between devices: 11.6 us -> 4.08 us  [shards(): lax.ppermute(lax.dynamic_index_in_dim(cot, 1 - side[0], 1, False), 'local...]
    ppermute x2 -> x3, waiting for transfers between devices: 0.01 us -> 7.49 us  [the longest x1 7.48 us: shards(): far_tok_b = lax.ppermute(leave[:, cut:], 'local', pair)]
    ppermute x2 -> x3, starting transfers between devices: 17.9 us -> 23.1 us  [the longest x1 17.3 us: shards(): far_tok_a = lax.ppermute(leave[:, :cut], ('node', 'local'), step)]
    all_to_all x1, starting transfers between devices: 10.5 us -> 7.55 us  [shards(): lax.all_to_all(partial.reshape(ys, 2 * mine, units), 'local', 0, 0, axis_...]
    pallas_call x1, Pallas kernels: 4.08 us -> 1.16 us  [shards(): pl.pallas_call(project_own, out_shape=[jax.ShapeDtypeStruct((feat, units)...]
    pallas_call x6 -> x7, Pallas kernels: 5.32 us -> 7.59 us  [call(): pl.pallas_call(kernel, out_shape=[jax.ShapeDtypeStruct(s, d) for s, d in...]
  transfers between devices with their start and end apart: 8 -> 9, of which waited for: 4 -> 5; matrix products, arithmetic and copies ran while one was open for 1% -> 2% of each run, Pallas kernels for 3% -> 4%
where the time goes in v5:
time: 140 us; the launch traced here: 139 us
  starting transfers between devices  51.2 us (37%)
  waiting for transfers between devices  44.6 us (32%)
  blocking collectives  26.1 us (19%)
  Pallas kernels  8.75 us (6%)
  local copies, waits for them, and re-layouts  7.6 us (5%)
    all_gather x1, blocking collectives, shards(): lax.all_gather(slope.reshape(2 * mine, units), 'local', axis=0, tiled=Tru...  26.1 us
    ppermute x1, starting transfers between devices, shards(): far_tok_a = lax.ppermute(leave[:, :cut], ('node', 'local'), step)  17.3 us
    all_to_all x1, waiting for transfers between devices, shards(): lax.all_to_all(partial.reshape(ys, 2 * mine, units), 'local', 0, 0, axis_...  14.2 us
    ppermute x1, waiting for transfers between devices, shards(): act_far = lax.ppermute(act_far, 'local', pair)  11.9 us
    all_to_all x1, starting transfers between devices, shards(): lax.all_to_all(both.reshape(nodes, sub, feat), ('node', 'local'), 0, 0, a...  10.2 us
    pallas_call x7, Pallas kernels, call(): pl.pallas_call(kernel, out_shape=[jax.ShapeDtypeStruct(s, d) for s, d in...  7.59 us
    all_to_all x1, starting transfers between devices, shards(): lax.all_to_all(partial.reshape(ys, 2 * mine, units), 'local', 0, 0, axis_...  7.55 us
    ppermute x1, waiting for transfers between devices, shards(): far_tok_b = lax.ppermute(leave[:, cut:], 'local', pair)  7.48 us
  transfers between devices with their start and end apart: 9, of which 5 were waited for; matrix products, arithmetic and copies ran while one was open for 2% of the time, Pallas kernels for 4%

profile of v5, /device:TPU:4, one launch (start us, length us, event | category | flops | bytes accessed | tf_op | source)
XLA Modules:
  0.0 139.2 jit_solution(7653637374117329652)
XLA Ops:
  0.7 1.4 dynamic-slice_bitcast_fusion
  2.0 0.9 slice.8
  2.9 17.3 %collective-permute-start.1 = (bf16[2,6,4,16,384]{4,3,2,1,0:T(8,128)(2,1)}, bf16[2,6,4,16,384]{4,3,2,1,0:T(8,128)(2,1)S(1)}, u32[]{:S(2)}, u32[]{:S(2)}) collective-permute-start(bf16[2,6,4,16,384]{4,3,2,1,0:T(8,128)(2,1)} %slice.8), channel_id=1, source_target_pairs={{0,776},{1,777},{2,778},{3,779},{4,780},{5,781},{6,782},{7,783},{8... | collective-permute-start | bytes 1769480 | tf_op jit(solution)/shard_map/ppermute | solution.py:179
  20.2 1.9 %collective-permute-start = (bf16[384,384]{1,0:T(8,128)(2,1)S(1)}, bf16[384,384]{1,0:T(8,128)(2,1)S(1)}, u32[]{:S(2)}, u32[]{:S(2)}) collective-permute-start(bf16[384,384]{1,0:T(8,128)(2,1)S(1)} %copy-done.5), channel_id=1, source_target_pairs={{0,8},{1,9},{2,10},{3,11},{4,12},{5,13},{6,14},{7,15},{8,0},{9,1},... | collective-permute-start | bytes 884744 | tf_op jit(solution)/shard_map/ppermute | solution.py:170
  22.2 3.9 %collective-permute-start.2 = (bf16[2,2,4,16,384]{4,3,2,1,0:T(8,128)(2,1)S(1)}, bf16[2,2,4,16,384]{4,3,2,1,0:T(8,128)(2,1)S(1)}, u32[]{:S(2)}, u32[]{:S(2)}) collective-permute-start(bf16[2,2,4,16,384]{4,3,2,1,0:T(8,128)(2,1)S(1)} %slice.9), channel_id=1, source_target_pairs={{0,8},{1,9},{2,10},{3,11},{4,12},{5,13},{6,14},{7,15},{8,0},{9,1},... | collective-permute-start | bytes 589832 | tf_op jit(solution)/shard_map/ppermute | solution.py:180
  26.2 1.2 shard_map.67
  27.3 7.5 %collective-permute-done.2.tok_b_ref = bf16[2,2,4,16,384]{4,3,2,1,0:T(8,128)(2,1)S(1)} collective-permute-done((bf16[2,2,4,16,384]{4,3,2,1,0:T(8,128)(2,1)S(1)}, bf16[2,2,4,16,384]{4,3,2,1,0:T(8,128)(2,1)S(1)}, u32[]{:S(2)}, u32[]{:S(2)}) %collective-permute-start.2) | collective-permute-done | bytes 196640 | tf_op jit(solution)/shard_map/ppermute | solution.py:180
  34.8 0.7 shard_map.68
  35.6 0.9 copy-done.4
  36.4 7.5 %all-to-all-start = ((bf16[8,128,384]{2,1,0:T(8,128)(2,1)}), bf16[8,128,384]{2,1,0:T(8,128)(2,1)S(1)}, u32[]{:S(2)}, u32[]{:S(2)}) async-start(bf16[8,128,384]{2,1,0:T(8,128)(2,1)} %bitcast.31), calls=%async_computation | async-start | bytes 1572864 | tf_op jit(solution)/shard_map/all_to_all | solution.py:207
  44.0 1.4 %dynamic-slice_bitcast_fusion.1 = bf16[4,16,384]{2,1,0:T(8,128)(2,1)} fusion(bf16[4,2,16,384]{3,2,1,0:T(8,128)(2,1)} %bitcast.32, s32[]{:T(128)S(6)} %select_n.56), kind=kLoop, calls=%fused_computation.2 | loop fusion | bytes 98308 | tf_op jit(solution)/shard_map/jit(dynamic_index_in_dim)/squeeze | solution.py:211
  45.4 2.2 %collective-permute-start.3 = (bf16[4,16,384]{2,1,0:T(8,128)(2,1)}, bf16[4,16,384]{2,1,0:T(8,128)(2,1)}, u32[]{:S(2)}, u32[]{:S(2)}) collective-permute-start(bf16[4,16,384]{2,1,0:T(8,128)(2,1)} %dynamic-slice_bitcast_fusion.1), channel_id=1, source_target_pairs={{0,8},{1,9},{2,10},{3,11},{4,12},{5,13},{6,14},{7,15},{8,0},{9,1},... | collective-permute-start | bytes 147464 | tf_op jit(solution)/shard_map/ppermute | solution.py:210
  47.6 4.1 %collective-permute-done.3.far_cot_ref = bf16[4,16,384]{2,1,0:T(8,128)(2,1)} collective-permute-done((bf16[4,16,384]{2,1,0:T(8,128)(2,1)}, bf16[4,16,384]{2,1,0:T(8,128)(2,1)}, u32[]{:S(2)}, u32[]{:S(2)}) %collective-permute-start.3) | collective-permute-done | bytes 49184 | tf_op jit(solution)/shard_map/ppermute | solution.py:210
  51.7 14.2 %all-to-all-done = bf16[8,128,384]{2,1,0:T(8,128)(2,1)S(1)} async-done(((bf16[8,128,384]{2,1,0:T(8,128)(2,1)}), bf16[8,128,384]{2,1,0:T(8,128)(2,1)S(1)}, u32[]{:S(2)}, u32[]{:S(2)}) %all-to-all-start) | async-done | bytes 786464 | tf_op jit(solution)/shard_map/all_to_all | solution.py:207
  65.9 0.9 copy-done.6
  66.8 1.0 shard_map.69
  67.9 0.6 copy-done.10
  68.5 26.1 %all_gather.3 = bf16[1024,384]{1,0:T(8,128)(2,1)S(1)} all-gather(bf16[128,384]{1,0:T(8,128)(2,1)S(1)} %bitcast.34), channel_id=1, replica_groups={{0,1,2,3,4,5,6,7},{8,9,10,11,12,13,14,15},{16,17,18,19,20,21,22,23},{24..., dimensions={0}, use_global_device_ids=true | all-gather | bytes 884736 | tf_op jit(solution)/shard_map/all_gather | solution.py:220
  94.5 0.7 shard_map.70
  95.2 1.9 %collective-permute-start.4 = (bf16[2,512,384]{2,1,0:T(8,128)(2,1)S(1)}, bf16[2,512,384]{2,1,0:T(8,128)(2,1)S(1)}, u32[]{:S(2)}, u32[]{:S(2)}) collective-permute-start(bf16[2,512,384]{2,1,0:T(8,128)(2,1)S(1)} %shard_map.70), channel_id=1, source_target_pairs={{0,16},{16,0},{32,48},{48,32},{64,80},{80,64},{96,112},{112,96},{1... | collective-permute-start | bytes 2359304 | tf_op jit(solution)/shard_map/ppermute | solution.py:232
  97.1 1.4 %shard_map.73 = bf16[384,384]{1,0:T(8,128)(2,1)} custom-call(bf16[2,6,4,16,384]{4,3,2,1,0:T(8,128)(2,1)S(1)} %collective-permute-done.1.tok_a_ref, bf16[2,2,4,16,384]{4,3,2,1,0:T(8,128)(2,1)S(1)} %copy-done.3, bf16[8,2,4,16,384]{4,3,2,1,0:T(8,128)(2,1)S(1)} %bitcast.22), custom_call_target="tpu_custom_call" | custom-call | flops 301989888 | bytes 1572864 | tf_op jit(solution)/shard_map/pallas_call | solution.py:20
  98.6 2.6 %collective-permute-start.6 = (bf16[384,384]{1,0:T(8,128)(2,1)}, bf16[384,384]{1,0:T(8,128)(2,1)}, u32[]{:S(2)}, u32[]{:S(2)}) collective-permute-start(bf16[384,384]{1,0:T(8,128)(2,1)} %shard_map.73), channel_id=1, source_target_pairs={{0,8},{1,9},{2,10},{3,11},{4,12},{5,13},{6,14},{7,15},{8,0},{9,1},... | collective-permute-start | bytes 884744 | tf_op jit(solution)/shard_map/ppermute | solution.py:237
  101.2 0.6 shard_map.71
  101.8 0.9 copy-done.1
  102.7 10.2 %all-to-all-start.1 = ((bf16[64,16,384]{2,1,0:T(8,128)(2,1)}), bf16[64,16,384]{2,1,0:T(8,128)(2,1)S(1)}, u32[]{:S(2)}, u32[]{:S(2)}) async-start(bf16[64,16,384]{2,1,0:T(8,128)(2,1)} %bitcast.30), calls=%async_computation.1 | async-start | bytes 1572864 | tf_op jit(solution)/shard_map/all_to_all | solution.py:257
  112.9 0.0 copy-start.8
  112.9 3.6 %collective-permute-start.5 = (bf16[64,384]{1,0:T(8,128)(2,1)}, bf16[64,384]{1,0:T(8,128)(2,1)S(1)}, u32[]{:S(2)}, u32[]{:S(2)}) collective-permute-start(bf16[64,384]{1,0:T(8,128)(2,1)} %copy-done.10), channel_id=1, source_target_pairs={{0,8},{1,9},{2,10},{3,11},{4,12},{5,13},{6,14},{7,15},{8,0},{9,1},... | collective-permute-start | bytes 147464 | tf_op jit(solution)/shard_map/ppermute | solution.py:271
  116.6 2.4 %shard_map.74 = f32[384,384]{1,0:T(8,128)} custom-call(s32[1]{0:T(128)} %bitcast.side_ref, bf16[2,8,4,2,16,384]{5,4,3,2,1,0:T(8,128)(2,1)S(1)} %bitcast.27, bf16[8,2,4,16,384]{4,3,2,1,0:T(8,128)(2,1)S(1)} %bitcast.24, bf16[384,384]{1,0:T(8,128)(2,1)} %collective-permute-done.6.far_ref), custom_call_target="tpu_custom_call" | custom-call | flops 12079595520 | bytes 1572864 | tf_op jit(solution)/shard_map/pallas_call | solution.py:20
  119.0 11.9 %collective-permute-done.5 = bf16[64,384]{1,0:T(8,128)(2,1)S(1)} collective-permute-done((bf16[64,384]{1,0:T(8,128)(2,1)}, bf16[64,384]{1,0:T(8,128)(2,1)S(1)}, u32[]{:S(2)}, u32[]{:S(2)}) %collective-permute-start.5) | collective-permute-done | bytes 49184 | tf_op jit(solution)/shard_map/ppermute | solution.py:271
  130.9 0.7 copy.7
  131.6 7.0 %all-to-all-done.1 = bf16[64,16,384]{2,1,0:T(8,128)(2,1)S(1)} async-done(((bf16[64,16,384]{2,1,0:T(8,128)(2,1)}), bf16[64,16,384]{2,1,0:T(8,128)(2,1)S(1)}, u32[]{:S(2)}, u32[]{:S(2)}) %all-to-all-start.1) | async-done | bytes 786464 | tf_op jit(solution)/shard_map/all_to_all | solution.py:257
  138.5 0.7 shard_map.72
  (24 shorter events, 0.1 us)
Async XLA Ops:
  0.6 19.6 %copy-start.5 = (bf16[384,384]{1,0:T(8,128)(2,1)S(1)}, bf16[384,384]{1,0:T(8,128)(2,1)}, u32[]{:S(2)}) copy-start(bf16[384,384]{1,0:T(8,128)(2,1)} %codes_hbm.1) | copy-start | bytes 884740
  0.7 25.5 %copy-start = (bf16[2048,384]{1,0:T(8,128)(2,1)S(1)}, bf16[2048,384]{1,0:T(8,128)(2,1)}, u32[]{:S(2)}) copy-start(bf16[2048,384]{1,0:T(8,128)(2,1)} %param.4) | copy-start | bytes 4718596
  0.7 25.5 %copy-start.9 = (f32[3,384]{1,0:T(4,128)S(1)}, f32[3,384]{1,0:T(4,128)}, u32[]{:S(2)}) copy-start(f32[3,384]{1,0:T(4,128)} %scales_ref.1) | copy-start | bytes 13828
  2.9 31.9 %collective-permute-start.1 = (bf16[2,6,4,16,384]{4,3,2,1,0:T(8,128)(2,1)}, bf16[2,6,4,16,384]{4,3,2,1,0:T(8,128)(2,1)S(1)}, u32[]{:S(2)}, u32[]{:S(2)}) collective-permute-start(bf16[2,6,4,16,384]{4,3,2,1,0:T(8,128)(2,1)} %slice.8), channel_id=1, source_target_pairs={{0,776},{1,777},{2,778},{3,779},{4,780},{5,781},{6,782},{7,783},{8... | collective-permute-start | bytes 1769480 | tf_op jit(solution)/shard_map/ppermute | solution.py:179
  20.2 14.6 %collective-permute-start = (bf16[384,384]{1,0:T(8,128)(2,1)S(1)}, bf16[384,384]{1,0:T(8,128)(2,1)S(1)}, u32[]{:S(2)}, u32[]{:S(2)}) collective-permute-start(bf16[384,384]{1,0:T(8,128)(2,1)S(1)} %copy-done.5), channel_id=1, source_target_pairs={{0,8},{1,9},{2,10},{3,11},{4,12},{5,13},{6,14},{7,15},{8,0},{9,1},... | collective-permute-start | bytes 884744 | tf_op jit(solution)/shard_map/ppermute | solution.py:170
  22.2 12.6 %collective-permute-start.2 = (bf16[2,2,4,16,384]{4,3,2,1,0:T(8,128)(2,1)S(1)}, bf16[2,2,4,16,384]{4,3,2,1,0:T(8,128)(2,1)S(1)}, u32[]{:S(2)}, u32[]{:S(2)}) collective-permute-start(bf16[2,2,4,16,384]{4,3,2,1,0:T(8,128)(2,1)S(1)} %slice.9), channel_id=1, source_target_pairs={{0,8},{1,9},{2,10},{3,11},{4,12},{5,13},{6,14},{7,15},{8,0},{9,1},... | collective-permute-start | bytes 589832 | tf_op jit(solution)/shard_map/ppermute | solution.py:180
  34.8 1.6 %copy-start.2 = (bf16[2,2,4,16,384]{4,3,2,1,0:T(8,128)(2,1)}, bf16[2,2,4,16,384]{4,3,2,1,0:T(8,128)(2,1)S(1)}, u32[]{:S(2)}) copy-start(bf16[2,2,4,16,384]{4,3,2,1,0:T(8,128)(2,1)S(1)} %collective-permute-done.2.tok_b_ref) | copy-start | bytes 589828
  35.6 0.9 copy-start.4
  36.4 29.5 %all-to-all-start = ((bf16[8,128,384]{2,1,0:T(8,128)(2,1)}), bf16[8,128,384]{2,1,0:T(8,128)(2,1)S(1)}, u32[]{:S(2)}, u32[]{:S(2)}) async-start(bf16[8,128,384]{2,1,0:T(8,128)(2,1)} %bitcast.31), calls=%async_computation | async-start | bytes 1572864 | tf_op jit(solution)/shard_map/all_to_all | solution.py:207
  45.4 6.3 %collective-permute-start.3 = (bf16[4,16,384]{2,1,0:T(8,128)(2,1)}, bf16[4,16,384]{2,1,0:T(8,128)(2,1)}, u32[]{:S(2)}, u32[]{:S(2)}) collective-permute-start(bf16[4,16,384]{2,1,0:T(8,128)(2,1)} %dynamic-slice_bitcast_fusion.1), channel_id=1, source_target_pairs={{0,8},{1,9},{2,10},{3,11},{4,12},{5,13},{6,14},{7,15},{8,0},{9,1},... | collective-permute-start | bytes 147464 | tf_op jit(solution)/shard_map/ppermute | solution.py:210
  65.9 0.9 copy-start.6
  67.9 0.6 copy-start.10
  68.5 26.1 %copy-start.7 = (bf16[64,384]{1,0:T(8,128)(2,1)}, bf16[64,384]{1,0:T(8,128)(2,1)S(1)}, u32[]{:S(2)}) copy-start(bf16[64,384]{1,0:T(8,128)(2,1)S(1)} %get-tuple-element.14) | copy-start | bytes 147460
  68.5 28.6 %copy-start.3 = (bf16[2,2,4,16,384]{4,3,2,1,0:T(8,128)(2,1)S(1)}, bf16[2,2,4,16,384]{4,3,2,1,0:T(8,128)(2,1)}, u32[]{:S(2)}) copy-start(bf16[2,2,4,16,384]{4,3,2,1,0:T(8,128)(2,1)} %copy-done.2) | copy-start | bytes 589828
  95.2 6.0 %collective-permute-start.4 = (bf16[2,512,384]{2,1,0:T(8,128)(2,1)S(1)}, bf16[2,512,384]{2,1,0:T(8,128)(2,1)S(1)}, u32[]{:S(2)}, u32[]{:S(2)}) collective-permute-start(bf16[2,512,384]{2,1,0:T(8,128)(2,1)S(1)} %shard_map.70), channel_id=1, source_target_pairs={{0,16},{16,0},{32,48},{48,32},{64,80},{80,64},{96,112},{112,96},{1... | collective-permute-start | bytes 2359304 | tf_op jit(solution)/shard_map/ppermute | solution.py:232
  98.6 18.0 %collective-permute-start.6 = (bf16[384,384]{1,0:T(8,128)(2,1)}, bf16[384,384]{1,0:T(8,128)(2,1)}, u32[]{:S(2)}, u32[]{:S(2)}) collective-permute-start(bf16[384,384]{1,0:T(8,128)(2,1)} %shard_map.73), channel_id=1, source_target_pairs={{0,8},{1,9},{2,10},{3,11},{4,12},{5,13},{6,14},{7,15},{8,0},{9,1},... | collective-permute-start | bytes 884744 | tf_op jit(solution)/shard_map/ppermute | solution.py:237
  101.8 0.9 copy-start.1
  102.7 35.8 %all-to-all-start.1 = ((bf16[64,16,384]{2,1,0:T(8,128)(2,1)}), bf16[64,16,384]{2,1,0:T(8,128)(2,1)S(1)}, u32[]{:S(2)}, u32[]{:S(2)}) async-start(bf16[64,16,384]{2,1,0:T(8,128)(2,1)} %bitcast.30), calls=%async_computation.1 | async-start | bytes 1572864 | tf_op jit(solution)/shard_map/all_to_all | solution.py:257
  112.9 17.9 %copy-start.8 = (bf16[64,384]{1,0:T(8,128)(2,1)S(1)}, bf16[64,384]{1,0:T(8,128)(2,1)}, u32[]{:S(2)}) copy-start(bf16[64,384]{1,0:T(8,128)(2,1)} %copy-done.7) | copy-start | bytes 147460
  112.9 17.9 %collective-permute-start.5 = (bf16[64,384]{1,0:T(8,128)(2,1)}, bf16[64,384]{1,0:T(8,128)(2,1)S(1)}, u32[]{:S(2)}, u32[]{:S(2)}) collective-permute-start(bf16[64,384]{1,0:T(8,128)(2,1)} %copy-done.10), channel_id=1, source_target_pairs={{0,8},{1,9},{2,10},{3,11},{4,12},{5,13},{6,14},{7,15},{8,0},{9,1},... | collective-permute-start | bytes 147464 | tf_op jit(solution)/shard_map/ppermute | solution.py:271

commit v6 on v4

--- a/solution.py
+++ b/solution.py
@@ -30,7 +30,7 @@
 HBM = pl.BlockSpec(memory_space=pltpu.HBM)
 
 
-def project(start_ref, tok_hbm, codes_hbm, scales_hbm, w_ref, out_ref, tok_ref, codes_ref, scales_ref, sems):
+def project(start_ref, tok_hbm, codes_hbm, scales_hbm, w_ref, out_hbm, tok_ref, codes_ref, scales_ref, out_ref, sems):
     feat, units = codes_ref.shape
     cuts = [(z, y) for z in range(2) for y in (0, 1)]
     span = tok_ref.shape[1] // 2
@@ -56,7 +56,8 @@
         scale = jnp.where(row >= i * BLOCK, scales_ref[i : i + 1, :], scale)
     weight = (codes_ref[...].astype(F32) * scale).astype(BF16)
     w_ref[...] = weight
-    for (z, y), copy in zip(cuts, loads):
+    stores = []
+    for i, ((z, y), copy) in enumerate(zip(cuts, loads)):
         copy.wait()
         ys = slice(y * span, (y + 1) * span)
         piece = tok_ref[z, ys]
@@ -64,6 +65,14 @@
         res = res.astype(BF16).reshape(piece.shape[:-1] + (units,))
         for h in range(2):
             out_ref[h, ys, z] = res[:, :, h]
+        part = pl.ds(y * span, span)
+        store = pltpu.make_async_copy(
+            out_ref.at[:, part, z], out_hbm.at[:, part, z], sems.at[6 + i]
+        )
+        store.start()
+        stores.append(store)
+    for store in stores:
+        store.wait()
 
 
 def activate(side_ref, got_ref, cot_ref, far_cot_ref, act_ref, far_act_ref, slope_ref):
@@ -106,11 +115,16 @@
     for k, weight in enumerate((w_ref, far_w_ref)):
         total = back(core, slope_ref, weight) + other_ref[k].astype(F32)
         which = side if k == 0 else 1 - side
-        out_ref[which] = total.astype(BF16).reshape(out_ref.shape[1:])
+        high, mid, _, wide, low, rows, feat = out_ref.shape
+        total = total.astype(BF16).reshape(mid, wide, high, low, rows, feat)
+        for t in range(high):
+            out_ref[t, :, which] = total[:, :, t]
 
 
 def finish(got_ref, out_ref):
-    out_ref[...] = jnp.sum(got_ref[...].astype(F32), axis=1).astype(BF16)
+    for k in range(2):
+        part = got_ref[:, k].astype(F32)
+        out_ref[k] = jnp.sum(part.reshape((-1,) + part.shape[2:]), axis=0).astype(BF16)
 
 
 def outer(rows, grads):
@@ -158,12 +172,13 @@
             jax.ShapeDtypeStruct((2, ys, 2, per, sub, units), BF16),
         ],
         in_specs=[SMEM, HBM, HBM, HBM],
-        out_specs=[VMEM, VMEM],
+        out_specs=[VMEM, HBM],
         scratch_shapes=[
             pltpu.VMEM(tok.shape, BF16),
             pltpu.VMEM(codes.shape, BF16),
             pltpu.VMEM(scales.shape, F32),
-            pltpu.SemaphoreType.DMA((6,)),
+            pltpu.VMEM((2, ys, 2, per, sub, units), BF16),
+            pltpu.SemaphoreType.DMA((10,)),
         ],
         compiler_params=pltpu.CompilerParams(vmem_limit_bytes=58 * 2**20),
         cost_estimate=pl.CostEstimate(flops=flops, bytes_accessed=2 * size, transcendentals=0),
@@ -214,7 +229,7 @@
     far_part = lax.ppermute(far_part, "local", pair)
     (both,) = call(
         back_mine,
-        [((2, ys, 2, per // 2, sub, feat), BF16)],
+        [((2, 2, 2, ys // 2, per // 2, sub, feat), BF16)],
         [SMEM, SMEM, VMEM, VMEM, VMEM, VMEM],
         flops // 2, size,
         core, side, by_core, weight, far_weight, other,
@@ -223,9 +238,10 @@
     groups = [
         [
             (per * (ys * t + y) + 2 * h + c) * locals_ + z * ys + own
+            for t in range(2)
+            for m in range(2)
             for z in range(2)
-            for y in range(ys)
-            for t in range(2)
+            for y in range(m * ys // 2, (m + 1) * ys // 2)
             for h in range(per // 2)
         ]
         for c in range(2)
@@ -234,7 +250,7 @@
     sums = lax.all_to_all(
         both.reshape(nodes, sub, feat),
         ("node", "local"), 0, 0, axis_index_groups=groups, tiled=True,
-    ).reshape(2, nodes // 2, sub, feat)
+    ).reshape(4, 2, nodes // 8, sub, feat)
     (weight_grad,) = call(
         functools.partial(weigh_own, rows ** (-0.5)),
         [((feat, units), F32)],

time: 135 us -> 135 us (level)
  the two profiles are of different devices: /device:TPU:4 before, /device:TPU:14 now
where the time goes in v6:
time: 135 us; the launch traced here: 133 us
  starting transfers between devices  61.3 us (45%)
  waiting for transfers between devices  31.8 us (24%)
  blocking collectives  26.3 us (19%)
  Pallas kernels  9.72 us (7%)
  local copies, waits for them, and re-layouts  3.08 us (2%)
    all_gather x1, blocking collectives, shards(): lax.all_gather(slope.reshape(2 * mine, units), 'local', axis=0, tiled=Tru...  26.3 us
    all_to_all x1, starting transfers between devices, shards(): lax.all_to_all(both.reshape(nodes, sub, feat), ('node', 'local'), 0, 0, a...  20.5 us
    ppermute x1, starting transfers between devices, shards(): lax.ppermute(lax.dynamic_index_in_dim(tok, 1 - side[0], 3, False), ('node...  15.9 us
    ppermute x1, waiting for transfers between devices, shards(): act_far = lax.ppermute(act_far, 'local', pair)  12 us
    ppermute x1, waiting for transfers between devices, shards(): lax.ppermute(lax.dynamic_index_in_dim(cot, 1 - side[0], 1, False), 'local...  11.6 us
    all_to_all x1, starting transfers between devices, shards(): lax.all_to_all(partial.reshape(locals_, 2 * mine, units), 'local', 0, 0,...  10.5 us
    pallas_call x6, Pallas kernels, call(): pl.pallas_call(kernel, out_shape=[jax.ShapeDtypeStruct(s, d) for s, d in...  5.31 us
    all_to_all x1, waiting for transfers between devices, shards(): lax.all_to_all(both.reshape(nodes, sub, feat), ('node', 'local'), 0, 0, a...  4.7 us
  transfers between devices with their start and end apart: 8, of which 4 were waited for; matrix products, arithmetic and copies ran while one was open for 1% of the time, Pallas kernels for 3%

profile of v6, /device:TPU:14, one launch (start us, length us, event | category | flops | bytes accessed | tf_op | source)
XLA Modules:
  0.0 133.1 jit_solution(11590090442522154995)
XLA Ops:
  0.6 4.4 %shard_map.67 = (bf16[384,384]{1,0:T(8,128)(2,1)}, bf16[2,8,2,4,16,384]{5,4,3,2,1,0:T(8,128)(2,1)}) custom-call(s32[1]{0:T(128)} %bitcast.1.start_ref, bf16[2,8,4,2,16,384]{5,4,3,2,1,0:T(8,128)(2,1)} %bitcast.26, bf16[384,384]{1,0:T(8,128)(2,1)} %codes_hbm.1, f32[3,384]{1,0:T(4,128)} %scales_hbm.1), custom_call_target="tpu_custom_call" | custom-call | flops 603979776 | bytes 3145728 | tf_op jit(solution)/shard_map/pallas_call | solution.py:168
  5.0 0.0 copy-start.1
  5.1 10.5 %all-to-all-start = ((bf16[16,128,384]{2,1,0:T(8,128)(2,1)}), bf16[16,128,384]{2,1,0:T(8,128)(2,1)S(1)}, u32[]{:S(2)}, u32[]{:S(2)}) async-start(bf16[16,128,384]{2,1,0:T(8,128)(2,1)} %bitcast.32), calls=%async_computation | async-start | bytes 3145728 | tf_op jit(solution)/shard_map/all_to_all | solution.py:186
  15.6 0.0 copy-start
  15.6 0.0 copy-start.3
  15.6 0.0 copy-done.1
  15.6 1.0 dynamic-slice_bitcast_fusion
  16.6 15.9 %collective-permute-start.2 = (bf16[2,8,4,16,384]{4,3,2,1,0:T(8,128)(2,1)}, bf16[2,8,4,16,384]{4,3,2,1,0:T(8,128)(2,1)S(1)}, u32[]{:S(2)}, u32[]{:S(2)}) collective-permute-start(bf16[2,8,4,16,384]{4,3,2,1,0:T(8,128)(2,1)} %dynamic-slice_bitcast_fusion), channel_id=1, source_target_pairs={{0,776},{1,777},{2,778},{3,779},{4,780},{5,781},{6,782},{7,783},{8... | collective-permute-start | bytes 2359304 | tf_op jit(solution)/shard_map/ppermute | solution.py:199
  32.6 1.9 %collective-permute-start.1 = (bf16[384,384]{1,0:T(8,128)(2,1)S(1)}, bf16[384,384]{1,0:T(8,128)(2,1)S(1)}, u32[]{:S(2)}, u32[]{:S(2)}) collective-permute-start(bf16[384,384]{1,0:T(8,128)(2,1)S(1)} %copy-done), channel_id=1, source_target_pairs={{0,8},{1,9},{2,10},{3,11},{4,12},{5,13},{6,14},{7,15},{8,0},{9,1},... | collective-permute-start | bytes 884744 | tf_op jit(solution)/shard_map/ppermute | solution.py:192
  34.6 3.9 %collective-permute-start = (bf16[4,16,384]{2,1,0:T(8,128)(2,1)S(1)}, bf16[4,16,384]{2,1,0:T(8,128)(2,1)S(1)}, u32[]{:S(2)}, u32[]{:S(2)}) collective-permute-start(bf16[4,16,384]{2,1,0:T(8,128)(2,1)S(1)} %dynamic-slice_bitcast_fusion.1), channel_id=1, source_target_pairs={{0,8},{1,9},{2,10},{3,11},{4,12},{5,13},{6,14},{7,15},{8,0},{9,1},... | collective-permute-start | bytes 147464 | tf_op jit(solution)/shard_map/ppermute | solution.py:189
  38.5 11.6 %collective-permute-done.far_cot_ref = bf16[4,16,384]{2,1,0:T(8,128)(2,1)S(1)} collective-permute-done((bf16[4,16,384]{2,1,0:T(8,128)(2,1)S(1)}, bf16[4,16,384]{2,1,0:T(8,128)(2,1)S(1)}, u32[]{:S(2)}, u32[]{:S(2)}) %collective-permute-start) | collective-permute-done | bytes 49184 | tf_op jit(solution)/shard_map/ppermute | solution.py:189
  50.1 0.0 collective-permute-done.1.far_w_ref
  50.1 0.0 collective-permute-done.2.far_tok_ref
  50.1 3.6 %all-to-all-done = bf16[16,128,384]{2,1,0:T(8,128)(2,1)S(1)} async-done(((bf16[16,128,384]{2,1,0:T(8,128)(2,1)}), bf16[16,128,384]{2,1,0:T(8,128)(2,1)S(1)}, u32[]{:S(2)}, u32[]{:S(2)}) %all-to-all-start) | async-done | bytes 1572896 | tf_op jit(solution)/shard_map/all_to_all | solution.py:186
  53.7 0.4 shard_map.68
  54.0 26.3 %all_gather.3 = bf16[1024,384]{1,0:T(8,128)(2,1)S(1)} all-gather(bf16[128,384]{1,0:T(8,128)(2,1)S(1)} %bitcast.31), channel_id=1, replica_groups={{0,1,2,3,4,5,6,7},{8,9,10,11,12,13,14,15},{16,17,18,19,20,21,22,23},{24..., dimensions={0}, use_global_device_ids=true | all-gather | bytes 884736 | tf_op jit(solution)/shard_map/all_gather | solution.py:213
  80.3 0.7 shard_map.69
  81.0 1.9 %collective-permute-start.3 = (bf16[2,512,384]{2,1,0:T(8,128)(2,1)S(1)}, bf16[2,512,384]{2,1,0:T(8,128)(2,1)S(1)}, u32[]{:S(2)}, u32[]{:S(2)}) collective-permute-start(bf16[2,512,384]{2,1,0:T(8,128)(2,1)S(1)} %shard_map.69), channel_id=1, source_target_pairs={{0,16},{16,0},{32,48},{48,32},{64,80},{80,64},{96,112},{112,96},{1... | collective-permute-start | bytes 2359304 | tf_op jit(solution)/shard_map/ppermute | solution.py:225
  82.9 0.6 shard_map.72
  83.5 3.1 %collective-permute-start.5 = (bf16[384,384]{1,0:T(8,128)(2,1)S(1)}, bf16[384,384]{1,0:T(8,128)(2,1)S(1)}, u32[]{:S(2)}, u32[]{:S(2)}) collective-permute-start(bf16[384,384]{1,0:T(8,128)(2,1)S(1)} %shard_map.72), channel_id=1, source_target_pairs={{0,8},{1,9},{2,10},{3,11},{4,12},{5,13},{6,14},{7,15},{8,0},{9,1},... | collective-permute-start | bytes 884744 | tf_op jit(solution)/shard_map/ppermute | solution.py:229
  86.6 0.0 collective-permute-done.3.other_ref
  86.7 1.6 %shard_map.70 = bf16[2,2,2,4,2,16,384]{6,5,4,3,2,1,0:T(8,128)(2,1)} custom-call(s32[1]{0:T(128)} %bitcast.8.core_ref, s32[1]{0:T(128)} %bitcast.side_ref, bf16[8,2,2,2,16,384]{5,4,3,2,1,0:T(8,128)(2,1)S(1)} %bitcast.22, bf16[384,384]{1,0:T(8,128)(2,1)S(1)} %copy-done, bf16[384,384]{1,0:T(8,128)(2,1)S(1)} %collective-permute-done.1.far_w_ref, ...), custom_call_target="tpu_custom_call" | custom-call | flops 301989888 | bytes 1572864 | tf_op jit(solution)/shard_map/pallas_call | solution.py:20
  88.2 20.5 %all-to-all-start.1 = ((bf16[64,16,384]{2,1,0:T(8,128)(2,1)}), bf16[64,16,384]{2,1,0:T(8,128)(2,1)S(1)}, u32[]{:S(2)}, u32[]{:S(2)}) async-start(bf16[64,16,384]{2,1,0:T(8,128)(2,1)} %bitcast.14), calls=%async_computation.1 | async-start | bytes 1572864 | tf_op jit(solution)/shard_map/all_to_all | solution.py:250
  108.7 3.4 %collective-permute-start.4 = (bf16[64,384]{1,0:T(8,128)(2,1)S(1)}, bf16[64,384]{1,0:T(8,128)(2,1)S(1)}, u32[]{:S(2)}, u32[]{:S(2)}) collective-permute-start(bf16[64,384]{1,0:T(8,128)(2,1)S(1)} %get-tuple-element.22), channel_id=1, source_target_pairs={{0,8},{1,9},{2,10},{3,11},{4,12},{5,13},{6,14},{7,15},{8,0},{9,1},... | collective-permute-start | bytes 147464 | tf_op jit(solution)/shard_map/ppermute | solution.py:264
  112.1 0.0 collective-permute-done.5.far_ref
  112.1 0.0 copy-start.2
  112.2 1.4 %copy-done.2 = bf16[2048,384]{1,0:T(8,128)(2,1)S(1)} copy-done((bf16[2048,384]{1,0:T(8,128)(2,1)S(1)}, bf16[2048,384]{1,0:T(8,128)(2,1)}, u32[]{:S(2)}) %copy-start.2) | copy-done | bytes 1572888
  113.6 1.4 %shard_map.73 = f32[384,384]{1,0:T(8,128)} custom-call(s32[1]{0:T(128)} %bitcast.side_ref, bf16[2,8,4,2,16,384]{5,4,3,2,1,0:T(8,128)(2,1)S(1)} %bitcast.28, bf16[8,2,4,16,384]{4,3,2,1,0:T(8,128)(2,1)S(1)} %bitcast.23, bf16[384,384]{1,0:T(8,128)(2,1)S(1)} %collective-permute-done.5.far_ref), custom_call_target="tpu_custom_call" | custom-call | flops 12079595520 | bytes 1572864 | tf_op jit(solution)/shard_map/pallas_call | solution.py:20
  115.0 12.0 %collective-permute-done.4 = bf16[64,384]{1,0:T(8,128)(2,1)S(1)} collective-permute-done((bf16[64,384]{1,0:T(8,128)(2,1)S(1)}, bf16[64,384]{1,0:T(8,128)(2,1)S(1)}, u32[]{:S(2)}, u32[]{:S(2)}) %collective-permute-start.4) | collective-permute-done | bytes 49184 | tf_op jit(solution)/shard_map/ppermute | solution.py:264
  127.0 0.7 copy.7
  127.6 4.7 %all-to-all-done.1 = bf16[64,16,384]{2,1,0:T(8,128)(2,1)S(1)} async-done(((bf16[64,16,384]{2,1,0:T(8,128)(2,1)}), bf16[64,16,384]{2,1,0:T(8,128)(2,1)S(1)}, u32[]{:S(2)}, u32[]{:S(2)}) %all-to-all-start.1) | async-done | bytes 786464 | tf_op jit(solution)/shard_map/all_to_all | solution.py:250
  132.3 0.7 shard_map.71
  (5 shorter events, 0.1 us)
Async XLA Ops:
  5.0 10.6 %copy-start.1 = (bf16[2048,384]{1,0:T(8,128)(2,1)S(1)}, bf16[2048,384]{1,0:T(8,128)(2,1)}, u32[]{:S(2)}) copy-start(bf16[2048,384]{1,0:T(8,128)(2,1)} %param.4) | copy-start | bytes 4718596
  5.1 48.6 %all-to-all-start = ((bf16[16,128,384]{2,1,0:T(8,128)(2,1)}), bf16[16,128,384]{2,1,0:T(8,128)(2,1)S(1)}, u32[]{:S(2)}, u32[]{:S(2)}) async-start(bf16[16,128,384]{2,1,0:T(8,128)(2,1)} %bitcast.32), calls=%async_computation | async-start | bytes 3145728 | tf_op jit(solution)/shard_map/all_to_all | solution.py:186
  15.6 17.0 %copy-start = (bf16[384,384]{1,0:T(8,128)(2,1)S(1)}, bf16[384,384]{1,0:T(8,128)(2,1)}, u32[]{:S(2)}) copy-start(bf16[384,384]{1,0:T(8,128)(2,1)} %get-tuple-element.15.w_ref) | copy-start | bytes 884740
  15.6 18.9 %copy-start.3 = (bf16[128,384]{1,0:T(8,128)(2,1)S(1)}, bf16[128,384]{1,0:T(8,128)(2,1)}, u32[]{:S(2)}) copy-start(bf16[128,384]{1,0:T(8,128)(2,1)} %param.7) | copy-start | bytes 294916
  16.6 33.4 %collective-permute-start.2 = (bf16[2,8,4,16,384]{4,3,2,1,0:T(8,128)(2,1)}, bf16[2,8,4,16,384]{4,3,2,1,0:T(8,128)(2,1)S(1)}, u32[]{:S(2)}, u32[]{:S(2)}) collective-permute-start(bf16[2,8,4,16,384]{4,3,2,1,0:T(8,128)(2,1)} %dynamic-slice_bitcast_fusion), channel_id=1, source_target_pairs={{0,776},{1,777},{2,778},{3,779},{4,780},{5,781},{6,782},{7,783},{8... | collective-permute-start | bytes 2359304 | tf_op jit(solution)/shard_map/ppermute | solution.py:199
  32.6 17.5 %collective-permute-start.1 = (bf16[384,384]{1,0:T(8,128)(2,1)S(1)}, bf16[384,384]{1,0:T(8,128)(2,1)S(1)}, u32[]{:S(2)}, u32[]{:S(2)}) collective-permute-start(bf16[384,384]{1,0:T(8,128)(2,1)S(1)} %copy-done), channel_id=1, source_target_pairs={{0,8},{1,9},{2,10},{3,11},{4,12},{5,13},{6,14},{7,15},{8,0},{9,1},... | collective-permute-start | bytes 884744 | tf_op jit(solution)/shard_map/ppermute | solution.py:192
  34.6 15.5 %collective-permute-start = (bf16[4,16,384]{2,1,0:T(8,128)(2,1)S(1)}, bf16[4,16,384]{2,1,0:T(8,128)(2,1)S(1)}, u32[]{:S(2)}, u32[]{:S(2)}) collective-permute-start(bf16[4,16,384]{2,1,0:T(8,128)(2,1)S(1)} %dynamic-slice_bitcast_fusion.1), channel_id=1, source_target_pairs={{0,8},{1,9},{2,10},{3,11},{4,12},{5,13},{6,14},{7,15},{8,0},{9,1},... | collective-permute-start | bytes 147464 | tf_op jit(solution)/shard_map/ppermute | solution.py:189
  81.0 5.7 %collective-permute-start.3 = (bf16[2,512,384]{2,1,0:T(8,128)(2,1)S(1)}, bf16[2,512,384]{2,1,0:T(8,128)(2,1)S(1)}, u32[]{:S(2)}, u32[]{:S(2)}) collective-permute-start(bf16[2,512,384]{2,1,0:T(8,128)(2,1)S(1)} %shard_map.69), channel_id=1, source_target_pairs={{0,16},{16,0},{32,48},{48,32},{64,80},{80,64},{96,112},{112,96},{1... | collective-permute-start | bytes 2359304 | tf_op jit(solution)/shard_map/ppermute | solution.py:225
  83.5 28.6 %collective-permute-start.5 = (bf16[384,384]{1,0:T(8,128)(2,1)S(1)}, bf16[384,384]{1,0:T(8,128)(2,1)S(1)}, u32[]{:S(2)}, u32[]{:S(2)}) collective-permute-start(bf16[384,384]{1,0:T(8,128)(2,1)S(1)} %shard_map.72), channel_id=1, source_target_pairs={{0,8},{1,9},{2,10},{3,11},{4,12},{5,13},{6,14},{7,15},{8,0},{9,1},... | collective-permute-start | bytes 884744 | tf_op jit(solution)/shard_map/ppermute | solution.py:229
  88.2 44.1 %all-to-all-start.1 = ((bf16[64,16,384]{2,1,0:T(8,128)(2,1)}), bf16[64,16,384]{2,1,0:T(8,128)(2,1)S(1)}, u32[]{:S(2)}, u32[]{:S(2)}) async-start(bf16[64,16,384]{2,1,0:T(8,128)(2,1)} %bitcast.14), calls=%async_computation.1 | async-start | bytes 1572864 | tf_op jit(solution)/shard_map/all_to_all | solution.py:250
  108.7 18.2 %collective-permute-start.4 = (bf16[64,384]{1,0:T(8,128)(2,1)S(1)}, bf16[64,384]{1,0:T(8,128)(2,1)S(1)}, u32[]{:S(2)}, u32[]{:S(2)}) collective-permute-start(bf16[64,384]{1,0:T(8,128)(2,1)S(1)} %get-tuple-element.22), channel_id=1, source_target_pairs={{0,8},{1,9},{2,10},{3,11},{4,12},{5,13},{6,14},{7,15},{8,0},{9,1},... | collective-permute-start | bytes 147464 | tf_op jit(solution)/shard_map/ppermute | solution.py:264
  112.1 1.4 %copy-start.2 = (bf16[2048,384]{1,0:T(8,128)(2,1)S(1)}, bf16[2048,384]{1,0:T(8,128)(2,1)}, u32[]{:S(2)}) copy-start(bf16[2048,384]{1,0:T(8,128)(2,1)} %param.4) | copy-start | bytes 4718596

commit v7 on v6

v7 whole, which is shorter than its diff:
```python
import functools
import math

import jax
import jax.numpy as jnp
from jax import lax
from jax.experimental import pallas as pl
from jax.experimental.pallas import tpu as pltpu
from jax.sharding import PartitionSpec as P

BLOCK = 2048
F32 = jnp.float32
BF16 = jnp.bfloat16
ROOT = math.sqrt(2.0 / math.pi)
VMEM = pl.BlockSpec(memory_space=pltpu.VMEM)
SMEM = pl.BlockSpec(memory_space=pltpu.SMEM)


def call(kernel, outs, specs, flops, size, *args):
    return pl.pallas_call(
        kernel,
        out_shape=[jax.ShapeDtypeStruct(s, d) for s, d in outs],
        in_specs=specs,
        out_specs=[VMEM] * len(outs),
        compiler_params=pltpu.CompilerParams(vmem_limit_bytes=40 * 2**20),
        cost_estimate=pl.CostEstimate(flops=flops, bytes_accessed=size, transcendentals=0),
    )(*args)


HBM = pl.BlockSpec(memory_space=pltpu.HBM)


def project(start_ref, tok_hbm, codes_hbm, scales_hbm, w_ref, out_hbm, tok_ref, codes_ref, scales_ref, out_ref, sems):
    feat, units = codes_ref.shape
    cuts = [(z, y) for z in range(2) for y in (0, 1)]
    span = tok_ref.shape[1] // 2
    first = [
        pltpu.make_async_copy(codes_hbm, codes_ref, sems.at[0]),
        pltpu.make_async_copy(scales_hbm, scales_ref, sems.at[1]),
    ]
    loads = [
        pltpu.make_async_copy(
            tok_hbm.at[z, pl.ds(y * span, span)],
            tok_ref.at[z, pl.ds(y * span, span)],
            sems.at[2 + i],
        )
        for i, (z, y) in enumerate(cuts)
    ]
    for copy in first + loads:
        copy.start()
    for copy in first:
        copy.wait()
    row = start_ref[0] + lax.broadcasted_iota(jnp.int32, (feat, units), 0)
    scale = jnp.broadcast_to(scales_ref[0:1, :], (feat, units))
    for i in range(1, scales_ref.shape[0]):
        scale = jnp.where(row >= i * BLOCK, scales_ref[i : i + 1, :], scale)
    weight = (codes_ref[...].astype(F32) * scale).astype(BF16)
    w_ref[...] = weight
    stores = []
    for i, ((z, y), copy) in enumerate(zip(cuts, loads)):
        copy.wait()
        ys = slice(y * span, (y + 1) * span)
        piece = tok_ref[z, ys]
        res = jnp.dot(piece.reshape(-1, feat), weight, preferred_element_type=F32)
        res = res.astype(BF16).reshape(piece.shape[:-1] + (units,))
        for q in range(2):
            for h in range(2):
                out_ref[q, h, ys, z] = res[:, q, :, h]
        part = pl.ds(y * span, span)
        store = pltpu.make_async_copy(
            out_ref.at[:, :, part, z], out_hbm.at[:, :, part, z], sems.at[6 + i]
        )
        store.start()
        stores.append(store)
    for store in stores:
        store.wait()


def activate(feat, par_ref, side_ref, got_ref, *refs):
    cots, acts, slope_ref = refs[:4], refs[4:8], refs[8]
    par, side = par_ref[0], side_ref[0]
    for i in range(4):
        unit, half = i % 2, i // 2
        q = par if unit == 0 else 1 - par
        t = side if half == 0 else 1 - side
        pre = jnp.sum(got_ref[q, :, t].astype(F32), axis=0)
        cot = cots[i][par, :, side] if i == 0 else cots[i][feat:, :]
        cot = cot.reshape(pre.shape).astype(F32)
        square = pre * pre
        tanh = jnp.tanh(ROOT * (pre + 0.044715 * square * pre))
        acts[i][...] = (0.5 * pre * (1.0 + tanh)).astype(BF16)
        inner = ROOT * (1.0 + 3.0 * 0.044715 * square)
        grad = 0.5 * (1.0 + tanh) + 0.5 * pre * (1.0 - tanh * tanh) * inner
        slope_ref[unit, t] = (cot * grad).astype(BF16)


def gather(par_ref, side_ref, own_ref, x_ref, z_ref, both_ref, out_ref):
    par, side = par_ref[0], side_ref[0]
    for i, ref in enumerate((own_ref, x_ref, z_ref, both_ref)):
        q = par if i % 2 == 0 else 1 - par
        t = side if i < 2 else 1 - side
        out_ref[q, :, t] = ref[...].reshape(out_ref.shape[1], *out_ref.shape[3:])


def back(core, slope_ref, weights, out_feat):
    total = None
    for unit, weight in enumerate(weights):
        rows = slope_ref[:, unit, :, core]
        part = lax.dot_general(
            rows.reshape(-1, rows.shape[-1]),
            weight[: out_feat, :],
            (((1,), (1,)), ((), ())),
            preferred_element_type=F32,
        )
        total = part if total is None else total + part
    return total


def back_other(core_ref, slope_ref, *refs):
    core, out_ref = 1 - core_ref[0], refs[4]
    for k in range(2):
        out_ref[k] = back(
            core, slope_ref, refs[2 * k : 2 * k + 2], out_ref.shape[-1]
        ).astype(BF16)


def back_mine(core_ref, side_ref, slope_ref, *refs):
    core, side = core_ref[0], side_ref[0]
    other_ref, out_ref = refs[4:]
    high, mid, _, wide, rows, feat = out_ref.shape
    for k in range(2):
        total = back(core, slope_ref, refs[2 * k : 2 * k + 2], feat)
        total = total + other_ref[k].astype(F32)
        which = side if k == 0 else 1 - side
        total = total.astype(BF16).reshape(mid, wide, high, rows, feat)
        for t in range(high):
            out_ref[t, :, which] = total[:, :, t]


def finish(got_ref, out_ref):
    for k in range(2):
        part = got_ref[:, k].astype(F32)
        out_ref[k] = jnp.sum(part.reshape((-1,) + part.shape[2:]), axis=0).astype(BF16)


def outer(toks, slope_ref, unit):
    total = None
    for z, rows in enumerate(toks):
        grads = slope_ref[:, unit, z]
        part = lax.dot_general(
            rows.reshape(-1, rows.shape[-1]),
            grads.reshape(-1, grads.shape[-1]),
            (((0,), (0,)), ((), ())),
            preferred_element_type=F32,
        )
        total = part if total is None else total + part
    return total


def weigh_far(par_ref, side_ref, tok_ref, far_tok_ref, slope_ref, x_ref, z_ref, both_ref):
    par, side = par_ref[0], side_ref[0]
    mine = [tok_ref[z, :, par, :, side] for z in range(2)]
    far = [far_tok_ref[z] for z in range(2)]
    z_ref[...] = outer(far, slope_ref, 0).astype(BF16)
    both_ref[...] = outer(far, slope_ref, 1).astype(BF16)
    x_ref[...] = outer(mine, slope_ref, 1).astype(BF16)


def weigh_own(factor, par_ref, side_ref, tok_ref, slope_ref, x_ref, z_ref, both_ref, out_ref):
    par, side = par_ref[0], side_ref[0]
    total = outer([tok_ref[z, :, par, :, side] for z in range(2)], slope_ref, 0)
    for ref in (x_ref, z_ref, both_ref):
        total = total + ref[...].astype(F32)
    out_ref[...] = total * factor


def shards(locals_, nodes, tokens, codes, scales, cotangent):
    rows, feat = tokens.shape
    units = codes.shape[1]
    ys = locals_ // 2
    per = nodes // locals_
    sub = rows // nodes // 2
    mine = 2 * sub
    node = lax.axis_index("node").astype(jnp.int32)
    local = lax.axis_index("local").astype(jnp.int32)
    start = (local * feat).reshape(1)
    core = (node % 2).reshape(1)
    par = (node // 2 % 2).reshape(1)
    side = (local // ys).reshape(1)
    tok = tokens.reshape(2, ys, 2, 2, 2, sub, feat)
    cot = cotangent.reshape(2, 2, 2, sub, units)
    flops = 2 * rows * feat * units
    size = 2 * rows * feat

    def moved(n, l):
        return n % nodes * locals_ + l

    spots = [(n, l) for n in range(nodes) for l in range(locals_)]
    over_x = [(i, i ^ 2) for i in range(nodes)]
    over_z = [(i, (i + ys) % locals_) for i in range(locals_)]
    over_both = [(moved(n, l), moved(n ^ 2, (l + ys) % locals_)) for n, l in spots]

    def send(x, z, both):
        return (
            lax.ppermute(x, "node", over_x),
            lax.ppermute(z, "local", over_z),
            lax.ppermute(both, ("node", "local"), over_both),
        )

    weight, partial = pl.pallas_call(
        project,
        out_shape=[
            jax.ShapeDtypeStruct((feat, units), BF16),
            jax.ShapeDtypeStruct((2, 2, ys, 2, 2, sub, units), BF16),
        ],
        in_specs=[SMEM, HBM, HBM, HBM],
        out_specs=[VMEM, HBM],
        scratch_shapes=[
            pltpu.VMEM(tok.shape, BF16),
            pltpu.VMEM(codes.shape, BF16),
            pltpu.VMEM(scales.shape, F32),
            pltpu.VMEM((2, 2, ys, 2, 2, sub, units), BF16),
            pltpu.SemaphoreType.DMA((10,)),
        ],
        compiler_params=pltpu.CompilerParams(vmem_limit_bytes=58 * 2**20),
        cost_estimate=pl.CostEstimate(flops=flops, bytes_accessed=2 * size, transcendentals=0),
    )(start, tok, codes, scales)
    members = [
        [moved(n + 2 * q, l) for q in range(2) for l in range(locals_)]
        for n in range(nodes)
        if n & 2 == 0
    ]
    got = lax.all_to_all(
        partial.reshape(2 * locals_, 2 * mine, units),
        ("node", "local"), 0, 0, axis_index_groups=members, tiled=True,
    ).reshape(2, locals_, 2, mine, units)

    def piece(q, t):
        part = lax.dynamic_index_in_dim(
            lax.dynamic_index_in_dim(cot, q, 0, False), t, 1, False
        )
        return jnp.concatenate([weight, part.reshape(mine, units)], axis=0)

    p, z = par[0], side[0]
    far = send(piece(1 - p, z), piece(p, 1 - z), piece(1 - p, 1 - z))
    block = nodes // 4
    step = [
        (moved(n, l), moved(n + (block if l >= ys else nodes - block), (l + ys) % locals_))
        for n, l in spots
    ]
    leave = lax.dynamic_index_in_dim(lax.dynamic_index_in_dim(tok, p, 2, False), 1 - z, 3, False)
    far_tok = lax.ppermute(leave, ("node", "local"), step)
    got, far, far_tok = lax.optimization_barrier((got, far, far_tok))
    *acts, slope = call(
        functools.partial(activate, feat),
        [((mine, units), BF16)] * 4 + [((2, 2, mine, units), BF16)],
        [SMEM, SMEM] + [VMEM] * 5,
        rows * units * 4, size,
        par, side, got, cot, *far,
    )
    lines = [list(range(t * ys, (t + 1) * ys)) for t in range(2)]
    spread = lax.all_gather(
        slope.reshape(4 * mine, units), "local", axis=0, tiled=True, axis_index_groups=lines
    ).reshape(ys, 2, 2, 2, sub, units)
    weights = (weight,) + tuple(far)
    (other,) = call(
        back_other,
        [((2, rows // 8, feat), BF16)],
        [SMEM] + [VMEM] * 5,
        flops // 2, size,
        core, spread, *weights,
    )
    other = lax.ppermute(other, "node", [(i, i ^ 1) for i in range(nodes)])
    shares = call(
        weigh_far,
        [((feat, units), BF16)] * 3,
        [SMEM, SMEM, VMEM, VMEM, VMEM],
        flops // 2, size,
        par, side, tok, far_tok, spread,
    )
    shares = send(*shares)
    (both,) = call(
        back_mine,
        [((2, 2, 2, ys // 2, sub, feat), BF16)],
        [SMEM, SMEM] + [VMEM] * 6,
        flops // 2, size,
        core, side, spread, *weights, other,
    )
    both, acts = lax.optimization_barrier((both, acts))
    groups = [
        [
            moved(per * (ys * t + y) + low, k * ys + own)
            for t in range(2)
            for m in range(2)
            for k in range(2)
            for y in range(m * ys // 2, (m + 1) * ys // 2)
        ]
        for low in range(per)
        for own in range(ys)
    ]
    sums = lax.all_to_all(
        both.reshape(nodes // 2, sub, feat),
        ("node", "local"), 0, 0, axis_index_groups=groups, tiled=True,
    ).reshape(4, 2, nodes // 16, sub, feat)
    (weight_grad,) = call(
        functools.partial(weigh_own, rows ** (-0.5)),
        [((feat, units), F32)],
        [SMEM, SMEM] + [VMEM] * 5,
        10 * flops, size,
        par, side, tok, spread, *shares,
    )
    (input_grad,) = call(
        finish, [((2, sub, feat), BF16)], [VMEM], rows * feat, size // 2, sums
    )
    (act,) = call(
        gather,
        [((2, 2, 2, sub, units), BF16)],
        [SMEM, SMEM] + [VMEM] * 4,
        rows * units // locals_, size // locals_,
        par, side, acts[0], *send(*acts[1:]),
    )
    return (
        act.reshape(rows // locals_, units),
        input_grad.reshape(rows // nodes, feat),
        weight_grad,
    )


def solution(mesh):
    body = functools.partial(shards, mesh.shape["local"], mesh.shape["node"])
    placed = (P(None, "local"), P("local", "node"), P(None, "node"), P("local", "node"))
    return jax.shard_map(
        lambda *args: body(*args),
        mesh=mesh,
        in_specs=placed,
        out_specs=(P("local", "node"), P("node", "local"), P("local", "node")),
        check_vma=False,
    )
```

time: 135 us -> 137 us (1.015)
  waiting for transfers between devices: 31.8 us -> 17 us
  starting transfers between devices: 61.3 us -> 73.7 us
  Pallas kernels: 9.72 us -> 12.1 us
    ppermute x5 -> x10, starting transfers between devices: 28.3 us -> 43.1 us  [the longest x1 15.5 us: shards(): far_tok = lax.ppermute(leave, ('node', 'local'), step)]
    all_to_all x2, waiting for transfers between devices: 8.28 us -> 0.42 us  [the longest x1 0.42 us: shards(): lax.all_to_all(both.reshape(nodes // 2, sub, feat), ('node', 'local'), 0,...]
    ppermute x5 -> x10, waiting for transfers between devices: 23.5 us -> 16.6 us  [the longest x3 13.7 us: send(): lax.ppermute(z, 'local', over_z)]
    all_to_all x2, starting transfers between devices: 31 us -> 28.7 us  [the longest x1 16.6 us: shards(): lax.all_to_all(both.reshape(nodes // 2, sub, feat), ('node', 'local'), 0,...]
    pallas_call x6 -> x7, Pallas kernels: 5.31 us -> 7.63 us  [call(): pl.pallas_call(kernel, out_shape=[jax.ShapeDtypeStruct(s, d) for s, d in...]
  transfers between devices with their start and end apart: 8 -> 13, of which waited for: 4 -> 4; matrix products, arithmetic and copies ran while one was open for 1% -> 2% of each run, Pallas kernels for 3% -> 4%
where the time goes in v7:
time: 137 us; the launch traced here: 134 us
  starting transfers between devices  73.7 us (54%)
  blocking collectives  26.4 us (19%)
  waiting for transfers between devices  17 us (12%)
  Pallas kernels  12.1 us (9%)
  local copies, waits for them, and re-layouts  3.24 us (2%)
    all_gather x1, blocking collectives, shards(): lax.all_gather(slope.reshape(4 * mine, units), 'local', axis=0, tiled=Tru...  26.4 us
    all_to_all x1, starting transfers between devices, shards(): lax.all_to_all(both.reshape(nodes // 2, sub, feat), ('node', 'local'), 0,...  16.6 us
    ppermute x1, starting transfers between devices, shards(): far_tok = lax.ppermute(leave, ('node', 'local'), step)  15.5 us
    ppermute x3, waiting for transfers between devices, send(): lax.ppermute(z, 'local', over_z)  13.7 us
    all_to_all x1, starting transfers between devices, shards(): lax.all_to_all(partial.reshape(2 * locals_, 2 * mine, units), ('node', 'l...  12 us
    ppermute x3, starting transfers between devices, send(): lax.ppermute(both, ('node', 'local'), over_both)  11.3 us
    ppermute x3, starting transfers between devices, send(): lax.ppermute(x, 'node', over_x)  8.61 us
    ppermute x3, starting transfers between devices, send(): lax.ppermute(z, 'local', over_z)  7.66 us
  transfers between devices with their start and end apart: 13, of which 4 were waited for; matrix products, arithmetic and copies ran while one was open for 2% of the time, Pallas kernels for 4%

profile of v7, /device:TPU:14, one launch (start us, length us, event | category | flops | bytes accessed | tf_op | source)
XLA Modules:
  0.0 134.5 jit_solution(14541143052333879550)
XLA Ops:
  0.6 4.5 %shard_map.67 = (bf16[384,384]{1,0:T(8,128)(2,1)}, bf16[2,2,8,2,2,16,384]{6,5,4,3,2,1,0:T(8,128)(2,1)}) custom-call(s32[1]{0:T(128)} %bitcast.3.start_ref, bf16[2,8,2,2,2,16,384]{6,5,4,3,2,1,0:T(8,128)(2,1)} %bitcast.24, bf16[384,384]{1,0:T(8,128)(2,1)} %codes_hbm.1, f32[3,384]{1,0:T(4,128)} %scales_hbm.1), custom_call_target="tpu_custom_call" | custom-call | flops 603979776 | bytes 3145728 | tf_op jit(solution)/shard_map/pallas_call | solution.py:210
  5.1 0.0 copy-start.3
  5.1 12.0 %all-to-all-start = ((bf16[32,64,384]{2,1,0:T(8,128)(2,1)}), bf16[32,64,384]{2,1,0:T(8,128)(2,1)S(1)}, u32[]{:S(2)}, u32[]{:S(2)}) async-start(bf16[32,64,384]{2,1,0:T(8,128)(2,1)} %bitcast.32), calls=%async_computation | async-start | bytes 3145728 | tf_op jit(solution)/shard_map/all_to_all | solution.py:233
  17.2 1.8 %dynamic-slice_bitcast_fusion = bf16[2,8,2,16,384]{4,3,2,1,0:T(8,128)(2,1)} fusion(bf16[2,8,2,2,2,16,384]{6,5,4,3,2,1,0:T(8,128)(2,1)} %bitcast.25, s32[]{:T(128)S(6)} %select_n.55, s32[]{:T(128)S(6)} %select_n.57), kind=kLoop, calls=%fused_computation | loop fusion | bytes 786440 | tf_op jit(solution)/shard_map/jit(dynamic_index_in_dim)/squeeze | solution.py:251
  19.0 15.5 %collective-permute-start.3 = (bf16[2,8,2,16,384]{4,3,2,1,0:T(8,128)(2,1)}, bf16[2,8,2,16,384]{4,3,2,1,0:T(8,128)(2,1)S(1)}, u32[]{:S(2)}, u32[]{:S(2)}) collective-permute-start(bf16[2,8,2,16,384]{4,3,2,1,0:T(8,128)(2,1)} %dynamic-slice_bitcast_fusion), channel_id=1, source_target_pairs={{0,776},{1,777},{2,778},{3,779},{4,780},{5,781},{6,782},{7,783},{8... | collective-permute-start | bytes 1179656 | tf_op jit(solution)/shard_map/ppermute | solution.py:252
  34.6 1.1 pad_maximum_fusion.2
  35.7 2.4 %collective-permute-start = (bf16[416,384]{1,0:T(8,128)(2,1)}, bf16[416,384]{1,0:T(8,128)(2,1)S(1)}, u32[]{:S(2)}, u32[]{:S(2)}) collective-permute-start(bf16[416,384]{1,0:T(8,128)(2,1)} %get-tuple-element.45), channel_id=1, source_target_pairs={{0,32},{16,48},{32,0},{48,16},{64,96},{80,112},{96,64},{112,80},{1... | collective-permute-start | bytes 958472 | tf_op jit(solution)/shard_map/ppermute | solution.py:205
  38.1 1.9 %collective-permute-start.1 = (bf16[416,384]{1,0:T(8,128)(2,1)}, bf16[416,384]{1,0:T(8,128)(2,1)S(1)}, u32[]{:S(2)}, u32[]{:S(2)}) collective-permute-start(bf16[416,384]{1,0:T(8,128)(2,1)} %get-tuple-element.44), channel_id=1, source_target_pairs={{0,8},{1,9},{2,10},{3,11},{4,12},{5,13},{6,14},{7,15},{8,0},{9,1},... | collective-permute-start | bytes 958472 | tf_op jit(solution)/shard_map/ppermute | solution.py:206
  40.0 4.9 %collective-permute-start.2 = (bf16[416,384]{1,0:T(8,128)(2,1)}, bf16[416,384]{1,0:T(8,128)(2,1)S(1)}, u32[]{:S(2)}, u32[]{:S(2)}) collective-permute-start(bf16[416,384]{1,0:T(8,128)(2,1)} %get-tuple-element.43), channel_id=1, source_target_pairs={{0,40},{1,41},{2,42},{3,43},{4,44},{5,45},{6,46},{7,47},{8,32},{9,... | collective-permute-start | bytes 958472 | tf_op jit(solution)/shard_map/ppermute | solution.py:207
  44.9 2.8 %collective-permute-done.refs_1_ = bf16[416,384]{1,0:T(8,128)(2,1)S(1)} collective-permute-done((bf16[416,384]{1,0:T(8,128)(2,1)}, bf16[416,384]{1,0:T(8,128)(2,1)S(1)}, u32[]{:S(2)}, u32[]{:S(2)}) %collective-permute-start) | collective-permute-done | bytes 319520 | tf_op jit(solution)/shard_map/ppermute | solution.py:205
  47.8 13.7 %collective-permute-done.1.refs_2_ = bf16[416,384]{1,0:T(8,128)(2,1)S(1)} collective-permute-done((bf16[416,384]{1,0:T(8,128)(2,1)}, bf16[416,384]{1,0:T(8,128)(2,1)S(1)}, u32[]{:S(2)}, u32[]{:S(2)}) %collective-permute-start.1) | collective-permute-done | bytes 319520 | tf_op jit(solution)/shard_map/ppermute | solution.py:206
  61.4 0.4 shard_map.68
  61.8 0.0 copy-start.1
  61.8 26.4 %all_gather.3 = bf16[1024,384]{1,0:T(8,128)(2,1)S(1)} all-gather(bf16[128,384]{1,0:T(8,128)(2,1)S(1)} %bitcast.31), channel_id=1, replica_groups={{0,1,2,3,4,5,6,7},{8,9,10,11,12,13,14,15},{16,17,18,19,20,21,22,23},{24..., dimensions={0}, use_global_device_ids=true | all-gather | bytes 884736 | tf_op jit(solution)/shard_map/all_gather | solution.py:262
  88.3 0.7 shard_map.69
  88.9 1.9 %collective-permute-start.4 = (bf16[2,256,384]{2,1,0:T(8,128)(2,1)S(1)}, bf16[2,256,384]{2,1,0:T(8,128)(2,1)S(1)}, u32[]{:S(2)}, u32[]{:S(2)}) collective-permute-start(bf16[2,256,384]{2,1,0:T(8,128)(2,1)S(1)} %shard_map.69), channel_id=1, source_target_pairs={{0,16},{16,0},{32,48},{48,32},{64,80},{80,64},{96,112},{112,96},{1... | collective-permute-start | bytes 1179656 | tf_op jit(solution)/shard_map/ppermute | solution.py:273
  90.9 1.5 %shard_map.73 = (bf16[384,384]{1,0:T(8,128)(2,1)}, bf16[384,384]{1,0:T(8,128)(2,1)}, bf16[384,384]{1,0:T(8,128)(2,1)}) custom-call(s32[1]{0:T(128)} %bitcast.par_ref, s32[1]{0:T(128)} %bitcast.1.side_ref, bf16[2,8,2,2,2,16,384]{6,5,4,3,2,1,0:T(8,128)(2,1)S(1)} %bitcast.26, bf16[2,8,2,16,384]{4,3,2,1,0:T(8,128)(2,1)S(1)} %collective-permute-done.3.far_tok_ref, ...), custom_call_target="tpu_custom_call" | custom-call | flops 301989888 | bytes 1572864 | tf_op jit(solution)/shard_map/pallas_call | solution.py:20
  92.4 3.2 %collective-permute-start.8 = (bf16[384,384]{1,0:T(8,128)(2,1)}, bf16[384,384]{1,0:T(8,128)(2,1)S(1)}, u32[]{:S(2)}, u32[]{:S(2)}) collective-permute-start(bf16[384,384]{1,0:T(8,128)(2,1)} %get-tuple-element.40), channel_id=1, source_target_pairs={{0,32},{16,48},{32,0},{48,16},{64,96},{80,112},{96,64},{112,80},{1... | collective-permute-start | bytes 884744 | tf_op jit(solution)/shard_map/ppermute | solution.py:205
  95.6 2.4 %collective-permute-start.9 = (bf16[384,384]{1,0:T(8,128)(2,1)}, bf16[384,384]{1,0:T(8,128)(2,1)}, u32[]{:S(2)}, u32[]{:S(2)}) collective-permute-start(bf16[384,384]{1,0:T(8,128)(2,1)} %get-tuple-element.41), channel_id=1, source_target_pairs={{0,8},{1,9},{2,10},{3,11},{4,12},{5,13},{6,14},{7,15},{8,0},{9,1},... | collective-permute-start | bytes 884744 | tf_op jit(solution)/shard_map/ppermute | solution.py:206
  97.9 3.7 %collective-permute-start.10 = (bf16[384,384]{1,0:T(8,128)(2,1)}, bf16[384,384]{1,0:T(8,128)(2,1)}, u32[]{:S(2)}, u32[]{:S(2)}) collective-permute-start(bf16[384,384]{1,0:T(8,128)(2,1)} %get-tuple-element.42), channel_id=1, source_target_pairs={{0,40},{1,41},{2,42},{3,43},{4,44},{5,45},{6,46},{7,47},{8,32},{9,... | collective-permute-start | bytes 884744 | tf_op jit(solution)/shard_map/ppermute | solution.py:207
  101.6 1.4 %shard_map.70 = bf16[2,2,2,4,16,384]{5,4,3,2,1,0:T(8,128)(2,1)} custom-call(s32[1]{0:T(128)} %bitcast.2.core_ref, s32[1]{0:T(128)} %bitcast.1.side_ref, bf16[8,2,2,2,16,384]{5,4,3,2,1,0:T(8,128)(2,1)S(1)} %bitcast.21, bf16[384,384]{1,0:T(8,128)(2,1)S(1)} %copy-done, bf16[416,384]{1,0:T(8,128)(2,1)S(1)} %collective-permute-done.refs_1_, ...), custom_call_target="tpu_custom_call" | custom-call | flops 301989888 | bytes 1572864 | tf_op jit(solution)/shard_map/pallas_call | solution.py:20
  103.1 16.6 %all-to-all-start.1 = ((bf16[32,16,384]{2,1,0:T(8,128)(2,1)}), bf16[32,16,384]{2,1,0:T(8,128)(2,1)S(1)}, u32[]{:S(2)}, u32[]{:S(2)}) async-start(bf16[32,16,384]{2,1,0:T(8,128)(2,1)} %bitcast.15), calls=%async_computation.1 | async-start | bytes 786432 | tf_op jit(solution)/shard_map/all_to_all | solution.py:301
  119.7 3.0 %collective-permute-start.5 = (bf16[32,384]{1,0:T(8,128)(2,1)S(1)}, bf16[32,384]{1,0:T(8,128)(2,1)S(1)}, u32[]{:S(2)}, u32[]{:S(2)}) collective-permute-start(bf16[32,384]{1,0:T(8,128)(2,1)S(1)} %get-tuple-element.35), channel_id=1, source_target_pairs={{0,32},{16,48},{32,0},{48,16},{64,96},{80,112},{96,64},{112,80},{1... | collective-permute-start | bytes 73736 | tf_op jit(solution)/shard_map/ppermute | solution.py:205
  122.7 3.4 %collective-permute-start.6 = (bf16[32,384]{1,0:T(8,128)(2,1)S(1)}, bf16[32,384]{1,0:T(8,128)(2,1)S(1)}, u32[]{:S(2)}, u32[]{:S(2)}) collective-permute-start(bf16[32,384]{1,0:T(8,128)(2,1)S(1)} %get-tuple-element.36), channel_id=1, source_target_pairs={{0,8},{1,9},{2,10},{3,11},{4,12},{5,13},{6,14},{7,15},{8,0},{9,1},... | collective-permute-start | bytes 73736 | tf_op jit(solution)/shard_map/ppermute | solution.py:206
  126.1 2.8 %collective-permute-start.7 = (bf16[32,384]{1,0:T(8,128)(2,1)S(1)}, bf16[32,384]{1,0:T(8,128)(2,1)S(1)}, u32[]{:S(2)}, u32[]{:S(2)}) collective-permute-start(bf16[32,384]{1,0:T(8,128)(2,1)S(1)} %get-tuple-element.37), channel_id=1, source_target_pairs={{0,40},{1,41},{2,42},{3,43},{4,44},{5,45},{6,46},{7,47},{8,32},{9,... | collective-permute-start | bytes 73736 | tf_op jit(solution)/shard_map/ppermute | solution.py:207
  128.9 0.0 copy-start.2
  129.0 1.4 %copy-done.2 = bf16[2048,384]{1,0:T(8,128)(2,1)S(1)} copy-done((bf16[2048,384]{1,0:T(8,128)(2,1)S(1)}, bf16[2048,384]{1,0:T(8,128)(2,1)}, u32[]{:S(2)}) %copy-start.2) | copy-done | bytes 1572888
  130.4 2.3 %shard_map.74 = f32[384,384]{1,0:T(8,128)} custom-call(s32[1]{0:T(128)} %bitcast.par_ref, s32[1]{0:T(128)} %bitcast.1.side_ref, bf16[2,8,2,2,2,16,384]{6,5,4,3,2,1,0:T(8,128)(2,1)S(1)} %bitcast.27, bf16[8,2,2,2,16,384]{5,4,3,2,1,0:T(8,128)(2,1)S(1)} %bitcast.22, bf16[384,384]{1,0:T(8,128)(2,1)S(1)} %collective-permute-done.8.x_ref, ...), custom_call_target="tpu_custom_call" | custom-call | flops 6039797760 | bytes 1572864 | tf_op jit(solution)/shard_map/pallas_call | solution.py:20
  132.7 0.1 collective-permute-done.7.both_ref
  132.7 0.7 shard_map.71
  133.4 0.4 all-to-all-done.1
  133.8 0.7 shard_map.72
  (14 shorter events, 0.1 us)
Async XLA Ops:
  5.1 29.5 %copy-start.3 = (bf16[128,384]{1,0:T(8,128)(2,1)S(1)}, bf16[128,384]{1,0:T(8,128)(2,1)}, u32[]{:S(2)}) copy-start(bf16[128,384]{1,0:T(8,128)(2,1)} %param.7) | copy-start | bytes 294916
  5.1 29.5 %copy-start = (bf16[384,384]{1,0:T(8,128)(2,1)S(1)}, bf16[384,384]{1,0:T(8,128)(2,1)}, u32[]{:S(2)}) copy-start(bf16[384,384]{1,0:T(8,128)(2,1)} %get-tuple-element.24.refs_0_) | copy-start | bytes 884740
  5.1 56.3 %all-to-all-start = ((bf16[32,64,384]{2,1,0:T(8,128)(2,1)}), bf16[32,64,384]{2,1,0:T(8,128)(2,1)S(1)}, u32[]{:S(2)}, u32[]{:S(2)}) async-start(bf16[32,64,384]{2,1,0:T(8,128)(2,1)} %bitcast.32), calls=%async_computation | async-start | bytes 3145728 | tf_op jit(solution)/shard_map/all_to_all | solution.py:233
  19.0 42.4 %collective-permute-start.3 = (bf16[2,8,2,16,384]{4,3,2,1,0:T(8,128)(2,1)}, bf16[2,8,2,16,384]{4,3,2,1,0:T(8,128)(2,1)S(1)}, u32[]{:S(2)}, u32[]{:S(2)}) collective-permute-start(bf16[2,8,2,16,384]{4,3,2,1,0:T(8,128)(2,1)} %dynamic-slice_bitcast_fusion), channel_id=1, source_target_pairs={{0,776},{1,777},{2,778},{3,779},{4,780},{5,781},{6,782},{7,783},{8... | collective-permute-start | bytes 1179656 | tf_op jit(solution)/shard_map/ppermute | solution.py:252
  35.7 12.1 %collective-permute-start = (bf16[416,384]{1,0:T(8,128)(2,1)}, bf16[416,384]{1,0:T(8,128)(2,1)S(1)}, u32[]{:S(2)}, u32[]{:S(2)}) collective-permute-start(bf16[416,384]{1,0:T(8,128)(2,1)} %get-tuple-element.45), channel_id=1, source_target_pairs={{0,32},{16,48},{32,0},{48,16},{64,96},{80,112},{96,64},{112,80},{1... | collective-permute-start | bytes 958472 | tf_op jit(solution)/shard_map/ppermute | solution.py:205
  38.1 23.3 %collective-permute-start.1 = (bf16[416,384]{1,0:T(8,128)(2,1)}, bf16[416,384]{1,0:T(8,128)(2,1)S(1)}, u32[]{:S(2)}, u32[]{:S(2)}) collective-permute-start(bf16[416,384]{1,0:T(8,128)(2,1)} %get-tuple-element.44), channel_id=1, source_target_pairs={{0,8},{1,9},{2,10},{3,11},{4,12},{5,13},{6,14},{7,15},{8,0},{9,1},... | collective-permute-start | bytes 958472 | tf_op jit(solution)/shard_map/ppermute | solution.py:206
  40.0 21.4 %collective-permute-start.2 = (bf16[416,384]{1,0:T(8,128)(2,1)}, bf16[416,384]{1,0:T(8,128)(2,1)S(1)}, u32[]{:S(2)}, u32[]{:S(2)}) collective-permute-start(bf16[416,384]{1,0:T(8,128)(2,1)} %get-tuple-element.43), channel_id=1, source_target_pairs={{0,40},{1,41},{2,42},{3,43},{4,44},{5,45},{6,46},{7,47},{8,32},{9,... | collective-permute-start | bytes 958472 | tf_op jit(solution)/shard_map/ppermute | solution.py:207
  61.8 29.0 %copy-start.1 = (bf16[2048,384]{1,0:T(8,128)(2,1)S(1)}, bf16[2048,384]{1,0:T(8,128)(2,1)}, u32[]{:S(2)}) copy-start(bf16[2048,384]{1,0:T(8,128)(2,1)} %param.4) | copy-start | bytes 4718596
  88.9 12.7 %collective-permute-start.4 = (bf16[2,256,384]{2,1,0:T(8,128)(2,1)S(1)}, bf16[2,256,384]{2,1,0:T(8,128)(2,1)S(1)}, u32[]{:S(2)}, u32[]{:S(2)}) collective-permute-start(bf16[2,256,384]{2,1,0:T(8,128)(2,1)S(1)} %shard_map.69), channel_id=1, source_target_pairs={{0,16},{16,0},{32,48},{48,32},{64,80},{80,64},{96,112},{112,96},{1... | collective-permute-start | bytes 1179656 | tf_op jit(solution)/shard_map/ppermute | solution.py:273
  92.4 33.7 %collective-permute-start.8 = (bf16[384,384]{1,0:T(8,128)(2,1)}, bf16[384,384]{1,0:T(8,128)(2,1)S(1)}, u32[]{:S(2)}, u32[]{:S(2)}) collective-permute-start(bf16[384,384]{1,0:T(8,128)(2,1)} %get-tuple-element.40), channel_id=1, source_target_pairs={{0,32},{16,48},{32,0},{48,16},{64,96},{80,112},{96,64},{112,80},{1... | collective-permute-start | bytes 884744 | tf_op jit(solution)/shard_map/ppermute | solution.py:205
  95.6 33.4 %collective-permute-start.9 = (bf16[384,384]{1,0:T(8,128)(2,1)}, bf16[384,384]{1,0:T(8,128)(2,1)}, u32[]{:S(2)}, u32[]{:S(2)}) collective-permute-start(bf16[384,384]{1,0:T(8,128)(2,1)} %get-tuple-element.41), channel_id=1, source_target_pairs={{0,8},{1,9},{2,10},{3,11},{4,12},{5,13},{6,14},{7,15},{8,0},{9,1},... | collective-permute-start | bytes 884744 | tf_op jit(solution)/shard_map/ppermute | solution.py:206
  97.9 31.0 %collective-permute-start.10 = (bf16[384,384]{1,0:T(8,128)(2,1)}, bf16[384,384]{1,0:T(8,128)(2,1)}, u32[]{:S(2)}, u32[]{:S(2)}) collective-permute-start(bf16[384,384]{1,0:T(8,128)(2,1)} %get-tuple-element.42), channel_id=1, source_target_pairs={{0,40},{1,41},{2,42},{3,43},{4,44},{5,45},{6,46},{7,47},{8,32},{9,... | collective-permute-start | bytes 884744 | tf_op jit(solution)/shard_map/ppermute | solution.py:207
  103.1 30.7 %all-to-all-start.1 = ((bf16[32,16,384]{2,1,0:T(8,128)(2,1)}), bf16[32,16,384]{2,1,0:T(8,128)(2,1)S(1)}, u32[]{:S(2)}, u32[]{:S(2)}) async-start(bf16[32,16,384]{2,1,0:T(8,128)(2,1)} %bitcast.15), calls=%async_computation.1 | async-start | bytes 786432 | tf_op jit(solution)/shard_map/all_to_all | solution.py:301
  119.7 13.0 %collective-permute-start.5 = (bf16[32,384]{1,0:T(8,128)(2,1)S(1)}, bf16[32,384]{1,0:T(8,128)(2,1)S(1)}, u32[]{:S(2)}, u32[]{:S(2)}) collective-permute-start(bf16[32,384]{1,0:T(8,128)(2,1)S(1)} %get-tuple-element.35), channel_id=1, source_target_pairs={{0,32},{16,48},{32,0},{48,16},{64,96},{80,112},{96,64},{112,80},{1... | collective-permute-start | bytes 73736 | tf_op jit(solution)/shard_map/ppermute | solution.py:205
  122.7 10.0 %collective-permute-start.6 = (bf16[32,384]{1,0:T(8,128)(2,1)S(1)}, bf16[32,384]{1,0:T(8,128)(2,1)S(1)}, u32[]{:S(2)}, u32[]{:S(2)}) collective-permute-start(bf16[32,384]{1,0:T(8,128)(2,1)S(1)} %get-tuple-element.36), channel_id=1, source_target_pairs={{0,8},{1,9},{2,10},{3,11},{4,12},{5,13},{6,14},{7,15},{8,0},{9,1},... | collective-permute-start | bytes 73736 | tf_op jit(solution)/shard_map/ppermute | solution.py:206
  126.1 6.6 %collective-permute-start.7 = (bf16[32,384]{1,0:T(8,128)(2,1)S(1)}, bf16[32,384]{1,0:T(8,128)(2,1)S(1)}, u32[]{:S(2)}, u32[]{:S(2)}) collective-permute-start(bf16[32,384]{1,0:T(8,128)(2,1)S(1)} %get-tuple-element.37), channel_id=1, source_target_pairs={{0,40},{1,41},{2,42},{3,43},{4,44},{5,45},{6,46},{7,47},{8,32},{9,... | collective-permute-start | bytes 73736 | tf_op jit(solution)/shard_map/ppermute | solution.py:207
  128.9 1.4 %copy-start.2 = (bf16[2048,384]{1,0:T(8,128)(2,1)S(1)}, bf16[2048,384]{1,0:T(8,128)(2,1)}, u32[]{:S(2)}) copy-start(bf16[2048,384]{1,0:T(8,128)(2,1)} %param.4) | copy-start | bytes 4718596

commit v8 on v7

--- a/solution.py
+++ b/solution.py
@@ -91,7 +91,8 @@
         acts[i][...] = (0.5 * pre * (1.0 + tanh)).astype(BF16)
         inner = ROOT * (1.0 + 3.0 * 0.044715 * square)
         grad = 0.5 * (1.0 + tanh) + 0.5 * pre * (1.0 - tanh * tanh) * inner
-        slope_ref[unit, t] = (cot * grad).astype(BF16)
+        slope = (cot * grad).astype(BF16)
+        slope_ref[:, unit, t] = jnp.broadcast_to(slope[None], (slope_ref.shape[0],) + slope.shape)
 
 
 def gather(par_ref, side_ref, own_ref, x_ref, z_ref, both_ref, out_ref):
@@ -249,19 +250,28 @@
         for n, l in spots
     ]
     leave = lax.dynamic_index_in_dim(lax.dynamic_index_in_dim(tok, p, 2, False), 1 - z, 3, False)
-    far_tok = lax.ppermute(leave, ("node", "local"), step)
-    got, far, far_tok = lax.optimization_barrier((got, far, far_tok))
+    got, far = lax.optimization_barrier((got, far))
     *acts, slope = call(
         functools.partial(activate, feat),
-        [((mine, units), BF16)] * 4 + [((2, 2, mine, units), BF16)],
+        [((mine, units), BF16)] * 4 + [((ys, 2, 2, mine, units), BF16)],
         [SMEM, SMEM] + [VMEM] * 5,
         rows * units * 4, size,
         par, side, got, cot, *far,
     )
     lines = [list(range(t * ys, (t + 1) * ys)) for t in range(2)]
-    spread = lax.all_gather(
-        slope.reshape(4 * mine, units), "local", axis=0, tiled=True, axis_index_groups=lines
+    spread = lax.all_to_all(
+        slope.reshape(ys, 4 * mine, units), "local", 0, 0, axis_index_groups=lines, tiled=True
     ).reshape(ys, 2, 2, 2, sub, units)
+    acts, leave = lax.optimization_barrier((acts, leave))
+    far_tok = lax.ppermute(leave, ("node", "local"), step)
+    (act,) = call(
+        gather,
+        [((2, 2, 2, sub, units), BF16)],
+        [SMEM, SMEM] + [VMEM] * 4,
+        rows * units // locals_, size // locals_,
+        par, side, acts[0], *send(*acts[1:]),
+    )
+    spread, far_tok, act = lax.optimization_barrier((spread, far_tok, act))
     weights = (weight,) + tuple(far)
     (other,) = call(
         back_other,
@@ -286,7 +296,6 @@
         flops // 2, size,
         core, side, spread, *weights, other,
     )
-    both, acts = lax.optimization_barrier((both, acts))
     groups = [
         [
             moved(per * (ys * t + y) + low, k * ys + own)
@@ -312,13 +321,6 @@
     (input_grad,) = call(
         finish, [((2, sub, feat), BF16)], [VMEM], rows * feat, size // 2, sums
     )
-    (act,) = call(
-        gather,
-        [((2, 2, 2, sub, units), BF16)],
-        [SMEM, SMEM] + [VMEM] * 4,
-        rows * units // locals_, size // locals_,
-        par, side, acts[0], *send(*acts[1:]),
-    )
     return (
         act.reshape(rows // locals_, units),
         input_grad.reshape(rows // nodes, feat),

time: 137 us -> 138 us (level)
  waiting for transfers between devices: 17 us -> 45.2 us
  blocking collectives: 26.4 us -> 0 us
    all_gather x1 -> x0, blocking collectives: 26.4 us -> none  [shards(): lax.all_gather(slope.reshape(4 * mine, units), 'local', axis=0, tiled=Tru...]
    ppermute x3, waiting for transfers between devices: 2.83 us -> 19.9 us  [send(): lax.ppermute(x, 'node', over_x)]
    ppermute x3, waiting for transfers between devices: 0.06 us -> 14.3 us  [send(): lax.ppermute(both, ('node', 'local'), over_both)]
    ppermute x3, waiting for transfers between devices: 13.7 us -> 0.4 us  [send(): lax.ppermute(z, 'local', over_z)]
    all_to_all x1, waiting for transfers between devices: 0.42 us -> 10.6 us  [shards(): lax.all_to_all(both.reshape(nodes // 2, sub, feat), ('node', 'local'), 0,...]
    all_to_all x0 -> x1, starting transfers between devices: none -> 4.59 us  [shards(): lax.all_to_all(slope.reshape(ys, 4 * mine, units), 'local', 0, 0, axis_in...]
    all_to_all x1, starting transfers between devices: 16.6 us -> 13.9 us  [shards(): lax.all_to_all(both.reshape(nodes // 2, sub, feat), ('node', 'local'), 0,...]
    ppermute x1, starting transfers between devices: 15.5 us -> 13.3 us  [shards(): far_tok = lax.ppermute(leave, ('node', 'local'), step)]
  transfers between devices with their start and end apart: 13 -> 14, of which waited for: 4 -> 5; matrix products, arithmetic and copies ran while one was open for 2% -> 1% of each run, Pallas kernels for 4% -> 4%
where the time goes in v8:
time: 138 us; the launch traced here: 136 us
  starting transfers between devices  74 us (54%)
  waiting for transfers between devices  45.2 us (33%)
  Pallas kernels  12.1 us (9%)
  local copies, waits for them, and re-layouts  3.36 us (2%)
    ppermute x3, waiting for transfers between devices, send(): lax.ppermute(x, 'node', over_x)  19.9 us
    ppermute x3, waiting for transfers between devices, send(): lax.ppermute(both, ('node', 'local'), over_both)  14.3 us
    all_to_all x1, starting transfers between devices, shards(): lax.all_to_all(both.reshape(nodes // 2, sub, feat), ('node', 'local'), 0,...  13.9 us
    ppermute x1, starting transfers between devices, shards(): far_tok = lax.ppermute(leave, ('node', 'local'), step)  13.3 us
    all_to_all x1, starting transfers between devices, shards(): lax.all_to_all(partial.reshape(2 * locals_, 2 * mine, units), ('node', 'l...  12 us
    all_to_all x1, waiting for transfers between devices, shards(): lax.all_to_all(both.reshape(nodes // 2, sub, feat), ('node', 'local'), 0,...  10.6 us
    ppermute x3, starting transfers between devices, send(): lax.ppermute(both, ('node', 'local'), over_both)  10.1 us
    ppermute x3, starting transfers between devices, send(): lax.ppermute(x, 'node', over_x)  9.18 us
  transfers between devices with their start and end apart: 14, of which 5 were waited for; matrix products, arithmetic and copies ran while one was open for 1% of the time, Pallas kernels for 4%

profile of v8, /device:TPU:14, one launch (start us, length us, event | category | flops | bytes accessed | tf_op | source)
XLA Modules:
  0.0 135.7 jit_solution(6518825947910363268)
XLA Ops:
  0.6 4.4 %shard_map.67 = (bf16[384,384]{1,0:T(8,128)(2,1)}, bf16[2,2,8,2,2,16,384]{6,5,4,3,2,1,0:T(8,128)(2,1)}) custom-call(s32[1]{0:T(128)} %bitcast.2.start_ref, bf16[2,8,2,2,2,16,384]{6,5,4,3,2,1,0:T(8,128)(2,1)} %bitcast.24, bf16[384,384]{1,0:T(8,128)(2,1)} %codes_hbm.1, f32[3,384]{1,0:T(4,128)} %scales_hbm.1), custom_call_target="tpu_custom_call" | custom-call | flops 603979776 | bytes 3145728 | tf_op jit(solution)/shard_map/pallas_call | solution.py:211
  5.1 12.0 %all-to-all-start = ((bf16[32,64,384]{2,1,0:T(8,128)(2,1)}), bf16[32,64,384]{2,1,0:T(8,128)(2,1)S(1)}, u32[]{:S(2)}, u32[]{:S(2)}) async-start(bf16[32,64,384]{2,1,0:T(8,128)(2,1)} %bitcast.32), calls=%async_computation | async-start | bytes 3145728 | tf_op jit(solution)/shard_map/all_to_all | solution.py:234
  17.3 0.1 pad_maximum_fusion.2
  17.4 2.1 %collective-permute-start = (bf16[416,384]{1,0:T(8,128)(2,1)S(1)}, bf16[416,384]{1,0:T(8,128)(2,1)S(1)}, u32[]{:S(2)}, u32[]{:S(2)}) collective-permute-start(bf16[416,384]{1,0:T(8,128)(2,1)S(1)} %get-tuple-element.49), channel_id=1, source_target_pairs={{0,32},{16,48},{32,0},{48,16},{64,96},{80,112},{96,64},{112,80},{1... | collective-permute-start | bytes 958472 | tf_op jit(solution)/shard_map/ppermute | solution.py:206
  19.5 3.7 %collective-permute-start.1 = (bf16[416,384]{1,0:T(8,128)(2,1)S(1)}, bf16[416,384]{1,0:T(8,128)(2,1)S(1)}, u32[]{:S(2)}, u32[]{:S(2)}) collective-permute-start(bf16[416,384]{1,0:T(8,128)(2,1)S(1)} %get-tuple-element.48), channel_id=1, source_target_pairs={{0,8},{1,9},{2,10},{3,11},{4,12},{5,13},{6,14},{7,15},{8,0},{9,1},... | collective-permute-start | bytes 958472 | tf_op jit(solution)/shard_map/ppermute | solution.py:207
  23.2 3.4 %collective-permute-start.2 = (bf16[416,384]{1,0:T(8,128)(2,1)S(1)}, bf16[416,384]{1,0:T(8,128)(2,1)S(1)}, u32[]{:S(2)}, u32[]{:S(2)}) collective-permute-start(bf16[416,384]{1,0:T(8,128)(2,1)S(1)} %get-tuple-element.47), channel_id=1, source_target_pairs={{0,40},{1,41},{2,42},{3,43},{4,44},{5,45},{6,46},{7,47},{8,32},{9,... | collective-permute-start | bytes 958472 | tf_op jit(solution)/shard_map/ppermute | solution.py:208
  26.6 19.9 %collective-permute-done.refs_1_ = bf16[416,384]{1,0:T(8,128)(2,1)S(1)} collective-permute-done((bf16[416,384]{1,0:T(8,128)(2,1)S(1)}, bf16[416,384]{1,0:T(8,128)(2,1)S(1)}, u32[]{:S(2)}, u32[]{:S(2)}) %collective-permute-start) | collective-permute-done | bytes 319520 | tf_op jit(solution)/shard_map/ppermute | solution.py:206
  46.5 11.5 %collective-permute-done.2.refs_3_ = bf16[416,384]{1,0:T(8,128)(2,1)S(1)} collective-permute-done((bf16[416,384]{1,0:T(8,128)(2,1)S(1)}, bf16[416,384]{1,0:T(8,128)(2,1)S(1)}, u32[]{:S(2)}, u32[]{:S(2)}) %collective-permute-start.2) | collective-permute-done | bytes 319520 | tf_op jit(solution)/shard_map/ppermute | solution.py:208
  58.0 0.4 shard_map.68
  58.3 0.9 copy-done.3
  59.2 4.6 %all-to-all-start.1 = ((bf16[8,128,384]{2,1,0:T(8,128)(2,1)}), bf16[8,128,384]{2,1,0:T(8,128)(2,1)S(1)}, u32[]{:S(2)}, u32[]{:S(2)}) async-start(bf16[8,128,384]{2,1,0:T(8,128)(2,1)} %bitcast.29), calls=%async_computation.1 | async-start | bytes 1572864 | tf_op jit(solution)/shard_map/all_to_all | solution.py:262
  63.8 1.0 dynamic-slice_bitcast_fusion
  64.9 13.3 %collective-permute-start.3 = (bf16[2,8,2,16,384]{4,3,2,1,0:T(8,128)(2,1)S(1)}, bf16[2,8,2,16,384]{4,3,2,1,0:T(8,128)(2,1)S(1)}, u32[]{:S(2)}, u32[]{:S(2)}) collective-permute-start(bf16[2,8,2,16,384]{4,3,2,1,0:T(8,128)(2,1)S(1)} %dynamic-slice_bitcast_fusion), channel_id=1, source_target_pairs={{0,776},{1,777},{2,778},{3,779},{4,780},{5,781},{6,782},{7,783},{8... | collective-permute-start | bytes 1179656 | tf_op jit(solution)/shard_map/ppermute | solution.py:266
  78.1 4.6 %collective-permute-start.4 = (bf16[32,384]{1,0:T(8,128)(2,1)S(1)}, bf16[32,384]{1,0:T(8,128)(2,1)S(1)}, u32[]{:S(2)}, u32[]{:S(2)}) collective-permute-start(bf16[32,384]{1,0:T(8,128)(2,1)S(1)} %get-tuple-element.38), channel_id=1, source_target_pairs={{0,32},{16,48},{32,0},{48,16},{64,96},{80,112},{96,64},{112,80},{1... | collective-permute-start | bytes 73736 | tf_op jit(solution)/shard_map/ppermute | solution.py:206
  82.7 1.9 %collective-permute-start.5 = (bf16[32,384]{1,0:T(8,128)(2,1)S(1)}, bf16[32,384]{1,0:T(8,128)(2,1)S(1)}, u32[]{:S(2)}, u32[]{:S(2)}) collective-permute-start(bf16[32,384]{1,0:T(8,128)(2,1)S(1)} %get-tuple-element.39), channel_id=1, source_target_pairs={{0,8},{1,9},{2,10},{3,11},{4,12},{5,13},{6,14},{7,15},{8,0},{9,1},... | collective-permute-start | bytes 73736 | tf_op jit(solution)/shard_map/ppermute | solution.py:207
  84.6 3.4 %collective-permute-start.6 = (bf16[32,384]{1,0:T(8,128)(2,1)S(1)}, bf16[32,384]{1,0:T(8,128)(2,1)S(1)}, u32[]{:S(2)}, u32[]{:S(2)}) collective-permute-start(bf16[32,384]{1,0:T(8,128)(2,1)S(1)} %get-tuple-element.40), channel_id=1, source_target_pairs={{0,40},{1,41},{2,42},{3,43},{4,44},{5,45},{6,46},{7,47},{8,32},{9,... | collective-permute-start | bytes 73736 | tf_op jit(solution)/shard_map/ppermute | solution.py:208
  88.0 0.4 collective-permute-done.5.z_ref
  88.4 2.8 %collective-permute-done.6.both_ref = bf16[32,384]{1,0:T(8,128)(2,1)S(1)} collective-permute-done((bf16[32,384]{1,0:T(8,128)(2,1)S(1)}, bf16[32,384]{1,0:T(8,128)(2,1)S(1)}, u32[]{:S(2)}, u32[]{:S(2)}) %collective-permute-start.6) | collective-permute-done | bytes 24608 | tf_op jit(solution)/shard_map/ppermute | solution.py:208
  91.3 0.7 shard_map.69
  91.9 0.7 shard_map.70
  92.6 1.9 %collective-permute-start.7 = (bf16[2,256,384]{2,1,0:T(8,128)(2,1)S(1)}, bf16[2,256,384]{2,1,0:T(8,128)(2,1)S(1)}, u32[]{:S(2)}, u32[]{:S(2)}) collective-permute-start(bf16[2,256,384]{2,1,0:T(8,128)(2,1)S(1)} %shard_map.70), channel_id=1, source_target_pairs={{0,16},{16,0},{32,48},{48,32},{64,80},{80,64},{96,112},{112,96},{1... | collective-permute-start | bytes 1179656 | tf_op jit(solution)/shard_map/ppermute | solution.py:283
  94.5 1.5 %shard_map.73 = (bf16[384,384]{1,0:T(8,128)(2,1)}, bf16[384,384]{1,0:T(8,128)(2,1)}, bf16[384,384]{1,0:T(8,128)(2,1)S(1)}) custom-call(s32[1]{0:T(128)} %bitcast.par_ref, s32[1]{0:T(128)} %bitcast.1.side_ref, bf16[2,8,2,2,2,16,384]{6,5,4,3,2,1,0:T(8,128)(2,1)S(1)} %bitcast.26, bf16[2,8,2,16,384]{4,3,2,1,0:T(8,128)(2,1)S(1)} %collective-permute-done.3.far_tok_ref, ...), custom_call_target="tpu_custom_call" | custom-call | flops 301989888 | bytes 1572864 | tf_op jit(solution)/shard_map/pallas_call | solution.py:20
  96.1 2.5 %collective-permute-start.8 = (bf16[384,384]{1,0:T(8,128)(2,1)}, bf16[384,384]{1,0:T(8,128)(2,1)S(1)}, u32[]{:S(2)}, u32[]{:S(2)}) collective-permute-start(bf16[384,384]{1,0:T(8,128)(2,1)} %get-tuple-element.44), channel_id=1, source_target_pairs={{0,32},{16,48},{32,0},{48,16},{64,96},{80,112},{96,64},{112,80},{1... | collective-permute-start | bytes 884744 | tf_op jit(solution)/shard_map/ppermute | solution.py:206
  98.5 3.4 %collective-permute-start.9 = (bf16[384,384]{1,0:T(8,128)(2,1)}, bf16[384,384]{1,0:T(8,128)(2,1)}, u32[]{:S(2)}, u32[]{:S(2)}) collective-permute-start(bf16[384,384]{1,0:T(8,128)(2,1)} %get-tuple-element.45), channel_id=1, source_target_pairs={{0,8},{1,9},{2,10},{3,11},{4,12},{5,13},{6,14},{7,15},{8,0},{9,1},... | collective-permute-start | bytes 884744 | tf_op jit(solution)/shard_map/ppermute | solution.py:207
  101.9 3.4 %collective-permute-start.10 = (bf16[384,384]{1,0:T(8,128)(2,1)S(1)}, bf16[384,384]{1,0:T(8,128)(2,1)}, u32[]{:S(2)}, u32[]{:S(2)}) collective-permute-start(bf16[384,384]{1,0:T(8,128)(2,1)S(1)} %get-tuple-element.46), channel_id=1, source_target_pairs={{0,40},{1,41},{2,42},{3,43},{4,44},{5,45},{6,46},{7,47},{8,32},{9,... | collective-permute-start | bytes 884744 | tf_op jit(solution)/shard_map/ppermute | solution.py:208
  105.3 1.4 %shard_map.71 = bf16[2,2,2,4,16,384]{5,4,3,2,1,0:T(8,128)(2,1)} custom-call(s32[1]{0:T(128)} %bitcast.14.core_ref, s32[1]{0:T(128)} %bitcast.1.side_ref, bf16[8,2,2,2,16,384]{5,4,3,2,1,0:T(8,128)(2,1)S(1)} %bitcast.21, bf16[384,384]{1,0:T(8,128)(2,1)S(1)} %copy-done, bf16[416,384]{1,0:T(8,128)(2,1)S(1)} %collective-permute-done.refs_1_, ...), custom_call_target="tpu_custom_call" | custom-call | flops 301989888 | bytes 1572864 | tf_op jit(solution)/shard_map/pallas_call | solution.py:20
  106.7 13.9 %all-to-all-start.2 = ((bf16[32,16,384]{2,1,0:T(8,128)(2,1)}), bf16[32,16,384]{2,1,0:T(8,128)(2,1)S(1)}, u32[]{:S(2)}, u32[]{:S(2)}) async-start(bf16[32,16,384]{2,1,0:T(8,128)(2,1)} %bitcast.15), calls=%async_computation.2 | async-start | bytes 786432 | tf_op jit(solution)/shard_map/all_to_all | solution.py:310
  120.7 0.0 copy-start.2
  120.7 1.4 %copy-done.2 = bf16[2048,384]{1,0:T(8,128)(2,1)S(1)} copy-done((bf16[2048,384]{1,0:T(8,128)(2,1)S(1)}, bf16[2048,384]{1,0:T(8,128)(2,1)}, u32[]{:S(2)}) %copy-start.2) | copy-done | bytes 1572888
  122.1 2.3 %shard_map.74 = f32[384,384]{1,0:T(8,128)} custom-call(s32[1]{0:T(128)} %bitcast.par_ref, s32[1]{0:T(128)} %bitcast.1.side_ref, bf16[2,8,2,2,2,16,384]{6,5,4,3,2,1,0:T(8,128)(2,1)S(1)} %bitcast.27, bf16[8,2,2,2,16,384]{5,4,3,2,1,0:T(8,128)(2,1)S(1)} %bitcast.22, bf16[384,384]{1,0:T(8,128)(2,1)S(1)} %collective-permute-done.8.x_ref, ...), custom_call_target="tpu_custom_call" | custom-call | flops 6039797760 | bytes 1572864 | tf_op jit(solution)/shard_map/pallas_call | solution.py:20
  124.4 10.6 %all-to-all-done.2 = bf16[32,16,384]{2,1,0:T(8,128)(2,1)S(1)} async-done(((bf16[32,16,384]{2,1,0:T(8,128)(2,1)}), bf16[32,16,384]{2,1,0:T(8,128)(2,1)S(1)}, u32[]{:S(2)}, u32[]{:S(2)}) %all-to-all-start.2) | async-done | bytes 393248 | tf_op jit(solution)/shard_map/all_to_all | solution.py:310
  135.0 0.7 shard_map.72
  (17 shorter events, 0.1 us)
Async XLA Ops:
  5.1 12.1 %copy-start.4 = (bf16[128,384]{1,0:T(8,128)(2,1)S(1)}, bf16[128,384]{1,0:T(8,128)(2,1)}, u32[]{:S(2)}) copy-start(bf16[128,384]{1,0:T(8,128)(2,1)} %param.7) | copy-start | bytes 294916
  5.1 12.2 %copy-start = (bf16[384,384]{1,0:T(8,128)(2,1)S(1)}, bf16[384,384]{1,0:T(8,128)(2,1)}, u32[]{:S(2)}) copy-start(bf16[384,384]{1,0:T(8,128)(2,1)} %get-tuple-element.26.refs_0_) | copy-start | bytes 884740
  5.1 52.9 %all-to-all-start = ((bf16[32,64,384]{2,1,0:T(8,128)(2,1)}), bf16[32,64,384]{2,1,0:T(8,128)(2,1)S(1)}, u32[]{:S(2)}, u32[]{:S(2)}) async-start(bf16[32,64,384]{2,1,0:T(8,128)(2,1)} %bitcast.32), calls=%async_computation | async-start | bytes 3145728 | tf_op jit(solution)/shard_map/all_to_all | solution.py:234
  17.4 29.1 %collective-permute-start = (bf16[416,384]{1,0:T(8,128)(2,1)S(1)}, bf16[416,384]{1,0:T(8,128)(2,1)S(1)}, u32[]{:S(2)}, u32[]{:S(2)}) collective-permute-start(bf16[416,384]{1,0:T(8,128)(2,1)S(1)} %get-tuple-element.49), channel_id=1, source_target_pairs={{0,32},{16,48},{32,0},{48,16},{64,96},{80,112},{96,64},{112,80},{1... | collective-permute-start | bytes 958472 | tf_op jit(solution)/shard_map/ppermute | solution.py:206
  19.5 26.9 %collective-permute-start.1 = (bf16[416,384]{1,0:T(8,128)(2,1)S(1)}, bf16[416,384]{1,0:T(8,128)(2,1)S(1)}, u32[]{:S(2)}, u32[]{:S(2)}) collective-permute-start(bf16[416,384]{1,0:T(8,128)(2,1)S(1)} %get-tuple-element.48), channel_id=1, source_target_pairs={{0,8},{1,9},{2,10},{3,11},{4,12},{5,13},{6,14},{7,15},{8,0},{9,1},... | collective-permute-start | bytes 958472 | tf_op jit(solution)/shard_map/ppermute | solution.py:207
  23.2 34.7 %collective-permute-start.2 = (bf16[416,384]{1,0:T(8,128)(2,1)S(1)}, bf16[416,384]{1,0:T(8,128)(2,1)S(1)}, u32[]{:S(2)}, u32[]{:S(2)}) collective-permute-start(bf16[416,384]{1,0:T(8,128)(2,1)S(1)} %get-tuple-element.47), channel_id=1, source_target_pairs={{0,40},{1,41},{2,42},{3,43},{4,44},{5,45},{6,46},{7,47},{8,32},{9,... | collective-permute-start | bytes 958472 | tf_op jit(solution)/shard_map/ppermute | solution.py:208
  58.3 0.9 copy-start.3
  59.2 32.7 %all-to-all-start.1 = ((bf16[8,128,384]{2,1,0:T(8,128)(2,1)}), bf16[8,128,384]{2,1,0:T(8,128)(2,1)S(1)}, u32[]{:S(2)}, u32[]{:S(2)}) async-start(bf16[8,128,384]{2,1,0:T(8,128)(2,1)} %bitcast.29), calls=%async_computation.1 | async-start | bytes 1572864 | tf_op jit(solution)/shard_map/all_to_all | solution.py:262
  64.9 27.1 %collective-permute-start.3 = (bf16[2,8,2,16,384]{4,3,2,1,0:T(8,128)(2,1)S(1)}, bf16[2,8,2,16,384]{4,3,2,1,0:T(8,128)(2,1)S(1)}, u32[]{:S(2)}, u32[]{:S(2)}) collective-permute-start(bf16[2,8,2,16,384]{4,3,2,1,0:T(8,128)(2,1)S(1)} %dynamic-slice_bitcast_fusion), channel_id=1, source_target_pairs={{0,776},{1,777},{2,778},{3,779},{4,780},{5,781},{6,782},{7,783},{8... | collective-permute-start | bytes 1179656 | tf_op jit(solution)/shard_map/ppermute | solution.py:266
  78.1 9.9 %collective-permute-start.4 = (bf16[32,384]{1,0:T(8,128)(2,1)S(1)}, bf16[32,384]{1,0:T(8,128)(2,1)S(1)}, u32[]{:S(2)}, u32[]{:S(2)}) collective-permute-start(bf16[32,384]{1,0:T(8,128)(2,1)S(1)} %get-tuple-element.38), channel_id=1, source_target_pairs={{0,32},{16,48},{32,0},{48,16},{64,96},{80,112},{96,64},{112,80},{1... | collective-permute-start | bytes 73736 | tf_op jit(solution)/shard_map/ppermute | solution.py:206
  82.7 5.7 %collective-permute-start.5 = (bf16[32,384]{1,0:T(8,128)(2,1)S(1)}, bf16[32,384]{1,0:T(8,128)(2,1)S(1)}, u32[]{:S(2)}, u32[]{:S(2)}) collective-permute-start(bf16[32,384]{1,0:T(8,128)(2,1)S(1)} %get-tuple-element.39), channel_id=1, source_target_pairs={{0,8},{1,9},{2,10},{3,11},{4,12},{5,13},{6,14},{7,15},{8,0},{9,1},... | collective-permute-start | bytes 73736 | tf_op jit(solution)/shard_map/ppermute | solution.py:207
  84.6 6.6 %collective-permute-start.6 = (bf16[32,384]{1,0:T(8,128)(2,1)S(1)}, bf16[32,384]{1,0:T(8,128)(2,1)S(1)}, u32[]{:S(2)}, u32[]{:S(2)}) collective-permute-start(bf16[32,384]{1,0:T(8,128)(2,1)S(1)} %get-tuple-element.40), channel_id=1, source_target_pairs={{0,40},{1,41},{2,42},{3,43},{4,44},{5,45},{6,46},{7,47},{8,32},{9,... | collective-permute-start | bytes 73736 | tf_op jit(solution)/shard_map/ppermute | solution.py:208
  91.9 2.6 %copy-start.1 = (bf16[2048,384]{1,0:T(8,128)(2,1)S(1)}, bf16[2048,384]{1,0:T(8,128)(2,1)}, u32[]{:S(2)}) copy-start(bf16[2048,384]{1,0:T(8,128)(2,1)} %param.4) | copy-start | bytes 4718596
  92.6 12.7 %collective-permute-start.7 = (bf16[2,256,384]{2,1,0:T(8,128)(2,1)S(1)}, bf16[2,256,384]{2,1,0:T(8,128)(2,1)S(1)}, u32[]{:S(2)}, u32[]{:S(2)}) collective-permute-start(bf16[2,256,384]{2,1,0:T(8,128)(2,1)S(1)} %shard_map.70), channel_id=1, source_target_pairs={{0,16},{16,0},{32,48},{48,32},{64,80},{80,64},{96,112},{112,96},{1... | collective-permute-start | bytes 1179656 | tf_op jit(solution)/shard_map/ppermute | solution.py:283
  96.1 24.6 %collective-permute-start.8 = (bf16[384,384]{1,0:T(8,128)(2,1)}, bf16[384,384]{1,0:T(8,128)(2,1)S(1)}, u32[]{:S(2)}, u32[]{:S(2)}) collective-permute-start(bf16[384,384]{1,0:T(8,128)(2,1)} %get-tuple-element.44), channel_id=1, source_target_pairs={{0,32},{16,48},{32,0},{48,16},{64,96},{80,112},{96,64},{112,80},{1... | collective-permute-start | bytes 884744 | tf_op jit(solution)/shard_map/ppermute | solution.py:206
  98.5 22.1 %collective-permute-start.9 = (bf16[384,384]{1,0:T(8,128)(2,1)}, bf16[384,384]{1,0:T(8,128)(2,1)}, u32[]{:S(2)}, u32[]{:S(2)}) collective-permute-start(bf16[384,384]{1,0:T(8,128)(2,1)} %get-tuple-element.45), channel_id=1, source_target_pairs={{0,8},{1,9},{2,10},{3,11},{4,12},{5,13},{6,14},{7,15},{8,0},{9,1},... | collective-permute-start | bytes 884744 | tf_op jit(solution)/shard_map/ppermute | solution.py:207
  101.9 18.7 %collective-permute-start.10 = (bf16[384,384]{1,0:T(8,128)(2,1)S(1)}, bf16[384,384]{1,0:T(8,128)(2,1)}, u32[]{:S(2)}, u32[]{:S(2)}) collective-permute-start(bf16[384,384]{1,0:T(8,128)(2,1)S(1)} %get-tuple-element.46), channel_id=1, source_target_pairs={{0,40},{1,41},{2,42},{3,43},{4,44},{5,45},{6,46},{7,47},{8,32},{9,... | collective-permute-start | bytes 884744 | tf_op jit(solution)/shard_map/ppermute | solution.py:208
  106.7 28.3 %all-to-all-start.2 = ((bf16[32,16,384]{2,1,0:T(8,128)(2,1)}), bf16[32,16,384]{2,1,0:T(8,128)(2,1)S(1)}, u32[]{:S(2)}, u32[]{:S(2)}) async-start(bf16[32,16,384]{2,1,0:T(8,128)(2,1)} %bitcast.15), calls=%async_computation.2 | async-start | bytes 786432 | tf_op jit(solution)/shard_map/all_to_all | solution.py:310
  120.7 1.4 %copy-start.2 = (bf16[2048,384]{1,0:T(8,128)(2,1)S(1)}, bf16[2048,384]{1,0:T(8,128)(2,1)}, u32[]{:S(2)}) copy-start(bf16[2048,384]{1,0:T(8,128)(2,1)} %param.4) | copy-start | bytes 4718596

commit v9 on v8

--- a/solution.py
+++ b/solution.py
@@ -167,9 +167,13 @@
     x_ref[...] = outer(mine, slope_ref, 1).astype(BF16)
 
 
-def weigh_own(factor, par_ref, side_ref, tok_ref, slope_ref, x_ref, z_ref, both_ref, out_ref):
+def weigh_own(par_ref, side_ref, tok_ref, slope_ref, out_ref):
     par, side = par_ref[0], side_ref[0]
-    total = outer([tok_ref[z, :, par, :, side] for z in range(2)], slope_ref, 0)
+    out_ref[...] = outer([tok_ref[z, :, par, :, side] for z in range(2)], slope_ref, 0)
+
+
+def join(factor, own_ref, x_ref, z_ref, both_ref, out_ref):
+    total = own_ref[...]
     for ref in (x_ref, z_ref, both_ref):
         total = total + ref[...].astype(F32)
     out_ref[...] = total * factor
@@ -288,7 +292,8 @@
         flops // 2, size,
         par, side, tok, far_tok, spread,
     )
-    shares = send(*shares)
+    share_x, share_z, share_both = shares
+    share_z = lax.ppermute(share_z, "local", over_z)
     (both,) = call(
         back_mine,
         [((2, 2, 2, ys // 2, sub, feat), BF16)],
@@ -296,6 +301,9 @@
         flops // 2, size,
         core, side, spread, *weights, other,
     )
+    share_z, share_x, share_both = lax.optimization_barrier((share_z, share_x, share_both))
+    share_x = lax.ppermute(share_x, "node", over_x)
+    share_both = lax.ppermute(share_both, ("node", "local"), over_both)
     groups = [
         [
             moved(per * (ys * t + y) + low, k * ys + own)
@@ -311,12 +319,19 @@
         both.reshape(nodes // 2, sub, feat),
         ("node", "local"), 0, 0, axis_index_groups=groups, tiled=True,
     ).reshape(4, 2, nodes // 16, sub, feat)
+    (own,) = call(
+        weigh_own,
+        [((feat, units), F32)],
+        [SMEM, SMEM, VMEM, VMEM],
+        flops // 2, size,
+        par, side, tok, spread,
+    )
     (weight_grad,) = call(
-        functools.partial(weigh_own, rows ** (-0.5)),
+        functools.partial(join, rows ** (-0.5)),
         [((feat, units), F32)],
-        [SMEM, SMEM] + [VMEM] * 5,
-        10 * flops, size,
-        par, side, tok, spread, *shares,
+        [VMEM] * 4,
+        8 * flops, size,
+        own, share_x, share_z, share_both,
     )
     (input_grad,) = call(
         finish, [((2, sub, feat), BF16)], [VMEM], rows * feat, size // 2, sums

time: 138 us -> 146 us (1.058)
  waiting for transfers between devices: 45.2 us -> 51.5 us
  local copies, waits for them, and re-layouts: 3.36 us -> 6.04 us
    ppermute x0 -> x3, waiting for transfers between devices: none -> 16.9 us  [the longest x1 10.6 us: shards(): share_x = lax.ppermute(share_x, 'node', over_x)]
    ppermute x0 -> x3, starting transfers between devices: none -> 10.7 us  [the longest x1 3.91 us: shards(): share_z = lax.ppermute(share_z, 'local', over_z)]
    all_to_all x1, waiting for transfers between devices: 10.6 us -> 0.01 us  [shards(): lax.all_to_all(both.reshape(nodes // 2, sub, feat), ('node', 'local'), 0,...]
    ppermute x3 -> x2, starting transfers between devices: 9 us -> 5.62 us  [send(): lax.ppermute(z, 'local', over_z)]
    ppermute x3 -> x2, starting transfers between devices: 10.1 us -> 6.75 us  [send(): lax.ppermute(both, ('node', 'local'), over_both)]
    unnamed x10 -> x22, local copies, waits for them, and re-layouts: 2.3 us -> 5.22 us
    ppermute x3 -> x2, starting transfers between devices: 9.18 us -> 6.72 us  [send(): lax.ppermute(x, 'node', over_x)]
    pallas_call x7 -> x8, Pallas kernels: 7.62 us -> 7.49 us  [call(): pl.pallas_call(kernel, out_shape=[jax.ShapeDtypeStruct(s, d) for s, d in...]
  transfers between devices with their start and end apart: 14 -> 14, of which waited for: 5 -> 6; matrix products, arithmetic and copies ran while one was open for 1% -> 1% of each run, Pallas kernels for 4% -> 4%
where the time goes in v9:
time: 146 us; the launch traced here: 145 us
  starting transfers between devices  74.4 us (51%)
  waiting for transfers between devices  51.5 us (35%)
  Pallas kernels  11.9 us (8%)
  local copies, waits for them, and re-layouts  6.04 us (4%)
    ppermute x2, waiting for transfers between devices, send(): lax.ppermute(x, 'node', over_x)  19.9 us
    ppermute x2, waiting for transfers between devices, send(): lax.ppermute(both, ('node', 'local'), over_both)  14.3 us
    ppermute x1, starting transfers between devices, shards(): far_tok = lax.ppermute(leave, ('node', 'local'), step)  13.3 us
    all_to_all x1, starting transfers between devices, shards(): lax.all_to_all(both.reshape(nodes // 2, sub, feat), ('node', 'local'), 0,...  12.7 us
    all_to_all x1, starting transfers between devices, shards(): lax.all_to_all(partial.reshape(2 * locals_, 2 * mine, units), ('node', 'l...  12 us
    ppermute x1, waiting for transfers between devices, shards(): share_x = lax.ppermute(share_x, 'node', over_x)  10.6 us
    pallas_call x8, Pallas kernels, call(): pl.pallas_call(kernel, out_shape=[jax.ShapeDtypeStruct(s, d) for s, d in...  7.49 us
    ppermute x2, starting transfers between devices, send(): lax.ppermute(both, ('node', 'local'), over_both)  6.75 us
  transfers between devices with their start and end apart: 14, of which 6 were waited for; matrix products, arithmetic and copies ran while one was open for 1% of the time, Pallas kernels for 4%

profile of v9, /device:TPU:14, one launch (start us, length us, event | category | flops | bytes accessed | tf_op | source)
XLA Modules:
  0.0 144.9 jit_solution(6825691066640914590)
XLA Ops:
  0.6 4.4 %shard_map.67 = (bf16[384,384]{1,0:T(8,128)(2,1)}, bf16[2,2,8,2,2,16,384]{6,5,4,3,2,1,0:T(8,128)(2,1)}) custom-call(s32[1]{0:T(128)} %bitcast.2.start_ref, bf16[2,8,2,2,2,16,384]{6,5,4,3,2,1,0:T(8,128)(2,1)} %bitcast.23, bf16[384,384]{1,0:T(8,128)(2,1)} %codes_hbm.1, f32[3,384]{1,0:T(4,128)} %scales_hbm.1), custom_call_target="tpu_custom_call" | custom-call | flops 603979776 | bytes 3145728 | tf_op jit(solution)/shard_map/pallas_call | solution.py:215
  5.1 12.0 %all-to-all-start = ((bf16[32,64,384]{2,1,0:T(8,128)(2,1)}), bf16[32,64,384]{2,1,0:T(8,128)(2,1)S(1)}, u32[]{:S(2)}, u32[]{:S(2)}) async-start(bf16[32,64,384]{2,1,0:T(8,128)(2,1)} %bitcast.33), calls=%async_computation | async-start | bytes 3145728 | tf_op jit(solution)/shard_map/all_to_all | solution.py:238
  17.4 2.1 %collective-permute-start = (bf16[416,384]{1,0:T(8,128)(2,1)S(1)}, bf16[416,384]{1,0:T(8,128)(2,1)S(1)}, u32[]{:S(2)}, u32[]{:S(2)}) collective-permute-start(bf16[416,384]{1,0:T(8,128)(2,1)S(1)} %get-tuple-element.55), channel_id=1, source_target_pairs={{0,32},{16,48},{32,0},{48,16},{64,96},{80,112},{96,64},{112,80},{1... | collective-permute-start | bytes 958472 | tf_op jit(solution)/shard_map/ppermute | solution.py:210
  19.5 3.7 %collective-permute-start.1 = (bf16[416,384]{1,0:T(8,128)(2,1)S(1)}, bf16[416,384]{1,0:T(8,128)(2,1)S(1)}, u32[]{:S(2)}, u32[]{:S(2)}) collective-permute-start(bf16[416,384]{1,0:T(8,128)(2,1)S(1)} %get-tuple-element.54), channel_id=1, source_target_pairs={{0,8},{1,9},{2,10},{3,11},{4,12},{5,13},{6,14},{7,15},{8,0},{9,1},... | collective-permute-start | bytes 958472 | tf_op jit(solution)/shard_map/ppermute | solution.py:211
  23.2 3.4 %collective-permute-start.2 = (bf16[416,384]{1,0:T(8,128)(2,1)S(1)}, bf16[416,384]{1,0:T(8,128)(2,1)S(1)}, u32[]{:S(2)}, u32[]{:S(2)}) collective-permute-start(bf16[416,384]{1,0:T(8,128)(2,1)S(1)} %get-tuple-element.53), channel_id=1, source_target_pairs={{0,40},{1,41},{2,42},{3,43},{4,44},{5,45},{6,46},{7,47},{8,32},{9,... | collective-permute-start | bytes 958472 | tf_op jit(solution)/shard_map/ppermute | solution.py:212
  26.6 19.9 %collective-permute-done.refs_1_ = bf16[416,384]{1,0:T(8,128)(2,1)S(1)} collective-permute-done((bf16[416,384]{1,0:T(8,128)(2,1)S(1)}, bf16[416,384]{1,0:T(8,128)(2,1)S(1)}, u32[]{:S(2)}, u32[]{:S(2)}) %collective-permute-start) | collective-permute-done | bytes 319520 | tf_op jit(solution)/shard_map/ppermute | solution.py:210
  46.5 11.5 %collective-permute-done.2.refs_3_ = bf16[416,384]{1,0:T(8,128)(2,1)S(1)} collective-permute-done((bf16[416,384]{1,0:T(8,128)(2,1)S(1)}, bf16[416,384]{1,0:T(8,128)(2,1)S(1)}, u32[]{:S(2)}, u32[]{:S(2)}) %collective-permute-start.2) | collective-permute-done | bytes 319520 | tf_op jit(solution)/shard_map/ppermute | solution.py:212
  58.0 1.2 copy-done.1
  59.2 1.4 copy-done.2
  60.9 0.9 copy-done.7
  61.8 4.6 %all-to-all-start.1 = ((bf16[8,128,384]{2,1,0:T(8,128)(2,1)}), bf16[8,128,384]{2,1,0:T(8,128)(2,1)S(1)}, u32[]{:S(2)}, u32[]{:S(2)}) async-start(bf16[8,128,384]{2,1,0:T(8,128)(2,1)} %bitcast.30), calls=%async_computation.1 | async-start | bytes 1572864 | tf_op jit(solution)/shard_map/all_to_all | solution.py:266
  66.4 0.8 dynamic-slice_bitcast_fusion
  67.2 13.3 %collective-permute-start.3 = (bf16[2,8,2,16,384]{4,3,2,1,0:T(8,128)(2,1)}, bf16[2,8,2,16,384]{4,3,2,1,0:T(8,128)(2,1)}, u32[]{:S(2)}, u32[]{:S(2)}) collective-permute-start(bf16[2,8,2,16,384]{4,3,2,1,0:T(8,128)(2,1)} %dynamic-slice_bitcast_fusion), channel_id=1, source_target_pairs={{0,776},{1,777},{2,778},{3,779},{4,780},{5,781},{6,782},{7,783},{8... | collective-permute-start | bytes 1179656 | tf_op jit(solution)/shard_map/ppermute | solution.py:270
  80.5 4.6 %collective-permute-start.4 = (bf16[32,384]{1,0:T(8,128)(2,1)S(1)}, bf16[32,384]{1,0:T(8,128)(2,1)S(1)}, u32[]{:S(2)}, u32[]{:S(2)}) collective-permute-start(bf16[32,384]{1,0:T(8,128)(2,1)S(1)} %get-tuple-element.41), channel_id=1, source_target_pairs={{0,32},{16,48},{32,0},{48,16},{64,96},{80,112},{96,64},{112,80},{1... | collective-permute-start | bytes 73736 | tf_op jit(solution)/shard_map/ppermute | solution.py:210
  85.1 1.9 %collective-permute-start.5 = (bf16[32,384]{1,0:T(8,128)(2,1)S(1)}, bf16[32,384]{1,0:T(8,128)(2,1)S(1)}, u32[]{:S(2)}, u32[]{:S(2)}) collective-permute-start(bf16[32,384]{1,0:T(8,128)(2,1)S(1)} %get-tuple-element.42), channel_id=1, source_target_pairs={{0,8},{1,9},{2,10},{3,11},{4,12},{5,13},{6,14},{7,15},{8,0},{9,1},... | collective-permute-start | bytes 73736 | tf_op jit(solution)/shard_map/ppermute | solution.py:211
  87.0 3.4 %collective-permute-start.6 = (bf16[32,384]{1,0:T(8,128)(2,1)S(1)}, bf16[32,384]{1,0:T(8,128)(2,1)S(1)}, u32[]{:S(2)}, u32[]{:S(2)}) collective-permute-start(bf16[32,384]{1,0:T(8,128)(2,1)S(1)} %get-tuple-element.43), channel_id=1, source_target_pairs={{0,40},{1,41},{2,42},{3,43},{4,44},{5,45},{6,46},{7,47},{8,32},{9,... | collective-permute-start | bytes 73736 | tf_op jit(solution)/shard_map/ppermute | solution.py:212
  90.8 2.8 %collective-permute-done.6.both_ref = bf16[32,384]{1,0:T(8,128)(2,1)S(1)} collective-permute-done((bf16[32,384]{1,0:T(8,128)(2,1)S(1)}, bf16[32,384]{1,0:T(8,128)(2,1)S(1)}, u32[]{:S(2)}, u32[]{:S(2)}) %collective-permute-start.6) | collective-permute-done | bytes 24608 | tf_op jit(solution)/shard_map/ppermute | solution.py:212
  93.6 0.7 shard_map.69
  94.3 1.0 copy-done.4
  95.3 0.7 shard_map.70
  95.9 2.1 %collective-permute-start.7 = (bf16[2,256,384]{2,1,0:T(8,128)(2,1)S(1)}, bf16[2,256,384]{2,1,0:T(8,128)(2,1)S(1)}, u32[]{:S(2)}, u32[]{:S(2)}) collective-permute-start(bf16[2,256,384]{2,1,0:T(8,128)(2,1)S(1)} %shard_map.70), channel_id=1, source_target_pairs={{0,16},{16,0},{32,48},{48,32},{64,80},{80,64},{96,112},{112,96},{1... | collective-permute-start | bytes 1179656 | tf_op jit(solution)/shard_map/ppermute | solution.py:287
  98.0 2.1 %shard_map.74 = (bf16[384,384]{1,0:T(8,128)(2,1)S(1)}, bf16[384,384]{1,0:T(8,128)(2,1)}, bf16[384,384]{1,0:T(8,128)(2,1)S(1)}) custom-call(s32[1]{0:T(128)} %bitcast.par_ref, s32[1]{0:T(128)} %bitcast.1.side_ref, bf16[2,8,2,2,2,16,384]{6,5,4,3,2,1,0:T(8,128)(2,1)S(1)} %bitcast.25, bf16[2,8,2,16,384]{4,3,2,1,0:T(8,128)(2,1)} %collective-permute-done.3.far_tok_ref, ...), custom_call_target="tpu_custom_call" | custom-call | flops 301989888 | bytes 1572864 | tf_op jit(solution)/shard_map/pallas_call | solution.py:20
  100.1 3.9 %collective-permute-start.8 = (bf16[384,384]{1,0:T(8,128)(2,1)}, bf16[384,384]{1,0:T(8,128)(2,1)}, u32[]{:S(2)}, u32[]{:S(2)}) collective-permute-start(bf16[384,384]{1,0:T(8,128)(2,1)} %get-tuple-element.47), channel_id=1, source_target_pairs={{0,8},{1,9},{2,10},{3,11},{4,12},{5,13},{6,14},{7,15},{8,0},{9,1},... | collective-permute-start | bytes 884744 | tf_op jit(solution)/shard_map/ppermute | solution.py:296
  104.1 0.7 shard_map.71
  104.8 0.7 copy-done.6
  105.5 12.7 %all-to-all-start.2 = ((bf16[32,16,384]{2,1,0:T(8,128)(2,1)}), bf16[32,16,384]{2,1,0:T(8,128)(2,1)S(1)}, u32[]{:S(2)}, u32[]{:S(2)}) async-start(bf16[32,16,384]{2,1,0:T(8,128)(2,1)} %bitcast.28), calls=%async_computation.2 | async-start | bytes 786432 | tf_op jit(solution)/shard_map/all_to_all | solution.py:318
  118.2 3.4 %collective-permute-start.9 = (bf16[384,384]{1,0:T(8,128)(2,1)}, bf16[384,384]{1,0:T(8,128)(2,1)S(1)}, u32[]{:S(2)}, u32[]{:S(2)}) collective-permute-start(bf16[384,384]{1,0:T(8,128)(2,1)} %copy-done.10), channel_id=1, source_target_pairs={{0,32},{16,48},{32,0},{48,16},{64,96},{80,112},{96,64},{112,80},{1... | collective-permute-start | bytes 884744 | tf_op jit(solution)/shard_map/ppermute | solution.py:305
  121.7 3.3 %collective-permute-start.10 = (bf16[384,384]{1,0:T(8,128)(2,1)}, bf16[384,384]{1,0:T(8,128)(2,1)S(1)}, u32[]{:S(2)}, u32[]{:S(2)}) collective-permute-start(bf16[384,384]{1,0:T(8,128)(2,1)} %copy-done.9), channel_id=1, source_target_pairs={{0,40},{1,41},{2,42},{3,43},{4,44},{5,45},{6,46},{7,47},{8,32},{9,... | collective-permute-start | bytes 884744 | tf_op jit(solution)/shard_map/ppermute | solution.py:306
  125.4 10.6 %collective-permute-done.9.x_ref = bf16[384,384]{1,0:T(8,128)(2,1)S(1)} collective-permute-done((bf16[384,384]{1,0:T(8,128)(2,1)}, bf16[384,384]{1,0:T(8,128)(2,1)S(1)}, u32[]{:S(2)}, u32[]{:S(2)}) %collective-permute-start.9) | collective-permute-done | bytes 294944 | tf_op jit(solution)/shard_map/ppermute | solution.py:305
  136.1 6.3 %collective-permute-done.10.both_ref = bf16[384,384]{1,0:T(8,128)(2,1)S(1)} collective-permute-done((bf16[384,384]{1,0:T(8,128)(2,1)}, bf16[384,384]{1,0:T(8,128)(2,1)S(1)}, u32[]{:S(2)}, u32[]{:S(2)}) %collective-permute-start.10) | collective-permute-done | bytes 294944 | tf_op jit(solution)/shard_map/ppermute | solution.py:306
  142.3 1.9 %shard_map.75 = f32[384,384]{1,0:T(8,128)} custom-call(f32[384,384]{1,0:T(8,128)S(1)} %shard_map.73.own_ref, bf16[384,384]{1,0:T(8,128)(2,1)S(1)} %collective-permute-done.9.x_ref, bf16[384,384]{1,0:T(8,128)(2,1)} %collective-permute-done.8.z_ref, bf16[384,384]{1,0:T(8,128)(2,1)S(1)} %collective-permute-done.10.both_ref), custom_call_target="tpu_custom_call" | custom-call | flops 4831838208 | bytes 1572864 | tf_op jit(solution)/shard_map/pallas_call | solution.py:20
  144.3 0.7 shard_map.72
  (30 shorter events, 1.3 us)
Async XLA Ops:
  5.1 12.1 %copy-start.8 = (bf16[128,384]{1,0:T(8,128)(2,1)S(1)}, bf16[128,384]{1,0:T(8,128)(2,1)}, u32[]{:S(2)}) copy-start(bf16[128,384]{1,0:T(8,128)(2,1)} %param.7) | copy-start | bytes 294916
  5.1 12.2 %copy-start.3 = (bf16[384,384]{1,0:T(8,128)(2,1)S(1)}, bf16[384,384]{1,0:T(8,128)(2,1)}, u32[]{:S(2)}) copy-start(bf16[384,384]{1,0:T(8,128)(2,1)} %get-tuple-element.29.refs_0_) | copy-start | bytes 884740
  5.1 52.9 %all-to-all-start = ((bf16[32,64,384]{2,1,0:T(8,128)(2,1)}), bf16[32,64,384]{2,1,0:T(8,128)(2,1)S(1)}, u32[]{:S(2)}, u32[]{:S(2)}) async-start(bf16[32,64,384]{2,1,0:T(8,128)(2,1)} %bitcast.33), calls=%async_computation | async-start | bytes 3145728 | tf_op jit(solution)/shard_map/all_to_all | solution.py:238
  17.4 29.1 %collective-permute-start = (bf16[416,384]{1,0:T(8,128)(2,1)S(1)}, bf16[416,384]{1,0:T(8,128)(2,1)S(1)}, u32[]{:S(2)}, u32[]{:S(2)}) collective-permute-start(bf16[416,384]{1,0:T(8,128)(2,1)S(1)} %get-tuple-element.55), channel_id=1, source_target_pairs={{0,32},{16,48},{32,0},{48,16},{64,96},{80,112},{96,64},{112,80},{1... | collective-permute-start | bytes 958472 | tf_op jit(solution)/shard_map/ppermute | solution.py:210
  19.5 26.9 %collective-permute-start.1 = (bf16[416,384]{1,0:T(8,128)(2,1)S(1)}, bf16[416,384]{1,0:T(8,128)(2,1)S(1)}, u32[]{:S(2)}, u32[]{:S(2)}) collective-permute-start(bf16[416,384]{1,0:T(8,128)(2,1)S(1)} %get-tuple-element.54), channel_id=1, source_target_pairs={{0,8},{1,9},{2,10},{3,11},{4,12},{5,13},{6,14},{7,15},{8,0},{9,1},... | collective-permute-start | bytes 958472 | tf_op jit(solution)/shard_map/ppermute | solution.py:211
  23.2 34.7 %collective-permute-start.2 = (bf16[416,384]{1,0:T(8,128)(2,1)S(1)}, bf16[416,384]{1,0:T(8,128)(2,1)S(1)}, u32[]{:S(2)}, u32[]{:S(2)}) collective-permute-start(bf16[416,384]{1,0:T(8,128)(2,1)S(1)} %get-tuple-element.53), channel_id=1, source_target_pairs={{0,40},{1,41},{2,42},{3,43},{4,44},{5,45},{6,46},{7,47},{8,32},{9,... | collective-permute-start | bytes 958472 | tf_op jit(solution)/shard_map/ppermute | solution.py:212
  58.0 1.2 copy-start.1
  59.2 1.4 copy-start.2
  60.6 5.9 %copy-start = (bf16[2048,384]{1,0:T(8,128)(2,1)S(1)}, bf16[2048,384]{1,0:T(8,128)(2,1)}, u32[]{:S(2)}) copy-start(bf16[2048,384]{1,0:T(8,128)(2,1)} %param.4) | copy-start | bytes 4718596
  60.9 0.9 copy-start.7
  61.8 32.4 %all-to-all-start.1 = ((bf16[8,128,384]{2,1,0:T(8,128)(2,1)}), bf16[8,128,384]{2,1,0:T(8,128)(2,1)S(1)}, u32[]{:S(2)}, u32[]{:S(2)}) async-start(bf16[8,128,384]{2,1,0:T(8,128)(2,1)} %bitcast.30), calls=%async_computation.1 | async-start | bytes 1572864 | tf_op jit(solution)/shard_map/all_to_all | solution.py:266
  67.2 27.1 %collective-permute-start.3 = (bf16[2,8,2,16,384]{4,3,2,1,0:T(8,128)(2,1)}, bf16[2,8,2,16,384]{4,3,2,1,0:T(8,128)(2,1)}, u32[]{:S(2)}, u32[]{:S(2)}) collective-permute-start(bf16[2,8,2,16,384]{4,3,2,1,0:T(8,128)(2,1)} %dynamic-slice_bitcast_fusion), channel_id=1, source_target_pairs={{0,776},{1,777},{2,778},{3,779},{4,780},{5,781},{6,782},{7,783},{8... | collective-permute-start | bytes 1179656 | tf_op jit(solution)/shard_map/ppermute | solution.py:270
  80.5 9.9 %collective-permute-start.4 = (bf16[32,384]{1,0:T(8,128)(2,1)S(1)}, bf16[32,384]{1,0:T(8,128)(2,1)S(1)}, u32[]{:S(2)}, u32[]{:S(2)}) collective-permute-start(bf16[32,384]{1,0:T(8,128)(2,1)S(1)} %get-tuple-element.41), channel_id=1, source_target_pairs={{0,32},{16,48},{32,0},{48,16},{64,96},{80,112},{96,64},{112,80},{1... | collective-permute-start | bytes 73736 | tf_op jit(solution)/shard_map/ppermute | solution.py:210
  85.1 5.7 %collective-permute-start.5 = (bf16[32,384]{1,0:T(8,128)(2,1)S(1)}, bf16[32,384]{1,0:T(8,128)(2,1)S(1)}, u32[]{:S(2)}, u32[]{:S(2)}) collective-permute-start(bf16[32,384]{1,0:T(8,128)(2,1)S(1)} %get-tuple-element.42), channel_id=1, source_target_pairs={{0,8},{1,9},{2,10},{3,11},{4,12},{5,13},{6,14},{7,15},{8,0},{9,1},... | collective-permute-start | bytes 73736 | tf_op jit(solution)/shard_map/ppermute | solution.py:211
  87.0 6.6 %collective-permute-start.6 = (bf16[32,384]{1,0:T(8,128)(2,1)S(1)}, bf16[32,384]{1,0:T(8,128)(2,1)S(1)}, u32[]{:S(2)}, u32[]{:S(2)}) collective-permute-start(bf16[32,384]{1,0:T(8,128)(2,1)S(1)} %get-tuple-element.43), channel_id=1, source_target_pairs={{0,40},{1,41},{2,42},{3,43},{4,44},{5,45},{6,46},{7,47},{8,32},{9,... | collective-permute-start | bytes 73736 | tf_op jit(solution)/shard_map/ppermute | solution.py:212
  94.3 1.0 copy-start.4
  95.9 8.1 %copy-start.5 = (bf16[384,384]{1,0:T(8,128)(2,1)S(1)}, bf16[384,384]{1,0:T(8,128)(2,1)}, u32[]{:S(2)}) copy-start(bf16[384,384]{1,0:T(8,128)(2,1)} %get-tuple-element.29.refs_0_) | copy-start | bytes 884740
  95.9 8.1 %collective-permute-start.7 = (bf16[2,256,384]{2,1,0:T(8,128)(2,1)S(1)}, bf16[2,256,384]{2,1,0:T(8,128)(2,1)S(1)}, u32[]{:S(2)}, u32[]{:S(2)}) collective-permute-start(bf16[2,256,384]{2,1,0:T(8,128)(2,1)S(1)} %shard_map.70), channel_id=1, source_target_pairs={{0,16},{16,0},{32,48},{48,32},{64,80},{80,64},{96,112},{112,96},{1... | collective-permute-start | bytes 1179656 | tf_op jit(solution)/shard_map/ppermute | solution.py:287
  100.1 4.6 %copy-start.9 = (bf16[384,384]{1,0:T(8,128)(2,1)}, bf16[384,384]{1,0:T(8,128)(2,1)S(1)}, u32[]{:S(2)}) copy-start(bf16[384,384]{1,0:T(8,128)(2,1)S(1)} %get-tuple-element.52) | copy-start | bytes 884740
  100.1 4.6 %copy-start.10 = (bf16[384,384]{1,0:T(8,128)(2,1)}, bf16[384,384]{1,0:T(8,128)(2,1)S(1)}, u32[]{:S(2)}) copy-start(bf16[384,384]{1,0:T(8,128)(2,1)S(1)} %get-tuple-element.50) | copy-start | bytes 884740
  100.1 18.1 %collective-permute-start.8 = (bf16[384,384]{1,0:T(8,128)(2,1)}, bf16[384,384]{1,0:T(8,128)(2,1)}, u32[]{:S(2)}, u32[]{:S(2)}) collective-permute-start(bf16[384,384]{1,0:T(8,128)(2,1)} %get-tuple-element.47), channel_id=1, source_target_pairs={{0,8},{1,9},{2,10},{3,11},{4,12},{5,13},{6,14},{7,15},{8,0},{9,1},... | collective-permute-start | bytes 884744 | tf_op jit(solution)/shard_map/ppermute | solution.py:296
  104.8 0.8 copy-start.6
  105.5 38.7 %all-to-all-start.2 = ((bf16[32,16,384]{2,1,0:T(8,128)(2,1)}), bf16[32,16,384]{2,1,0:T(8,128)(2,1)S(1)}, u32[]{:S(2)}, u32[]{:S(2)}) async-start(bf16[32,16,384]{2,1,0:T(8,128)(2,1)} %bitcast.28), calls=%async_computation.2 | async-start | bytes 786432 | tf_op jit(solution)/shard_map/all_to_all | solution.py:318
  118.2 17.8 %collective-permute-start.9 = (bf16[384,384]{1,0:T(8,128)(2,1)}, bf16[384,384]{1,0:T(8,128)(2,1)S(1)}, u32[]{:S(2)}, u32[]{:S(2)}) collective-permute-start(bf16[384,384]{1,0:T(8,128)(2,1)} %copy-done.10), channel_id=1, source_target_pairs={{0,32},{16,48},{32,0},{48,16},{64,96},{80,112},{96,64},{112,80},{1... | collective-permute-start | bytes 884744 | tf_op jit(solution)/shard_map/ppermute | solution.py:305
  121.7 20.6 %collective-permute-start.10 = (bf16[384,384]{1,0:T(8,128)(2,1)}, bf16[384,384]{1,0:T(8,128)(2,1)S(1)}, u32[]{:S(2)}, u32[]{:S(2)}) collective-permute-start(bf16[384,384]{1,0:T(8,128)(2,1)} %copy-done.9), channel_id=1, source_target_pairs={{0,40},{1,41},{2,42},{3,43},{4,44},{5,45},{6,46},{7,47},{8,32},{9,... | collective-permute-start | bytes 884744 | tf_op jit(solution)/shard_map/ppermute | solution.py:306

commit v10 on v6

--- a/solution.py
+++ b/solution.py
@@ -30,7 +30,7 @@
 HBM = pl.BlockSpec(memory_space=pltpu.HBM)
 
 
-def project(start_ref, tok_hbm, codes_hbm, scales_hbm, w_ref, out_hbm, tok_ref, codes_ref, scales_ref, out_ref, sems):
+def project(start_ref, tok_hbm, codes_hbm, scales_hbm, w_hbm, out_hbm, tok_ref, codes_ref, scales_ref, w_ref, out_ref, sems):
     feat, units = codes_ref.shape
     cuts = [(z, y) for z in range(2) for y in (0, 1)]
     span = tok_ref.shape[1] // 2
@@ -56,7 +56,8 @@
         scale = jnp.where(row >= i * BLOCK, scales_ref[i : i + 1, :], scale)
     weight = (codes_ref[...].astype(F32) * scale).astype(BF16)
     w_ref[...] = weight
-    stores = []
+    stores = [pltpu.make_async_copy(w_ref, w_hbm, sems.at[10])]
+    stores[0].start()
     for i, ((z, y), copy) in enumerate(zip(cuts, loads)):
         copy.wait()
         ys = slice(y * span, (y + 1) * span)
@@ -172,13 +173,14 @@
             jax.ShapeDtypeStruct((2, ys, 2, per, sub, units), BF16),
         ],
         in_specs=[SMEM, HBM, HBM, HBM],
-        out_specs=[VMEM, HBM],
+        out_specs=[HBM, HBM],
         scratch_shapes=[
             pltpu.VMEM(tok.shape, BF16),
             pltpu.VMEM(codes.shape, BF16),
             pltpu.VMEM(scales.shape, F32),
+            pltpu.VMEM(codes.shape, BF16),
             pltpu.VMEM((2, ys, 2, per, sub, units), BF16),
-            pltpu.SemaphoreType.DMA((10,)),
+            pltpu.SemaphoreType.DMA((11,)),
         ],
         compiler_params=pltpu.CompilerParams(vmem_limit_bytes=58 * 2**20),
         cost_estimate=pl.CostEstimate(flops=flops, bytes_accessed=2 * size, transcendentals=0),

time: 135 us -> 134 us (level)
  no operation moved by 1% of the time
where the time goes in v10:
time: 134 us; the launch traced here: 132 us
  starting transfers between devices  61.3 us (46%)
  waiting for transfers between devices  31.8 us (24%)
  blocking collectives  26.3 us (20%)
  Pallas kernels  9.02 us (7%)
  local copies, waits for them, and re-layouts  3.08 us (2%)
    all_gather x1, blocking collectives, shards(): lax.all_gather(slope.reshape(2 * mine, units), 'local', axis=0, tiled=Tru...  26.3 us
    all_to_all x1, starting transfers between devices, shards(): lax.all_to_all(both.reshape(nodes, sub, feat), ('node', 'local'), 0, 0, a...  20.5 us
    ppermute x1, starting transfers between devices, shards(): lax.ppermute(lax.dynamic_index_in_dim(tok, 1 - side[0], 3, False), ('node...  15.9 us
    ppermute x1, waiting for transfers between devices, shards(): act_far = lax.ppermute(act_far, 'local', pair)  12 us
    ppermute x1, waiting for transfers between devices, shards(): lax.ppermute(lax.dynamic_index_in_dim(cot, 1 - side[0], 1, False), 'local...  11.6 us
    all_to_all x1, starting transfers between devices, shards(): lax.all_to_all(partial.reshape(locals_, 2 * mine, units), 'local', 0, 0,...  10.5 us
    pallas_call x6, Pallas kernels, call(): pl.pallas_call(kernel, out_shape=[jax.ShapeDtypeStruct(s, d) for s, d in...  5.32 us
    all_to_all x1, waiting for transfers between devices, shards(): lax.all_to_all(both.reshape(nodes, sub, feat), ('node', 'local'), 0, 0, a...  4.69 us
  transfers between devices with their start and end apart: 8, of which 4 were waited for; matrix products, arithmetic and copies ran while one was open for 1% of the time, Pallas kernels for 3%

profile of v10, /device:TPU:14, one launch (start us, length us, event | category | flops | bytes accessed | tf_op | source)
XLA Modules:
  0.0 132.4 jit_solution(10562453975189776138)
XLA Ops:
  0.6 3.7 %shard_map.67 = (bf16[384,384]{1,0:T(8,128)(2,1)}, bf16[2,8,2,4,16,384]{5,4,3,2,1,0:T(8,128)(2,1)}) custom-call(s32[1]{0:T(128)} %bitcast.1.start_ref, bf16[2,8,4,2,16,384]{5,4,3,2,1,0:T(8,128)(2,1)} %bitcast.26, bf16[384,384]{1,0:T(8,128)(2,1)} %codes_hbm.1, f32[3,384]{1,0:T(4,128)} %scales_hbm.1), custom_call_target="tpu_custom_call" | custom-call | flops 603979776 | bytes 3145728 | tf_op jit(solution)/shard_map/pallas_call | solution.py:169
  4.3 0.0 copy-start.1
  4.4 10.5 %all-to-all-start = ((bf16[16,128,384]{2,1,0:T(8,128)(2,1)}), bf16[16,128,384]{2,1,0:T(8,128)(2,1)S(1)}, u32[]{:S(2)}, u32[]{:S(2)}) async-start(bf16[16,128,384]{2,1,0:T(8,128)(2,1)} %bitcast.32), calls=%async_computation | async-start | bytes 3145728 | tf_op jit(solution)/shard_map/all_to_all | solution.py:188
  14.9 0.0 copy-start
  14.9 0.0 copy-start.3
  14.9 1.0 dynamic-slice_bitcast_fusion
  15.9 15.9 %collective-permute-start.2 = (bf16[2,8,4,16,384]{4,3,2,1,0:T(8,128)(2,1)}, bf16[2,8,4,16,384]{4,3,2,1,0:T(8,128)(2,1)S(1)}, u32[]{:S(2)}, u32[]{:S(2)}) collective-permute-start(bf16[2,8,4,16,384]{4,3,2,1,0:T(8,128)(2,1)} %dynamic-slice_bitcast_fusion), channel_id=1, source_target_pairs={{0,776},{1,777},{2,778},{3,779},{4,780},{5,781},{6,782},{7,783},{8... | collective-permute-start | bytes 2359304 | tf_op jit(solution)/shard_map/ppermute | solution.py:201
  31.9 0.0 copy-done
  31.9 1.9 %collective-permute-start.1 = (bf16[384,384]{1,0:T(8,128)(2,1)S(1)}, bf16[384,384]{1,0:T(8,128)(2,1)S(1)}, u32[]{:S(2)}, u32[]{:S(2)}) collective-permute-start(bf16[384,384]{1,0:T(8,128)(2,1)S(1)} %copy-done), channel_id=1, source_target_pairs={{0,8},{1,9},{2,10},{3,11},{4,12},{5,13},{6,14},{7,15},{8,0},{9,1},... | collective-permute-start | bytes 884744 | tf_op jit(solution)/shard_map/ppermute | solution.py:194
  33.9 3.9 %collective-permute-start = (bf16[4,16,384]{2,1,0:T(8,128)(2,1)S(1)}, bf16[4,16,384]{2,1,0:T(8,128)(2,1)S(1)}, u32[]{:S(2)}, u32[]{:S(2)}) collective-permute-start(bf16[4,16,384]{2,1,0:T(8,128)(2,1)S(1)} %dynamic-slice_bitcast_fusion.1), channel_id=1, source_target_pairs={{0,8},{1,9},{2,10},{3,11},{4,12},{5,13},{6,14},{7,15},{8,0},{9,1},... | collective-permute-start | bytes 147464 | tf_op jit(solution)/shard_map/ppermute | solution.py:191
  37.8 11.6 %collective-permute-done.far_cot_ref = bf16[4,16,384]{2,1,0:T(8,128)(2,1)S(1)} collective-permute-done((bf16[4,16,384]{2,1,0:T(8,128)(2,1)S(1)}, bf16[4,16,384]{2,1,0:T(8,128)(2,1)S(1)}, u32[]{:S(2)}, u32[]{:S(2)}) %collective-permute-start) | collective-permute-done | bytes 49184 | tf_op jit(solution)/shard_map/ppermute | solution.py:191
  49.4 0.0 collective-permute-done.1.far_w_ref
  49.4 0.0 collective-permute-done.2.far_tok_ref
  49.4 3.6 %all-to-all-done = bf16[16,128,384]{2,1,0:T(8,128)(2,1)S(1)} async-done(((bf16[16,128,384]{2,1,0:T(8,128)(2,1)}), bf16[16,128,384]{2,1,0:T(8,128)(2,1)S(1)}, u32[]{:S(2)}, u32[]{:S(2)}) %all-to-all-start) | async-done | bytes 1572896 | tf_op jit(solution)/shard_map/all_to_all | solution.py:188
  53.0 0.4 shard_map.68
  53.3 26.3 %all_gather.3 = bf16[1024,384]{1,0:T(8,128)(2,1)S(1)} all-gather(bf16[128,384]{1,0:T(8,128)(2,1)S(1)} %bitcast.31), channel_id=1, replica_groups={{0,1,2,3,4,5,6,7},{8,9,10,11,12,13,14,15},{16,17,18,19,20,21,22,23},{24..., dimensions={0}, use_global_device_ids=true | all-gather | bytes 884736 | tf_op jit(solution)/shard_map/all_gather | solution.py:215
  79.6 0.7 shard_map.69
  80.3 1.9 %collective-permute-start.3 = (bf16[2,512,384]{2,1,0:T(8,128)(2,1)S(1)}, bf16[2,512,384]{2,1,0:T(8,128)(2,1)S(1)}, u32[]{:S(2)}, u32[]{:S(2)}) collective-permute-start(bf16[2,512,384]{2,1,0:T(8,128)(2,1)S(1)} %shard_map.69), channel_id=1, source_target_pairs={{0,16},{16,0},{32,48},{48,32},{64,80},{80,64},{96,112},{112,96},{1... | collective-permute-start | bytes 2359304 | tf_op jit(solution)/shard_map/ppermute | solution.py:227
  82.2 0.6 shard_map.72
  82.8 3.1 %collective-permute-start.5 = (bf16[384,384]{1,0:T(8,128)(2,1)S(1)}, bf16[384,384]{1,0:T(8,128)(2,1)S(1)}, u32[]{:S(2)}, u32[]{:S(2)}) collective-permute-start(bf16[384,384]{1,0:T(8,128)(2,1)S(1)} %shard_map.72), channel_id=1, source_target_pairs={{0,8},{1,9},{2,10},{3,11},{4,12},{5,13},{6,14},{7,15},{8,0},{9,1},... | collective-permute-start | bytes 884744 | tf_op jit(solution)/shard_map/ppermute | solution.py:231
  85.9 0.0 collective-permute-done.3.other_ref
  86.0 1.6 %shard_map.70 = bf16[2,2,2,4,2,16,384]{6,5,4,3,2,1,0:T(8,128)(2,1)} custom-call(s32[1]{0:T(128)} %bitcast.8.core_ref, s32[1]{0:T(128)} %bitcast.side_ref, bf16[8,2,2,2,16,384]{5,4,3,2,1,0:T(8,128)(2,1)S(1)} %bitcast.22, bf16[384,384]{1,0:T(8,128)(2,1)S(1)} %copy-done, bf16[384,384]{1,0:T(8,128)(2,1)S(1)} %collective-permute-done.1.far_w_ref, ...), custom_call_target="tpu_custom_call" | custom-call | flops 301989888 | bytes 1572864 | tf_op jit(solution)/shard_map/pallas_call | solution.py:20
  87.5 20.5 %all-to-all-start.1 = ((bf16[64,16,384]{2,1,0:T(8,128)(2,1)}), bf16[64,16,384]{2,1,0:T(8,128)(2,1)S(1)}, u32[]{:S(2)}, u32[]{:S(2)}) async-start(bf16[64,16,384]{2,1,0:T(8,128)(2,1)} %bitcast.14), calls=%async_computation.1 | async-start | bytes 1572864 | tf_op jit(solution)/shard_map/all_to_all | solution.py:252
  108.0 3.4 %collective-permute-start.4 = (bf16[64,384]{1,0:T(8,128)(2,1)S(1)}, bf16[64,384]{1,0:T(8,128)(2,1)S(1)}, u32[]{:S(2)}, u32[]{:S(2)}) collective-permute-start(bf16[64,384]{1,0:T(8,128)(2,1)S(1)} %get-tuple-element.22), channel_id=1, source_target_pairs={{0,8},{1,9},{2,10},{3,11},{4,12},{5,13},{6,14},{7,15},{8,0},{9,1},... | collective-permute-start | bytes 147464 | tf_op jit(solution)/shard_map/ppermute | solution.py:266
  111.4 0.0 collective-permute-done.5.far_ref
  111.4 0.0 copy-start.2
  111.5 1.4 %copy-done.2 = bf16[2048,384]{1,0:T(8,128)(2,1)S(1)} copy-done((bf16[2048,384]{1,0:T(8,128)(2,1)S(1)}, bf16[2048,384]{1,0:T(8,128)(2,1)}, u32[]{:S(2)}) %copy-start.2) | copy-done | bytes 1572888
  112.9 1.4 %shard_map.73 = f32[384,384]{1,0:T(8,128)} custom-call(s32[1]{0:T(128)} %bitcast.side_ref, bf16[2,8,4,2,16,384]{5,4,3,2,1,0:T(8,128)(2,1)S(1)} %bitcast.28, bf16[8,2,4,16,384]{4,3,2,1,0:T(8,128)(2,1)S(1)} %bitcast.23, bf16[384,384]{1,0:T(8,128)(2,1)S(1)} %collective-permute-done.5.far_ref), custom_call_target="tpu_custom_call" | custom-call | flops 12079595520 | bytes 1572864 | tf_op jit(solution)/shard_map/pallas_call | solution.py:20
  114.3 12.0 %collective-permute-done.4 = bf16[64,384]{1,0:T(8,128)(2,1)S(1)} collective-permute-done((bf16[64,384]{1,0:T(8,128)(2,1)S(1)}, bf16[64,384]{1,0:T(8,128)(2,1)S(1)}, u32[]{:S(2)}, u32[]{:S(2)}) %collective-permute-start.4) | collective-permute-done | bytes 49184 | tf_op jit(solution)/shard_map/ppermute | solution.py:266
  126.3 0.7 copy.7
  126.9 4.7 %all-to-all-done.1 = bf16[64,16,384]{2,1,0:T(8,128)(2,1)S(1)} async-done(((bf16[64,16,384]{2,1,0:T(8,128)(2,1)}), bf16[64,16,384]{2,1,0:T(8,128)(2,1)S(1)}, u32[]{:S(2)}, u32[]{:S(2)}) %all-to-all-start.1) | async-done | bytes 786464 | tf_op jit(solution)/shard_map/all_to_all | solution.py:252
  131.6 0.7 shard_map.71
  (5 shorter events, 0.1 us)
Async XLA Ops:
  4.3 10.6 %copy-start.1 = (bf16[2048,384]{1,0:T(8,128)(2,1)S(1)}, bf16[2048,384]{1,0:T(8,128)(2,1)}, u32[]{:S(2)}) copy-start(bf16[2048,384]{1,0:T(8,128)(2,1)} %param.4) | copy-start | bytes 4718596
  4.4 48.6 %all-to-all-start = ((bf16[16,128,384]{2,1,0:T(8,128)(2,1)}), bf16[16,128,384]{2,1,0:T(8,128)(2,1)S(1)}, u32[]{:S(2)}, u32[]{:S(2)}) async-start(bf16[16,128,384]{2,1,0:T(8,128)(2,1)} %bitcast.32), calls=%async_computation | async-start | bytes 3145728 | tf_op jit(solution)/shard_map/all_to_all | solution.py:188
  14.9 17.0 %copy-start = (bf16[384,384]{1,0:T(8,128)(2,1)S(1)}, bf16[384,384]{1,0:T(8,128)(2,1)}, u32[]{:S(2)}) copy-start(bf16[384,384]{1,0:T(8,128)(2,1)} %get-tuple-element.15.w_ref) | copy-start | bytes 884740
  14.9 18.9 %copy-start.3 = (bf16[128,384]{1,0:T(8,128)(2,1)S(1)}, bf16[128,384]{1,0:T(8,128)(2,1)}, u32[]{:S(2)}) copy-start(bf16[128,384]{1,0:T(8,128)(2,1)} %param.7) | copy-start | bytes 294916
  15.9 33.4 %collective-permute-start.2 = (bf16[2,8,4,16,384]{4,3,2,1,0:T(8,128)(2,1)}, bf16[2,8,4,16,384]{4,3,2,1,0:T(8,128)(2,1)S(1)}, u32[]{:S(2)}, u32[]{:S(2)}) collective-permute-start(bf16[2,8,4,16,384]{4,3,2,1,0:T(8,128)(2,1)} %dynamic-slice_bitcast_fusion), channel_id=1, source_target_pairs={{0,776},{1,777},{2,778},{3,779},{4,780},{5,781},{6,782},{7,783},{8... | collective-permute-start | bytes 2359304 | tf_op jit(solution)/shard_map/ppermute | solution.py:201
  31.9 17.5 %collective-permute-start.1 = (bf16[384,384]{1,0:T(8,128)(2,1)S(1)}, bf16[384,384]{1,0:T(8,128)(2,1)S(1)}, u32[]{:S(2)}, u32[]{:S(2)}) collective-permute-start(bf16[384,384]{1,0:T(8,128)(2,1)S(1)} %copy-done), channel_id=1, source_target_pairs={{0,8},{1,9},{2,10},{3,11},{4,12},{5,13},{6,14},{7,15},{8,0},{9,1},... | collective-permute-start | bytes 884744 | tf_op jit(solution)/shard_map/ppermute | solution.py:194
  33.9 15.5 %collective-permute-start = (bf16[4,16,384]{2,1,0:T(8,128)(2,1)S(1)}, bf16[4,16,384]{2,1,0:T(8,128)(2,1)S(1)}, u32[]{:S(2)}, u32[]{:S(2)}) collective-permute-start(bf16[4,16,384]{2,1,0:T(8,128)(2,1)S(1)} %dynamic-slice_bitcast_fusion.1), channel_id=1, source_target_pairs={{0,8},{1,9},{2,10},{3,11},{4,12},{5,13},{6,14},{7,15},{8,0},{9,1},... | collective-permute-start | bytes 147464 | tf_op jit(solution)/shard_map/ppermute | solution.py:191
  80.3 5.7 %collective-permute-start.3 = (bf16[2,512,384]{2,1,0:T(8,128)(2,1)S(1)}, bf16[2,512,384]{2,1,0:T(8,128)(2,1)S(1)}, u32[]{:S(2)}, u32[]{:S(2)}) collective-permute-start(bf16[2,512,384]{2,1,0:T(8,128)(2,1)S(1)} %shard_map.69), channel_id=1, source_target_pairs={{0,16},{16,0},{32,48},{48,32},{64,80},{80,64},{96,112},{112,96},{1... | collective-permute-start | bytes 2359304 | tf_op jit(solution)/shard_map/ppermute | solution.py:227
  82.8 28.6 %collective-permute-start.5 = (bf16[384,384]{1,0:T(8,128)(2,1)S(1)}, bf16[384,384]{1,0:T(8,128)(2,1)S(1)}, u32[]{:S(2)}, u32[]{:S(2)}) collective-permute-start(bf16[384,384]{1,0:T(8,128)(2,1)S(1)} %shard_map.72), channel_id=1, source_target_pairs={{0,8},{1,9},{2,10},{3,11},{4,12},{5,13},{6,14},{7,15},{8,0},{9,1},... | collective-permute-start | bytes 884744 | tf_op jit(solution)/shard_map/ppermute | solution.py:231
  87.5 44.1 %all-to-all-start.1 = ((bf16[64,16,384]{2,1,0:T(8,128)(2,1)}), bf16[64,16,384]{2,1,0:T(8,128)(2,1)S(1)}, u32[]{:S(2)}, u32[]{:S(2)}) async-start(bf16[64,16,384]{2,1,0:T(8,128)(2,1)} %bitcast.14), calls=%async_computation.1 | async-start | bytes 1572864 | tf_op jit(solution)/shard_map/all_to_all | solution.py:252
  108.0 18.2 %collective-permute-start.4 = (bf16[64,384]{1,0:T(8,128)(2,1)S(1)}, bf16[64,384]{1,0:T(8,128)(2,1)S(1)}, u32[]{:S(2)}, u32[]{:S(2)}) collective-permute-start(bf16[64,384]{1,0:T(8,128)(2,1)S(1)} %get-tuple-element.22), channel_id=1, source_target_pairs={{0,8},{1,9},{2,10},{3,11},{4,12},{5,13},{6,14},{7,15},{8,0},{9,1},... | collective-permute-start | bytes 147464 | tf_op jit(solution)/shard_map/ppermute | solution.py:266
  111.4 1.4 %copy-start.2 = (bf16[2048,384]{1,0:T(8,128)(2,1)S(1)}, bf16[2048,384]{1,0:T(8,128)(2,1)}, u32[]{:S(2)}) copy-start(bf16[2048,384]{1,0:T(8,128)(2,1)} %param.4) | copy-start | bytes 4718596

commit v11 on v10

--- a/solution.py
+++ b/solution.py
@@ -32,8 +32,8 @@
 
 def project(start_ref, tok_hbm, codes_hbm, scales_hbm, w_hbm, out_hbm, tok_ref, codes_ref, scales_ref, w_ref, out_ref, sems):
     feat, units = codes_ref.shape
-    cuts = [(z, y) for z in range(2) for y in (0, 1)]
-    span = tok_ref.shape[1] // 2
+    cuts = [(z, y) for z in range(2) for y in range(4)]
+    span = tok_ref.shape[1] // 4
     first = [
         pltpu.make_async_copy(codes_hbm, codes_ref, sems.at[0]),
         pltpu.make_async_copy(scales_hbm, scales_ref, sems.at[1]),
@@ -56,7 +56,7 @@
         scale = jnp.where(row >= i * BLOCK, scales_ref[i : i + 1, :], scale)
     weight = (codes_ref[...].astype(F32) * scale).astype(BF16)
     w_ref[...] = weight
-    stores = [pltpu.make_async_copy(w_ref, w_hbm, sems.at[10])]
+    stores = [pltpu.make_async_copy(w_ref, w_hbm, sems.at[18])]
     stores[0].start()
     for i, ((z, y), copy) in enumerate(zip(cuts, loads)):
         copy.wait()
@@ -68,7 +68,7 @@
             out_ref[h, ys, z] = res[:, :, h]
         part = pl.ds(y * span, span)
         store = pltpu.make_async_copy(
-            out_ref.at[:, part, z], out_hbm.at[:, part, z], sems.at[6 + i]
+            out_ref.at[:, part, z], out_hbm.at[:, part, z], sems.at[10 + i]
         )
         store.start()
         stores.append(store)
@@ -180,7 +180,7 @@
             pltpu.VMEM(scales.shape, F32),
             pltpu.VMEM(codes.shape, BF16),
             pltpu.VMEM((2, ys, 2, per, sub, units), BF16),
-            pltpu.SemaphoreType.DMA((11,)),
+            pltpu.SemaphoreType.DMA((19,)),
         ],
         compiler_params=pltpu.CompilerParams(vmem_limit_bytes=58 * 2**20),
         cost_estimate=pl.CostEstimate(flops=flops, bytes_accessed=2 * size, transcendentals=0),

time: 134 us -> 134 us (level)
  no operation moved by 1% of the time
where the time goes in v11:
time: 134 us; the launch traced here: 133 us
  starting transfers between devices  61.3 us (46%)
  waiting for transfers between devices  31.8 us (24%)
  blocking collectives  26.3 us (20%)
  Pallas kernels  9.6 us (7%)
  local copies, waits for them, and re-layouts  3.08 us (2%)
    all_gather x1, blocking collectives, shards(): lax.all_gather(slope.reshape(2 * mine, units), 'local', axis=0, tiled=Tru...  26.3 us
    all_to_all x1, starting transfers between devices, shards(): lax.all_to_all(both.reshape(nodes, sub, feat), ('node', 'local'), 0, 0, a...  20.5 us
    ppermute x1, starting transfers between devices, shards(): lax.ppermute(lax.dynamic_index_in_dim(tok, 1 - side[0], 3, False), ('node...  15.9 us
    ppermute x1, waiting for transfers between devices, shards(): act_far = lax.ppermute(act_far, 'local', pair)  12 us
    ppermute x1, waiting for transfers between devices, shards(): lax.ppermute(lax.dynamic_index_in_dim(cot, 1 - side[0], 1, False), 'local...  11.6 us
    all_to_all x1, starting transfers between devices, shards(): lax.all_to_all(partial.reshape(locals_, 2 * mine, units), 'local', 0, 0,...  10.5 us
    pallas_call x6, Pallas kernels, call(): pl.pallas_call(kernel, out_shape=[jax.ShapeDtypeStruct(s, d) for s, d in...  5.32 us
    all_to_all x1, waiting for transfers between devices, shards(): lax.all_to_all(both.reshape(nodes, sub, feat), ('node', 'local'), 0, 0, a...  4.7 us
  transfers between devices with their start and end apart: 8, of which 4 were waited for; matrix products, arithmetic and copies ran while one was open for 1% of the time, Pallas kernels for 3%

profile of v11, /device:TPU:14, one launch (start us, length us, event | category | flops | bytes accessed | tf_op | source)
XLA Modules:
  0.0 132.9 jit_solution(5501089351389616315)
XLA Ops:
  0.6 4.3 %shard_map.67 = (bf16[384,384]{1,0:T(8,128)(2,1)}, bf16[2,8,2,4,16,384]{5,4,3,2,1,0:T(8,128)(2,1)}) custom-call(s32[1]{0:T(128)} %bitcast.1.start_ref, bf16[2,8,4,2,16,384]{5,4,3,2,1,0:T(8,128)(2,1)} %bitcast.26, bf16[384,384]{1,0:T(8,128)(2,1)} %codes_hbm.1, f32[3,384]{1,0:T(4,128)} %scales_hbm.1), custom_call_target="tpu_custom_call" | custom-call | flops 603979776 | bytes 3145728 | tf_op jit(solution)/shard_map/pallas_call | solution.py:169
  4.9 0.0 copy-start.1
  4.9 10.5 %all-to-all-start = ((bf16[16,128,384]{2,1,0:T(8,128)(2,1)}), bf16[16,128,384]{2,1,0:T(8,128)(2,1)S(1)}, u32[]{:S(2)}, u32[]{:S(2)}) async-start(bf16[16,128,384]{2,1,0:T(8,128)(2,1)} %bitcast.32), calls=%async_computation | async-start | bytes 3145728 | tf_op jit(solution)/shard_map/all_to_all | solution.py:188
  15.5 0.0 copy-start
  15.5 0.0 copy-start.3
  15.5 0.0 copy-done.1
  15.5 1.0 dynamic-slice_bitcast_fusion
  16.5 15.9 %collective-permute-start.2 = (bf16[2,8,4,16,384]{4,3,2,1,0:T(8,128)(2,1)}, bf16[2,8,4,16,384]{4,3,2,1,0:T(8,128)(2,1)S(1)}, u32[]{:S(2)}, u32[]{:S(2)}) collective-permute-start(bf16[2,8,4,16,384]{4,3,2,1,0:T(8,128)(2,1)} %dynamic-slice_bitcast_fusion), channel_id=1, source_target_pairs={{0,776},{1,777},{2,778},{3,779},{4,780},{5,781},{6,782},{7,783},{8... | collective-permute-start | bytes 2359304 | tf_op jit(solution)/shard_map/ppermute | solution.py:201
  32.5 1.9 %collective-permute-start.1 = (bf16[384,384]{1,0:T(8,128)(2,1)S(1)}, bf16[384,384]{1,0:T(8,128)(2,1)S(1)}, u32[]{:S(2)}, u32[]{:S(2)}) collective-permute-start(bf16[384,384]{1,0:T(8,128)(2,1)S(1)} %copy-done), channel_id=1, source_target_pairs={{0,8},{1,9},{2,10},{3,11},{4,12},{5,13},{6,14},{7,15},{8,0},{9,1},... | collective-permute-start | bytes 884744 | tf_op jit(solution)/shard_map/ppermute | solution.py:194
  34.4 3.9 %collective-permute-start = (bf16[4,16,384]{2,1,0:T(8,128)(2,1)S(1)}, bf16[4,16,384]{2,1,0:T(8,128)(2,1)S(1)}, u32[]{:S(2)}, u32[]{:S(2)}) collective-permute-start(bf16[4,16,384]{2,1,0:T(8,128)(2,1)S(1)} %dynamic-slice_bitcast_fusion.1), channel_id=1, source_target_pairs={{0,8},{1,9},{2,10},{3,11},{4,12},{5,13},{6,14},{7,15},{8,0},{9,1},... | collective-permute-start | bytes 147464 | tf_op jit(solution)/shard_map/ppermute | solution.py:191
  38.4 11.6 %collective-permute-done.far_cot_ref = bf16[4,16,384]{2,1,0:T(8,128)(2,1)S(1)} collective-permute-done((bf16[4,16,384]{2,1,0:T(8,128)(2,1)S(1)}, bf16[4,16,384]{2,1,0:T(8,128)(2,1)S(1)}, u32[]{:S(2)}, u32[]{:S(2)}) %collective-permute-start) | collective-permute-done | bytes 49184 | tf_op jit(solution)/shard_map/ppermute | solution.py:191
  49.9 0.0 collective-permute-done.1.far_w_ref
  49.9 0.0 collective-permute-done.2.far_tok_ref
  50.0 3.6 %all-to-all-done = bf16[16,128,384]{2,1,0:T(8,128)(2,1)S(1)} async-done(((bf16[16,128,384]{2,1,0:T(8,128)(2,1)}), bf16[16,128,384]{2,1,0:T(8,128)(2,1)S(1)}, u32[]{:S(2)}, u32[]{:S(2)}) %all-to-all-start) | async-done | bytes 1572896 | tf_op jit(solution)/shard_map/all_to_all | solution.py:188
  53.5 0.4 shard_map.68
  53.9 26.3 %all_gather.3 = bf16[1024,384]{1,0:T(8,128)(2,1)S(1)} all-gather(bf16[128,384]{1,0:T(8,128)(2,1)S(1)} %bitcast.31), channel_id=1, replica_groups={{0,1,2,3,4,5,6,7},{8,9,10,11,12,13,14,15},{16,17,18,19,20,21,22,23},{24..., dimensions={0}, use_global_device_ids=true | all-gather | bytes 884736 | tf_op jit(solution)/shard_map/all_gather | solution.py:215
  80.2 0.7 shard_map.69
  80.8 1.9 %collective-permute-start.3 = (bf16[2,512,384]{2,1,0:T(8,128)(2,1)S(1)}, bf16[2,512,384]{2,1,0:T(8,128)(2,1)S(1)}, u32[]{:S(2)}, u32[]{:S(2)}) collective-permute-start(bf16[2,512,384]{2,1,0:T(8,128)(2,1)S(1)} %shard_map.69), channel_id=1, source_target_pairs={{0,16},{16,0},{32,48},{48,32},{64,80},{80,64},{96,112},{112,96},{1... | collective-permute-start | bytes 2359304 | tf_op jit(solution)/shard_map/ppermute | solution.py:227
  82.8 0.6 shard_map.72
  83.4 3.1 %collective-permute-start.5 = (bf16[384,384]{1,0:T(8,128)(2,1)S(1)}, bf16[384,384]{1,0:T(8,128)(2,1)S(1)}, u32[]{:S(2)}, u32[]{:S(2)}) collective-permute-start(bf16[384,384]{1,0:T(8,128)(2,1)S(1)} %shard_map.72), channel_id=1, source_target_pairs={{0,8},{1,9},{2,10},{3,11},{4,12},{5,13},{6,14},{7,15},{8,0},{9,1},... | collective-permute-start | bytes 884744 | tf_op jit(solution)/shard_map/ppermute | solution.py:231
  86.5 0.0 collective-permute-done.3.other_ref
  86.5 1.6 %shard_map.70 = bf16[2,2,2,4,2,16,384]{6,5,4,3,2,1,0:T(8,128)(2,1)} custom-call(s32[1]{0:T(128)} %bitcast.8.core_ref, s32[1]{0:T(128)} %bitcast.side_ref, bf16[8,2,2,2,16,384]{5,4,3,2,1,0:T(8,128)(2,1)S(1)} %bitcast.22, bf16[384,384]{1,0:T(8,128)(2,1)S(1)} %copy-done, bf16[384,384]{1,0:T(8,128)(2,1)S(1)} %collective-permute-done.1.far_w_ref, ...), custom_call_target="tpu_custom_call" | custom-call | flops 301989888 | bytes 1572864 | tf_op jit(solution)/shard_map/pallas_call | solution.py:20
  88.1 20.5 %all-to-all-start.1 = ((bf16[64,16,384]{2,1,0:T(8,128)(2,1)}), bf16[64,16,384]{2,1,0:T(8,128)(2,1)S(1)}, u32[]{:S(2)}, u32[]{:S(2)}) async-start(bf16[64,16,384]{2,1,0:T(8,128)(2,1)} %bitcast.14), calls=%async_computation.1 | async-start | bytes 1572864 | tf_op jit(solution)/shard_map/all_to_all | solution.py:252
  108.6 3.4 %collective-permute-start.4 = (bf16[64,384]{1,0:T(8,128)(2,1)S(1)}, bf16[64,384]{1,0:T(8,128)(2,1)S(1)}, u32[]{:S(2)}, u32[]{:S(2)}) collective-permute-start(bf16[64,384]{1,0:T(8,128)(2,1)S(1)} %get-tuple-element.22), channel_id=1, source_target_pairs={{0,8},{1,9},{2,10},{3,11},{4,12},{5,13},{6,14},{7,15},{8,0},{9,1},... | collective-permute-start | bytes 147464 | tf_op jit(solution)/shard_map/ppermute | solution.py:266
  112.0 0.0 collective-permute-done.5.far_ref
  112.0 0.0 copy-start.2
  112.0 1.4 %copy-done.2 = bf16[2048,384]{1,0:T(8,128)(2,1)S(1)} copy-done((bf16[2048,384]{1,0:T(8,128)(2,1)S(1)}, bf16[2048,384]{1,0:T(8,128)(2,1)}, u32[]{:S(2)}) %copy-start.2) | copy-done | bytes 1572888
  113.4 1.4 %shard_map.73 = f32[384,384]{1,0:T(8,128)} custom-call(s32[1]{0:T(128)} %bitcast.side_ref, bf16[2,8,4,2,16,384]{5,4,3,2,1,0:T(8,128)(2,1)S(1)} %bitcast.28, bf16[8,2,4,16,384]{4,3,2,1,0:T(8,128)(2,1)S(1)} %bitcast.23, bf16[384,384]{1,0:T(8,128)(2,1)S(1)} %collective-permute-done.5.far_ref), custom_call_target="tpu_custom_call" | custom-call | flops 12079595520 | bytes 1572864 | tf_op jit(solution)/shard_map/pallas_call | solution.py:20
  114.9 12.0 %collective-permute-done.4 = bf16[64,384]{1,0:T(8,128)(2,1)S(1)} collective-permute-done((bf16[64,384]{1,0:T(8,128)(2,1)S(1)}, bf16[64,384]{1,0:T(8,128)(2,1)S(1)}, u32[]{:S(2)}, u32[]{:S(2)}) %collective-permute-start.4) | collective-permute-done | bytes 49184 | tf_op jit(solution)/shard_map/ppermute | solution.py:266
  126.9 0.7 copy.7
  127.5 4.7 %all-to-all-done.1 = bf16[64,16,384]{2,1,0:T(8,128)(2,1)S(1)} async-done(((bf16[64,16,384]{2,1,0:T(8,128)(2,1)}), bf16[64,16,384]{2,1,0:T(8,128)(2,1)S(1)}, u32[]{:S(2)}, u32[]{:S(2)}) %all-to-all-start.1) | async-done | bytes 786464 | tf_op jit(solution)/shard_map/all_to_all | solution.py:252
  132.2 0.7 shard_map.71
  (5 shorter events, 0.1 us)
Async XLA Ops:
  4.9 10.6 %copy-start.1 = (bf16[2048,384]{1,0:T(8,128)(2,1)S(1)}, bf16[2048,384]{1,0:T(8,128)(2,1)}, u32[]{:S(2)}) copy-start(bf16[2048,384]{1,0:T(8,128)(2,1)} %param.4) | copy-start | bytes 4718596
  4.9 48.6 %all-to-all-start = ((bf16[16,128,384]{2,1,0:T(8,128)(2,1)}), bf16[16,128,384]{2,1,0:T(8,128)(2,1)S(1)}, u32[]{:S(2)}, u32[]{:S(2)}) async-start(bf16[16,128,384]{2,1,0:T(8,128)(2,1)} %bitcast.32), calls=%async_computation | async-start | bytes 3145728 | tf_op jit(solution)/shard_map/all_to_all | solution.py:188
  15.5 17.0 %copy-start = (bf16[384,384]{1,0:T(8,128)(2,1)S(1)}, bf16[384,384]{1,0:T(8,128)(2,1)}, u32[]{:S(2)}) copy-start(bf16[384,384]{1,0:T(8,128)(2,1)} %get-tuple-element.15.w_ref) | copy-start | bytes 884740
  15.5 18.9 %copy-start.3 = (bf16[128,384]{1,0:T(8,128)(2,1)S(1)}, bf16[128,384]{1,0:T(8,128)(2,1)}, u32[]{:S(2)}) copy-start(bf16[128,384]{1,0:T(8,128)(2,1)} %param.7) | copy-start | bytes 294916
  16.5 33.4 %collective-permute-start.2 = (bf16[2,8,4,16,384]{4,3,2,1,0:T(8,128)(2,1)}, bf16[2,8,4,16,384]{4,3,2,1,0:T(8,128)(2,1)S(1)}, u32[]{:S(2)}, u32[]{:S(2)}) collective-permute-start(bf16[2,8,4,16,384]{4,3,2,1,0:T(8,128)(2,1)} %dynamic-slice_bitcast_fusion), channel_id=1, source_target_pairs={{0,776},{1,777},{2,778},{3,779},{4,780},{5,781},{6,782},{7,783},{8... | collective-permute-start | bytes 2359304 | tf_op jit(solution)/shard_map/ppermute | solution.py:201
  32.5 17.5 %collective-permute-start.1 = (bf16[384,384]{1,0:T(8,128)(2,1)S(1)}, bf16[384,384]{1,0:T(8,128)(2,1)S(1)}, u32[]{:S(2)}, u32[]{:S(2)}) collective-permute-start(bf16[384,384]{1,0:T(8,128)(2,1)S(1)} %copy-done), channel_id=1, source_target_pairs={{0,8},{1,9},{2,10},{3,11},{4,12},{5,13},{6,14},{7,15},{8,0},{9,1},... | collective-permute-start | bytes 884744 | tf_op jit(solution)/shard_map/ppermute | solution.py:194
  34.4 15.5 %collective-permute-start = (bf16[4,16,384]{2,1,0:T(8,128)(2,1)S(1)}, bf16[4,16,384]{2,1,0:T(8,128)(2,1)S(1)}, u32[]{:S(2)}, u32[]{:S(2)}) collective-permute-start(bf16[4,16,384]{2,1,0:T(8,128)(2,1)S(1)} %dynamic-slice_bitcast_fusion.1), channel_id=1, source_target_pairs={{0,8},{1,9},{2,10},{3,11},{4,12},{5,13},{6,14},{7,15},{8,0},{9,1},... | collective-permute-start | bytes 147464 | tf_op jit(solution)/shard_map/ppermute | solution.py:191
  80.8 5.7 %collective-permute-start.3 = (bf16[2,512,384]{2,1,0:T(8,128)(2,1)S(1)}, bf16[2,512,384]{2,1,0:T(8,128)(2,1)S(1)}, u32[]{:S(2)}, u32[]{:S(2)}) collective-permute-start(bf16[2,512,384]{2,1,0:T(8,128)(2,1)S(1)} %shard_map.69), channel_id=1, source_target_pairs={{0,16},{16,0},{32,48},{48,32},{64,80},{80,64},{96,112},{112,96},{1... | collective-permute-start | bytes 2359304 | tf_op jit(solution)/shard_map/ppermute | solution.py:227
  83.4 28.6 %collective-permute-start.5 = (bf16[384,384]{1,0:T(8,128)(2,1)S(1)}, bf16[384,384]{1,0:T(8,128)(2,1)S(1)}, u32[]{:S(2)}, u32[]{:S(2)}) collective-permute-start(bf16[384,384]{1,0:T(8,128)(2,1)S(1)} %shard_map.72), channel_id=1, source_target_pairs={{0,8},{1,9},{2,10},{3,11},{4,12},{5,13},{6,14},{7,15},{8,0},{9,1},... | collective-permute-start | bytes 884744 | tf_op jit(solution)/shard_map/ppermute | solution.py:231
  88.1 44.1 %all-to-all-start.1 = ((bf16[64,16,384]{2,1,0:T(8,128)(2,1)}), bf16[64,16,384]{2,1,0:T(8,128)(2,1)S(1)}, u32[]{:S(2)}, u32[]{:S(2)}) async-start(bf16[64,16,384]{2,1,0:T(8,128)(2,1)} %bitcast.14), calls=%async_computation.1 | async-start | bytes 1572864 | tf_op jit(solution)/shard_map/all_to_all | solution.py:252
  108.6 18.2 %collective-permute-start.4 = (bf16[64,384]{1,0:T(8,128)(2,1)S(1)}, bf16[64,384]{1,0:T(8,128)(2,1)S(1)}, u32[]{:S(2)}, u32[]{:S(2)}) collective-permute-start(bf16[64,384]{1,0:T(8,128)(2,1)S(1)} %get-tuple-element.22), channel_id=1, source_target_pairs={{0,8},{1,9},{2,10},{3,11},{4,12},{5,13},{6,14},{7,15},{8,0},{9,1},... | collective-permute-start | bytes 147464 | tf_op jit(solution)/shard_map/ppermute | solution.py:266
  112.0 1.4 %copy-start.2 = (bf16[2048,384]{1,0:T(8,128)(2,1)S(1)}, bf16[2048,384]{1,0:T(8,128)(2,1)}, u32[]{:S(2)}) copy-start(bf16[2048,384]{1,0:T(8,128)(2,1)} %param.4) | copy-start | bytes 4718596
